TPU v7x, 32 devices: a whole 2x2x4 slice. The times are simulated.
32 devices in a mesh: fsdp: 8 (over y, x, core), rep: 4 (over z).
Axes of the slice: x: 2, y: 2, z: 4, core: 2. Of those that a mesh axis runs over, the one named last changes fastest.
Arguments:
- images: bfloat16 [160, 197, 768], P(('fsdp', 'rep')), may hold values from -6 to 6
- cotangent: bfloat16 [160, 197, 768], P(('fsdp', 'rep')), may hold values from -6 to 6
- weight_in: float32 [2, 768, 5376], P(None, 'fsdp'), may hold values from -0.21875 to 0.21875
- weight_out: float32 [2, 3840, 768], P(None, 'fsdp'), may hold values from -0.3125 to 0.3125
- vector_params: float32 [2, 9216], P(None, 'fsdp'), may hold values from 0.5 to 1.5
- first_in: float32 [2, 768, 5376], P(None, 'fsdp'), may hold values from -56 to 56
- first_out: float32 [2, 3840, 768], P(None, 'fsdp'), may hold values from -56 to 56
- first_vec: float32 [2, 9216], P(None, 'fsdp'), may hold values from -56 to 56
- second_in: float32 [2, 768, 5376], P(None, 'fsdp'), may hold values from 3.152 to 12.608
- second_out: float32 [2, 3840, 768], P(None, 'fsdp'), may hold values from 3.152 to 12.608
- second_vec: float32 [2, 9216], P(None, 'fsdp'), may hold values from 3.152 to 12.608
Outputs:
- encoded: bfloat16 [160, 197, 768], P(('fsdp', 'rep'))
- image_grad: float32 [160, 197, 768], P(('fsdp', 'rep'))
- grad_in: float32 [2, 768, 5376], P(None, 'fsdp')
- grad_out: float32 [2, 3840, 768], P(None, 'fsdp')
- grad_vec: float32 [2, 9216], P(None, 'fsdp')
- new_in: float32 [2, 768, 5376], P(None, 'fsdp')
- new_out: float32 [2, 3840, 768], P(None, 'fsdp')
- new_vec: float32 [2, 9216], P(None, 'fsdp')
- moment_in: float32 [2, 768, 5376], P(None, 'fsdp')
- moment_out: float32 [2, 3840, 768], P(None, 'fsdp')
- moment_vec: float32 [2, 9216], P(None, 'fsdp')
- square_in: float32 [2, 768, 5376], P(None, 'fsdp')
- square_out: float32 [2, 3840, 768], P(None, 'fsdp')
- square_vec: float32 [2, 9216], P(None, 'fsdp')
All inputs are finite; a program needn't handle non-finite values.
Results may differ from a plain program's by a relative error of at most 0.013.
The roundings to bfloat16 on the way count: a program that leaves them out, or rounds other values in their place, can miss the bound.
Values may be sent and summed in bfloat16 or wider, within the bound.
A program may use at most 320 MiB of HBM per device.

v0:
```python
import jax
import jax.numpy as jnp
from jax import lax
from jax.sharding import PartitionSpec as P

D = 768
HEADS = 12
HEAD_DIM = 64
SEQ = 197
LAYERS = 2
STEP = 3


norm_eps = 1e-06
beta_one = 0.9
beta_two = 0.999
matrix_rate = 0.03
vector_rate = 0.2
matrix_decay = 0.05
adam_eps = 1e-08


def layer_norm(hidden, gain_row, shift_row):
    average = jnp.mean(hidden, axis=-1, keepdims=True)
    centred = hidden - average
    spread = jnp.mean(centred * centred, axis=-1, keepdims=True)
    return centred * lax.rsqrt(spread + norm_eps) * gain_row + shift_row


def exact_gelu(pre_act):
    return jax.nn.gelu(pre_act, approximate=False)


def rows_product(matrix_a, matrix_b):
    return lax.dot_general(
        matrix_a, matrix_b, (((0,), (0,)), ((), ())), preferred_element_type=jnp.float32
    )


def back_product(matrix_a, matrix_b):
    return lax.dot_general(
        matrix_a, matrix_b, (((1,), (1,)), ((), ())), preferred_element_type=jnp.float32
    )


def heads_view(matrix_a):
    return matrix_a.reshape(-1, SEQ, HEADS, HEAD_DIM)


def vector_rows(vec_weight):
    pieces = vec_weight.astype(jnp.float32)
    row_list = [pieces[slot_index * D : (slot_index + 1) * D] for slot_index in range(8)]
    return (row_list, pieces[8 * D :])


def attention_scores(queries, key_rows):
    score_scale = HEAD_DIM ** (-0.5)
    return (
        jnp.einsum(
            "bqhd,bkhd->bhqk",
            heads_view(queries),
            heads_view(key_rows),
            preferred_element_type=jnp.float32,
        )
        * score_scale
    )


def forward_layer(hidden, in_weight, out_weight, vec_weight):
    row_list, ff_bias = vector_rows(vec_weight)
    normed = layer_norm(hidden, row_list[0], row_list[1]).astype(jnp.bfloat16)
    mixed = jnp.dot(normed, in_weight[:, : 3 * D], preferred_element_type=jnp.float32)
    queries = (mixed[:, :D] + row_list[2]).astype(jnp.bfloat16)
    key_rows = mixed[:, D : 2 * D].astype(jnp.bfloat16)
    values = (mixed[:, 2 * D :] + row_list[3]).astype(jnp.bfloat16)
    scores = attention_scores(queries, key_rows)
    peak_score = jnp.max(scores, axis=-1, keepdims=True)
    log_total = peak_score + jnp.log(jnp.sum(jnp.exp(scores - peak_score), axis=-1, keepdims=True))
    soft_weights = jnp.exp(scores - log_total).astype(jnp.bfloat16)
    attended = jnp.einsum(
        "bhqk,bkhd->bqhd", soft_weights, heads_view(values), preferred_element_type=jnp.float32
    )
    attended = attended.reshape(-1, D).astype(jnp.bfloat16)
    inner = (
        hidden + jnp.dot(attended, out_weight[:D], preferred_element_type=jnp.float32) + row_list[4]
    )
    normed_two = layer_norm(inner, row_list[5], row_list[6]).astype(jnp.bfloat16)
    pre_act = (
        jnp.dot(normed_two, in_weight[:, 3 * D :], preferred_element_type=jnp.float32) + ff_bias
    )
    activated = exact_gelu(pre_act).astype(jnp.bfloat16)
    output = (
        inner + jnp.dot(activated, out_weight[D:], preferred_element_type=jnp.float32) + row_list[7]
    )
    saved = (
        hidden,
        normed,
        queries,
        key_rows,
        values,
        log_total,
        attended,
        inner,
        normed_two,
        pre_act,
        activated,
    )
    return (output, saved)


def backward_layer(upstream, saved, in_weight, out_weight, vec_weight):
    (
        hidden,
        normed,
        queries,
        key_rows,
        values,
        log_total,
        attended,
        inner,
        normed_two,
        pre_act,
        activated,
    ) = saved
    row_list, ff_bias = vector_rows(vec_weight)
    upstream_low = upstream.astype(jnp.bfloat16)
    grad_down = rows_product(activated, upstream_low)
    grad_act = back_product(upstream_low, out_weight[D:])
    unused, gelu_back = jax.vjp(exact_gelu, pre_act)
    grad_pre = gelu_back(grad_act)[0]
    grad_pre_low = grad_pre.astype(jnp.bfloat16)
    grad_up = rows_product(normed_two, grad_pre_low)
    grad_normed_two = back_product(grad_pre_low, in_weight[:, 3 * D :])
    unused, norm_back_two = jax.vjp(layer_norm, inner, row_list[5], row_list[6])
    grad_inner, grad_gain_two, grad_shift_two = norm_back_two(grad_normed_two)
    grad_inner = grad_inner + upstream
    grad_inner_low = grad_inner.astype(jnp.bfloat16)
    grad_attn_out = rows_product(attended, grad_inner_low)
    grad_attended = back_product(grad_inner_low, out_weight[:D]).astype(jnp.bfloat16)
    scores = attention_scores(queries, key_rows)
    soft_full = jnp.exp(scores - log_total)
    soft_weights = soft_full.astype(jnp.bfloat16)
    grad_heads = heads_view(grad_attended)
    grad_soft = jnp.einsum(
        "bqhd,bkhd->bhqk", grad_heads, heads_view(values), preferred_element_type=jnp.float32
    )
    grad_values = jnp.einsum(
        "bhqk,bqhd->bkhd", soft_weights, grad_heads, preferred_element_type=jnp.float32
    )
    weighted = jnp.sum(soft_full * grad_soft, axis=-1, keepdims=True)
    grad_scores = (soft_full * (grad_soft - weighted)).astype(jnp.bfloat16)
    score_scale = HEAD_DIM ** (-0.5)
    grad_queries = (
        jnp.einsum(
            "bhqk,bkhd->bqhd", grad_scores, heads_view(key_rows), preferred_element_type=jnp.float32
        )
        * score_scale
    )
    grad_keys = (
        jnp.einsum(
            "bhqk,bqhd->bkhd", grad_scores, heads_view(queries), preferred_element_type=jnp.float32
        )
        * score_scale
    )
    grad_queries = grad_queries.reshape(-1, D)
    grad_values = grad_values.reshape(-1, D)
    grad_mixed = jnp.concatenate([grad_queries, grad_keys.reshape(-1, D), grad_values], axis=1)
    grad_mixed_low = grad_mixed.astype(jnp.bfloat16)
    grad_qkv = rows_product(normed, grad_mixed_low)
    grad_normed = back_product(grad_mixed_low, in_weight[:, : 3 * D])
    unused, norm_back_one = jax.vjp(layer_norm, hidden, row_list[0], row_list[1])
    grad_hidden, grad_gain_one, grad_shift_one = norm_back_one(grad_normed)
    grad_hidden = grad_hidden + grad_inner
    grad_vector = jnp.concatenate(
        [
            grad_gain_one,
            grad_shift_one,
            jnp.sum(grad_queries, axis=0),
            jnp.sum(grad_values, axis=0),
            jnp.sum(grad_inner, axis=0),
            grad_gain_two,
            grad_shift_two,
            jnp.sum(upstream, axis=0),
            jnp.sum(grad_pre, axis=0),
        ]
    )
    grad_in_w = jnp.concatenate([grad_qkv, grad_up], axis=1)
    grad_out_w = jnp.concatenate([grad_attn_out, grad_down], axis=0)
    return (grad_hidden, grad_in_w, grad_out_w, grad_vector)


def adam_update(master, gradient, moment_one, moment_two, rate, decay_rate):
    moment_one = beta_one * moment_one + (1.0 - beta_one) * gradient
    moment_two = beta_two * moment_two + (1.0 - beta_two) * gradient * gradient
    corr_one = 1.0 - beta_one**STEP
    corr_two = 1.0 - beta_two**STEP
    adam_move = moment_one / corr_one / (jnp.sqrt(moment_two / corr_two) + adam_eps)
    return (master - rate * (adam_move + decay_rate * master), moment_one, moment_two)


def shards(
    images,
    cotangent,
    weight_in,
    weight_out,
    vector_params,
    first_in,
    first_out,
    first_vec,
    second_in,
    second_out,
    second_vec,
):
    hidden = images.reshape(-1, D).astype(jnp.float32)
    saved_all = []
    for depth_index in range(LAYERS):
        in_weight, out_weight, vec_weight = (
            lax.all_gather(weight_in[depth_index].astype(jnp.bfloat16), "fsdp", axis=0, tiled=True),
            lax.all_gather(
                weight_out[depth_index].astype(jnp.bfloat16), "fsdp", axis=0, tiled=True
            ),
            lax.all_gather(
                vector_params[depth_index].astype(jnp.bfloat16), "fsdp", axis=0, tiled=True
            ),
        )
        hidden, saved = forward_layer(hidden, in_weight, out_weight, vec_weight)
        saved_all.append(saved)
    encoded = hidden.reshape(images.shape).astype(jnp.bfloat16)
    upstream = cotangent.reshape(-1, D).astype(jnp.float32)
    owned_in = [None] * LAYERS
    owned_out = [None] * LAYERS
    owned_vec = [None] * LAYERS
    for depth_index in reversed(range(LAYERS)):
        in_weight, out_weight, vec_weight = (
            lax.all_gather(weight_in[depth_index].astype(jnp.bfloat16), "fsdp", axis=0, tiled=True),
            lax.all_gather(
                weight_out[depth_index].astype(jnp.bfloat16), "fsdp", axis=0, tiled=True
            ),
            lax.all_gather(
                vector_params[depth_index].astype(jnp.bfloat16), "fsdp", axis=0, tiled=True
            ),
        )
        upstream, grad_in_w, grad_out_w, grad_vector = backward_layer(
            upstream, saved_all[depth_index], in_weight, out_weight, vec_weight
        )
        share_in, share_out, share_vec = (
            lax.psum_scatter(grad_in_w, "fsdp", scatter_dimension=0, tiled=True),
            lax.psum_scatter(grad_out_w, "fsdp", scatter_dimension=0, tiled=True),
            lax.psum_scatter(grad_vector, "fsdp", scatter_dimension=0, tiled=True),
        )
        share_in, share_out, share_vec = lax.psum((share_in, share_out, share_vec), "rep")
        owned_in[depth_index] = share_in
        owned_out[depth_index] = share_out
        owned_vec[depth_index] = share_vec
    grad_in = jnp.stack(owned_in)
    grad_out = jnp.stack(owned_out)
    grad_vec = jnp.stack(owned_vec)
    image_grad = upstream.reshape(images.shape)
    new_in, moment_in, square_in = adam_update(
        weight_in, grad_in, first_in, second_in, matrix_rate, matrix_decay
    )
    new_out, moment_out, square_out = adam_update(
        weight_out, grad_out, first_out, second_out, matrix_rate, matrix_decay
    )
    new_vec, moment_vec, square_vec = adam_update(
        vector_params, grad_vec, first_vec, second_vec, vector_rate, 0.0
    )
    return (
        encoded,
        image_grad,
        grad_in,
        grad_out,
        grad_vec,
        new_in,
        new_out,
        new_vec,
        moment_in,
        moment_out,
        moment_vec,
        square_in,
        square_out,
        square_vec,
    )


def solution(mesh):
    in_specs = (
        P(("fsdp", "rep"), None, None),
        P(("fsdp", "rep"), None, None),
        P(None, "fsdp", None),
        P(None, "fsdp", None),
        P(None, "fsdp"),
        P(None, "fsdp", None),
        P(None, "fsdp", None),
        P(None, "fsdp"),
        P(None, "fsdp", None),
        P(None, "fsdp", None),
        P(None, "fsdp"),
    )
    out_specs = (
        P(("fsdp", "rep"), None, None),
        P(("fsdp", "rep"), None, None),
        P(None, "fsdp", None),
        P(None, "fsdp", None),
        P(None, "fsdp"),
        P(None, "fsdp", None),
        P(None, "fsdp", None),
        P(None, "fsdp"),
        P(None, "fsdp", None),
        P(None, "fsdp", None),
        P(None, "fsdp"),
        P(None, "fsdp", None),
        P(None, "fsdp", None),
        P(None, "fsdp"),
    )
    return jax.shard_map(shards, mesh=mesh, in_specs=in_specs, out_specs=out_specs, check_vma=False)
```

profile of v0, /device:TPU:8, one launch (start us, length us, event | category | flops | bytes accessed | tf_op | source)
XLA Modules:
  0.0 1118.8 jit_solution(9080934850015896550)
XLA Ops:
  16.9 9.1 all-gather.3
  26.6 9.1 all-gather
  40.2 26.2 %all-gather.11.cloned.1.call-done = bf16[1,768,5376]{2,1,0:T(8,128)(2,1)} async-done(((bf16[1,96,5376]{2,1,0:T(8,128)(2,1)}), bf16[1,768,5376]{2,1,0:T(8,128)(2,1)}) %all-gather.11.cloned.1.call-update) | async-done | bytes 8257552 | tf_op jit(solution)/shard_map/all_gather | solution.py:218
  66.3 6.9 fusion.33
  75.1 6.1 reshape.338
  81.2 6.0 copy.92
  87.2 4.4 reshape.339
  91.6 5.2 copy.93
  96.8 4.4 reshape.337
  101.2 6.5 copy.94
  123.4 4.8 fusion.88
  129.7 35.5 %multiply_convert_fusion.3 = (bf16[985,3072]{1,0:T(8,128)(2,1)S(1)}, f32[985,3072]{1,0:T(8,128)}, f32[985,3072]{1,0:T(8,128)}) fusion(f32[3072]{0:T(1024)S(1)} %bitcast.123, bf16[768,5376]{1,0:T(8,128)(2,1)} %bitcast.128, f32[985,768]{1,0:T(8,128)S(1)} %get-tuple-element.90, f32[768]{0:T(1024)S(1)} %get-tuple-element.35, f32[768]{0:T(1024)S(1)} %get-tuple-element.36, ...), kind=kOutput, calls=%fused_computation.29 | convolution fusion | flops 4851306496 | bytes 38030024 | tf_op jit(solution)/shard_map/dot_general | solution.py:89
  165.3 5.1 fusion.89
  171.9 6.0 fusion.29
  179.8 4.4 reshape.341
  184.2 6.6 copy.100
  190.8 4.4 reshape.342
  195.2 5.2 copy.101
  200.4 4.4 reshape.340
  204.8 6.0 copy.102
  226.5 4.4 fusion.90
  231.4 36.2 %multiply_convert_fusion.2 = (bf16[985,3072]{1,0:T(8,128)(2,1)}, f32[985,3072]{1,0:T(8,128)}, f32[985,3072]{1,0:T(8,128)}) fusion(f32[3072]{0:T(1024)S(1)} %bitcast.125, bf16[768,5376]{1,0:T(8,128)(2,1)} %bitcast.132, f32[985,768]{1,0:T(8,128)S(1)} %get-tuple-element.97, f32[768]{0:T(1024)S(1)} %copy-done.67, f32[768]{0:T(1024)S(1)} %copy-done.63, ...), kind=kOutput, calls=%fused_computation.16 | convolution fusion | flops 4851306496 | bytes 38030024 | tf_op jit(solution)/shard_map/dot_general | solution.py:89
  267.6 16.7 %fusion.91 = (f32[3072]{0:T(1024)}, bf16[985,3072]{1,0:T(8,128)(2,1)}) fusion(f32[985,3072]{1,0:T(8,128)} %get-tuple-element.73, bf16[985,768]{1,0:T(8,128)(2,1)S(1)} %copy-done.36, bf16[1,3840,768]{2,1,0:T(8,128)(2,1)} %all-gather.17.cloned.1.call-done, f32[985,3072]{1,0:T(8,128)} %get-tuple-element.98, f32[3072]{0:T(1024)S(1)} %bitcast.126), kind=kOutput, calls=%fused_computation.244 | convolution fusion | flops 4696224768 | bytes 36687360 | tf_op jit(solution)/shard_map/dot_general | solution.py:41
  284.3 10.1 multiply_reduce_fusion.5
  297.9 7.8 fusion.93
  308.7 9.5 pad_maximum_fusion.3
  322.5 6.2 reshape.343
  328.7 5.5 copy.106
  334.2 10.2 bitcast_convert_fusion.2
  347.7 5.6 reshape.298
  353.2 9.2 multiply_reduce_fusion.1
  362.4 7.0 multiply_convert_fusion.1
  376.4 5.5 reshape.296
  382.0 4.8 fusion.46
  395.4 9.2 multiply_reduce_fusion.6
  408.4 16.8 %fusion.92 = (f32[3072]{0:T(1024)}, bf16[985,3072]{1,0:T(8,128)(2,1)}) fusion(f32[985,3072]{1,0:T(8,128)} %get-tuple-element.75, bf16[1,3840,768]{2,1,0:T(8,128)(2,1)} %all-gather.13.cloned.1.call-done, f32[985,768]{1,0:T(8,128)S(1)} %get-tuple-element.61, f32[985,3072]{1,0:T(8,128)} %get-tuple-element.91, f32[3072]{0:T(1024)S(1)} %bitcast.124), kind=kOutput, calls=%fused_computation.245 | convolution fusion | flops 4696981504 | bytes 38200320 | tf_op jit(solution)/shard_map/dot_general | solution.py:41
  425.2 9.3 multiply_reduce_fusion.7
  441.1 8.1 fusion.57
  449.2 9.5 pad_maximum_fusion.2
  459.3 7.9 fusion.72
  467.3 8.7 fusion.42
  476.0 6.1 pad_maximum_fusion.1
  482.3 4.7 convolution_convert_fusion
  487.0 5.8 reshape.344
  492.8 6.1 copy.118
  499.0 9.8 bitcast_convert_fusion
  511.9 5.6 reshape.302
  517.5 9.4 multiply_reduce_fusion
  526.9 8.0 multiply_convert_fusion
  541.8 5.5 reshape.300
  547.4 5.4 fusion.47
  556.0 6.0 reshape.301
  567.0 4.5 fusion.71
  572.9 5.6 fusion.39
  578.5 6.0 pad_maximum_fusion
  598.1 10.8 multiply_reduce_fusion.8
  610.0 56.0 %reduce-scatter.7.cloned.1.call-done = f32[96,5376]{1,0:T(8,128)} async-done(((f32[768,5376]{1,0:T(8,128)}), f32[96,5376]{1,0:T(8,128)}) %reduce-scatter.7.cloned.1.call-update) | async-done | bytes 2064400 | tf_op jit(solution)/shard_map/reduce_scatter | solution.py:247
  666.0 118.9 %reduce-scatter.5.cloned.1.call-done = f32[96,5376]{1,0:T(8,128)} async-done(((f32[768,5376]{1,0:T(8,128)}), f32[96,5376]{1,0:T(8,128)}) %reduce-scatter.5.cloned.1.call-update) | async-done | bytes 2064400 | tf_op jit(solution)/shard_map/reduce_scatter | solution.py:247
  786.2 10.1 add_convert_fusion
  804.8 34.3 %all-reduce.8.cloned.1.call-done = (f32[9216]{0:T(1024)}, f32[9216]{0:T(1024)}) async-done(((f32[9216]{0:T(1024)}, f32[9216]{0:T(1024)}), (f32[9216]{0:T(1024)}, f32[9216]{0:T(1024)})) %all-reduce.8.cloned.1.call-update) | async-done | bytes 73744
  840.8 9.2 all-reduce.3
  850.6 239.6 %all-reduce.10.cloned.1.call-done = (f32[1,96,5376]{2,1,0:T(8,128)}, f32[1,96,5376]{2,1,0:T(8,128)}, f32[1,480,768]{2,1,0:T(8,128)}, f32[1,480,768]{2,1,0:T(8,128)}) async-done(((f32[1,96,5376]{2,1,0:T(8,128)}, f32[1,96,5376]{2,1,0:T(8,128)}, f32[1,480,768]{2,1,0:T(8,128)}, f32[1,480,768]{2,1,0:T(8,128)}), (f32[1,96,5376]{2,1,0:T(8,128)}, f32[1,96,5376]{2,1,0:T(8,128)}, f32[1,480,768]{2,1,0:T(8,128)}, ...) | async-done | bytes 7077904 | tf_op jit(solution)/shard_map/psum | solution.py:251
  1097.6 4.7 multiply_subtract_fusion.1
  1106.2 5.6 multiply_subtract_fusion
  (389 shorter events, 150.1 us)
Async XLA Ops:
  7.2 59.2 %all-gather.11.cloned.1.call-start = ((), (), s32[]{:S(2)}) async-start(), calls=%async_computation.8 | async-start | bytes 9289728 | tf_op jit(solution)/shard_map/all_gather | solution.py:218
  11.1 112.3 %all-gather.13.cloned.1.call-start = ((), (), s32[]{:S(2)}) async-start(), calls=%async_computation.9 | async-start | bytes 6635520 | tf_op jit(solution)/shard_map/all_gather | solution.py:219
  14.5 157.4 %all-gather.15.cloned.1.call-start = ((), (), s32[]{:S(2)}) async-start(), calls=%async_computation.10 | async-start | bytes 9289728 | tf_op jit(solution)/shard_map/all_gather | solution.py:218
  15.2 211.2 %all-gather.17.cloned.1.call-start = ((), (), s32[]{:S(2)}) async-start(), calls=%async_computation.11 | async-start | bytes 6635520 | tf_op jit(solution)/shard_map/all_gather | solution.py:219
  15.8 22.8 %copy-start.34 = (bf16[5,197,768]{2,1,0:T(8,128)(2,1)S(1)}, bf16[5,197,768]{2,1,0:T(8,128)(2,1)}, u32[]{:S(2)}) copy-start(bf16[5,197,768]{2,1,0:T(8,128)(2,1)} %param.12) | copy-start | bytes 4538884
  15.8 594.2 %reduce-scatter.11.cloned.1.call-start = ((), (), s32[]{:S(2)}) async-start(), calls=%async_computation.7 | async-start | bytes 13271040 | tf_op jit(solution)/shard_map/reduce_scatter | solution.py:248
  16.2 50.1 %copy-start.87 = (f32[985]{0:T(1024)}, f32[985]{0:T(1024)S(1)}, u32[]{:S(2)}) copy-start(f32[985]{0:T(1024)S(1)} %div.128) | copy-start | bytes 11824
  35.7 94.0 %copy-start.96 = (f32[1,3072]{1,0:T(1,128)}, f32[1,3072]{1,0:T(1,128)S(1)}, u32[]{:S(2)}) copy-start(f32[1,3072]{1,0:T(1,128)S(1)} %slice.216) | copy-start | bytes 36868
  37.9 28.5 %copy-start.77 = (f32[985]{0:T(1024)}, f32[985]{0:T(1024)S(1)}, u32[]{:S(2)}) copy-start(f32[985]{0:T(1024)S(1)} %add.269) | copy-start | bytes 11824
  37.9 35.4 %copy-start.89 = (f32[985]{0:T(1024)}, f32[985]{0:T(1024)S(1)}, u32[]{:S(2)}) copy-start(f32[985]{0:T(1024)S(1)} %rsqrt.44) | copy-start | bytes 11824
  38.5 133.4 %copy-start.83 = (f32[768]{0:T(1024)}, f32[768]{0:T(1024)S(1)}, u32[]{:S(2)}) copy-start(f32[768]{0:T(1024)S(1)} %get-tuple-element.33) | copy-start | bytes 9220
  38.5 133.4 %copy-start.105 = (f32[768]{0:T(1024)}, f32[768]{0:T(1024)S(1)}, u32[]{:S(2)}) copy-start(f32[768]{0:T(1024)S(1)} %get-tuple-element.32) | copy-start | bytes 9220
  38.6 34.7 %copy-start.81 = (f32[768]{0:T(1024)}, f32[768]{0:T(1024)S(1)}, u32[]{:S(2)}) copy-start(f32[768]{0:T(1024)S(1)} %get-tuple-element.41) | copy-start | bytes 9220
  38.6 34.7 %copy-start.103 = (f32[768]{0:T(1024)}, f32[768]{0:T(1024)S(1)}, u32[]{:S(2)}) copy-start(f32[768]{0:T(1024)S(1)} %get-tuple-element.40) | copy-start | bytes 9220
  38.6 91.1 %copy-start.61 = (f32[768]{0:T(1024)}, f32[768]{0:T(1024)S(1)}, u32[]{:S(2)}) copy-start(f32[768]{0:T(1024)S(1)} %get-tuple-element.36) | copy-start | bytes 9220
  38.6 91.1 %copy-start.65 = (f32[768]{0:T(1024)}, f32[768]{0:T(1024)S(1)}, u32[]{:S(2)}) copy-start(f32[768]{0:T(1024)S(1)} %get-tuple-element.35) | copy-start | bytes 9220
  96.8 10.9 copy-start.9
  123.4 41.9 %slice-start.2 = ((s8[5898240]{0:T(1024)(128)(4,1)}), s8[4194304]{0:T(1024)(128)(4,1)S(1)}, s32[]{:S(2)}) async-start(s8[5898240]{0:T(1024)(128)(4,1)} %bitcast.135), calls=%async_computation.16 | async-start | bytes 8388608
  128.2 37.0 %copy-start.6 = (f32[985,768]{1,0:T(8,128)}, f32[985,768]{1,0:T(8,128)S(1)}, u32[]{:S(2)}) copy-start(f32[985,768]{1,0:T(8,128)S(1)} %get-tuple-element.90) | copy-start | bytes 9077764
  128.2 37.0 %copy-start.53 = (f32[985]{0:T(1024)}, f32[985]{0:T(1024)S(1)}, u32[]{:S(2)}) copy-start(f32[985]{0:T(1024)S(1)} %broadcast_multiply_fusion.3) | copy-start | bytes 11824
  129.7 35.5 %copy-start.57 = (f32[985]{0:T(1024)}, f32[985]{0:T(1024)S(1)}, u32[]{:S(2)}) copy-start(f32[985]{0:T(1024)S(1)} %fusion.64) | copy-start | bytes 11824
  129.7 35.6 %slice-start.3 = ((s8[5898240]{0:T(1024)(128)(4,1)}), s8[1703936]{0:T(1024)(128)(4,1)S(1)}, s32[]{:S(2)}) async-start(s8[5898240]{0:T(1024)(128)(4,1)} %bitcast.135), calls=%async_computation.17 | async-start | bytes 3407872
  200.4 10.4 copy-start.11
  230.8 63.6 %copy-start.4 = (f32[985,768]{1,0:T(8,128)}, f32[985,768]{1,0:T(8,128)S(1)}, u32[]{:S(2)}) copy-start(f32[985,768]{1,0:T(8,128)S(1)} %get-tuple-element.97) | copy-start | bytes 9077764
  230.8 63.6 %copy-start.55 = (f32[985]{0:T(1024)}, f32[985]{0:T(1024)S(1)}, u32[]{:S(2)}) copy-start(f32[985]{0:T(1024)S(1)} %broadcast_multiply_fusion.1) | copy-start | bytes 11824
  231.4 63.1 %copy-start.59 = (f32[985]{0:T(1024)}, f32[985]{0:T(1024)S(1)}, u32[]{:S(2)}) copy-start(f32[985]{0:T(1024)S(1)} %fusion.66) | copy-start | bytes 11824
  231.4 36.2 %copy-start.36 = (bf16[985,768]{1,0:T(8,128)(2,1)S(1)}, bf16[985,768]{1,0:T(8,128)(2,1)}, u32[]{:S(2)}) copy-start(bf16[985,768]{1,0:T(8,128)(2,1)} %reshape.294) | copy-start | bytes 4538884
  295.9 22.3 %copy-start.22 = (f32[985,768]{1,0:T(8,128)}, f32[985,768]{1,0:T(8,128)S(1)}, u32[]{:S(2)}) copy-start(f32[985,768]{1,0:T(8,128)S(1)} %get-tuple-element.71) | copy-start | bytes 9077764
  318.2 291.8 %reduce-scatter.9.cloned.1.call-start = ((), (), s32[]{:S(2)}) async-start(), calls=%async_computation.6 | async-start | bytes 13271040 | tf_op jit(solution)/shard_map/reduce_scatter | solution.py:248
  334.2 10.2 copy-start.17
  344.4 8.9 copy-start.16
  373.3 8.7 copy-start.13
  395.4 9.2 copy-start.51
  395.4 9.2 copy-start.74
  408.4 16.8 %copy-start.7 = (f32[985,768]{1,0:T(8,128)S(1)}, f32[985,768]{1,0:T(8,128)}, u32[]{:S(2)}) copy-start(f32[985,768]{1,0:T(8,128)} %copy-done.6) | copy-start | bytes 9077764
  408.4 16.8 %copy-start.54 = (f32[985]{0:T(1024)S(1)}, f32[985]{0:T(1024)}, u32[]{:S(2)}) copy-start(f32[985]{0:T(1024)} %copy-done.53) | copy-start | bytes 11824
  408.4 16.8 %copy-start.58 = (f32[985]{0:T(1024)S(1)}, f32[985]{0:T(1024)}, u32[]{:S(2)}) copy-start(f32[985]{0:T(1024)} %copy-done.57) | copy-start | bytes 11824
  408.4 16.8 %copy-start.62 = (f32[768]{0:T(1024)S(1)}, f32[768]{0:T(1024)}, u32[]{:S(2)}) copy-start(f32[768]{0:T(1024)} %copy-done.61) | copy-start | bytes 9220
  425.2 9.3 copy-start.72
  458.7 8.6 copy-start.5
  458.7 8.6 copy-start.56
  458.7 8.6 copy-start.60
  458.7 207.3 %reduce-scatter.7.cloned.1.call-start = ((), (), s32[]{:S(2)}) async-start(), calls=%async_computation.5 | async-start | bytes 18579456 | tf_op jit(solution)/shard_map/reduce_scatter | solution.py:247
  482.1 302.9 %reduce-scatter.5.cloned.1.call-start = ((), (), s32[]{:S(2)}) async-start(), calls=%async_computation.4 | async-start | bytes 18579456 | tf_op jit(solution)/shard_map/reduce_scatter | solution.py:247
  556.0 9.4 copy-start.82
  556.0 9.4 copy-start.88
  556.0 9.4 copy-start.90
  556.0 9.4 copy-start.104
  584.5 254.7 %all-reduce.8.cloned.1.call-start = ((), (), s32[]{:S(2)}) async-start(), calls=%async_computation.12 | async-start | bytes 147456
  598.0 11.0 copy-start.93
  598.0 11.0 copy-start.94
  598.0 11.0 copy-start.109
  598.0 11.0 copy-start.108
  598.1 11.0 copy-start.98
  598.1 11.0 copy-start.95
  608.9 176.1 %copy-start.112 = (u32[32]{0:T(128)S(1)}, u32[32]{0:T(128)}, u32[]{:S(2)}) copy-start(u32[32]{0:T(128)} %constant.137) | copy-start | bytes 388
  608.9 177.3 %copy-start.102 = (f32[768]{0:T(1024)S(1)}, f32[768]{0:T(1024)}, u32[]{:S(2)}) copy-start(f32[768]{0:T(1024)} %get-tuple-element.26) | copy-start | bytes 9220
  609.8 480.5 %all-reduce.10.cloned.1.call-start = ((), (), s32[]{:S(2)}) async-start(), calls=%async_computation.13 | async-start | bytes 14155776 | tf_op jit(solution)/shard_map/psum | solution.py:251
  786.2 13.2 %copy-start.78 = (f32[985]{0:T(1024)S(1)}, f32[985]{0:T(1024)}, u32[]{:S(2)}) copy-start(f32[985]{0:T(1024)} %copy-done.77) | copy-start | bytes 11824
  802.8 47.1 %copy-start.76 = (f32[2,1152]{1,0:T(2,128)S(1)}, f32[2,1152]{1,0:T(2,128)}, u32[]{:S(2)}) copy-start(f32[2,1152]{1,0:T(2,128)} %param.15) | copy-start | bytes 27652
  802.8 47.1 %copy-start.100 = (f32[2,1152]{1,0:T(2,128)S(1)}, f32[2,1152]{1,0:T(2,128)}, u32[]{:S(2)}) copy-start(f32[2,1152]{1,0:T(2,128)} %param.18) | copy-start | bytes 27652
  802.8 47.1 %copy-start.101 = (f32[2,1152]{1,0:T(2,128)S(1)}, f32[2,1152]{1,0:T(2,128)}, u32[]{:S(2)}) copy-start(f32[2,1152]{1,0:T(2,128)} %param.21) | copy-start | bytes 27652
  1093.0 9.3 copy-start.29
  1097.6 8.6 copy-start.39
  (67 other events, 294.1 us)
Sparse Core Ops, SparseCore 0:
  11.2 55.1 all-gather.10
  68.8 43.8 all-gather.12
  115.2 53.8 all-gather.14
  171.4 43.8 all-gather.16
  318.3 88.1 reduce-scatter.10
  458.8 88.6 reduce-scatter.8
  551.3 114.6 reduce-scatter.6
  670.2 114.6 reduce-scatter.4
  789.2 49.8 all-reduce.7
  841.8 248.3 all-reduce.9
where the time goes:
time: 1130 us; the launch traced here: 1120 us
  waiting for transfers between devices  476 us (42%)
  matrix products  307 us (27%)
  local copies, waits for them, and re-layouts  196 us (17%)
  other arithmetic  94.5 us (8%)
  blocking collectives  27.4 us (2%)
  between operations  16.8 us (1%)
    psum x1, waiting for transfers between devices, shards(): lax.psum((share_in, share_out, share_vec), 'rep')  240 us
    reduce_scatter x2, waiting for transfers between devices, shards(): lax.psum_scatter(grad_in_w, 'fsdp', scatter_dimension=0, tiled=True)  175 us
    reshape x16, local copies, waits for them, and re-layouts, heads_view(): return matrix_a.reshape(-1, SEQ, HEADS, HEAD_DIM)  87.1 us
    dot_general x8, matrix products, back_product(): lax.dot_general(matrix_a, matrix_b, (((1,), (1,)), ((), ())), preferred_e...  81.8 us
    dot_general x2, matrix products, forward_layer(): jnp.dot(normed_two, in_weight[:, 3 * D:], preferred_element_type=jnp.floa...  71.7 us
    dot_general x8, matrix products, rows_product(): lax.dot_general(matrix_a, matrix_b, (((0,), (0,)), ((), ())), preferred_e...  48.4 us
    unnamed x11, waiting for transfers between devices  35.7 us
    unnamed x266, local copies, waits for them, and re-layouts  34.5 us
  transfers between devices with their start and end apart: 10, of which 5 were waited for; matrix products, arithmetic and copies ran while one was open for 42% of the time, Pallas kernels for 0%

commit v1 on v0

v1 whole, which is shorter than its diff:
```python
import functools
import jax, jax.numpy as jnp
from jax import lax
from jax.experimental import pallas as pl
from jax.experimental.pallas import tpu as pltpu
from jax.sharding import PartitionSpec as P

D=768; HD=64; SEQ=197; RP=208; EPS=1e-6
BF=jnp.bfloat16; F32=jnp.float32
def dot(a,b): return jnp.dot(a,b,preferred_element_type=F32)
def dot_t(a,b): return lax.dot_general(a,b,(((1,),(1,)),((),())),preferred_element_type=F32)
def dot_0(a,b): return lax.dot_general(a,b,(((0,),(0,)),((),())),preferred_element_type=F32)

def norm_stats(x):
    mean=jnp.mean(x,axis=-1,keepdims=True); xc=x-mean
    var=jnp.mean(xc*xc,axis=-1,keepdims=True)
    return xc, lax.rsqrt(var+EPS)

def attn_fwd(q,k,v):
    lane=lax.broadcasted_iota(jnp.int32,(1,128),1)
    col=lax.broadcasted_iota(jnp.int32,(1,RP),1)
    os=[]
    for half in range(2):
        m=jnp.where((lane<64) if half==0 else (lane>=64),0.125,0.0).astype(BF)
        s=dot_t(q*m,k)
        s=jnp.where(col<SEQ,s,-1e30)
        mx=jnp.max(s,axis=-1,keepdims=True)
        e=jnp.exp(s-mx)
        p=(e*(1.0/jnp.sum(e,axis=-1,keepdims=True))).astype(BF)
        os.append(dot(p,v))
    return jnp.where(lane<64,os[0],os[1]).astype(BF)

def attn_bwd(q,k,v,do):
    lane=lax.broadcasted_iota(jnp.int32,(1,128),1)
    row=lax.broadcasted_iota(jnp.int32,(RP,1),0)
    r=[]
    for half in range(2):
        sel=(lane<64) if half==0 else (lane>=64)
        m=jnp.where(sel,0.125,0.0).astype(BF)
        m1=jnp.where(sel,1.0,0.0).astype(BF)
        qs=q*m
        s=dot_t(k,qs)
        s=jnp.where(row<SEQ,s,-1e30)
        mx=jnp.max(s,axis=0,keepdims=True)
        e=jnp.exp(s-mx)
        p=e*(1.0/jnp.sum(e,axis=0,keepdims=True))
        pb=p.astype(BF)
        dp=dot_t(v,do*m1)
        dl=jnp.sum(p*dp,axis=0,keepdims=True)
        ds=(p*(dp-dl)).astype(BF)
        dv=dot(pb,do)
        dk=dot(ds,qs)
        dq=dot_0(ds,k)*0.125
        r.append((dq,dk,dv))
    return tuple(jnp.where(lane<64,a,b) for a,b in zip(*r))

def ka_kernel(h_ref,w_ref,vec_ref,qkv_ref,o_ref,a_ref):
    h=h_ref[0].astype(F32)
    xc,rs=norm_stats(h)
    a_ref[0]=(xc*rs*vec_ref[0:1]+vec_ref[1:2]).astype(BF)
    a=a_ref[0]
    for c in range(3):
        cs=slice(256*c,256*c+256)
        qkv_ref[0,:,256*c:256*c+256]=(dot(a,w_ref[:,256*c:256*c+256])+vec_ref[2:3,cs]).astype(BF)
        qkv_ref[0,:,D+256*c:D+256*c+256]=dot(a,w_ref[:,D+256*c:D+256*c+256]).astype(BF)
        qkv_ref[0,:,2*D+256*c:2*D+256*c+256]=(dot(a,w_ref[:,2*D+256*c:2*D+256*c+256])+vec_ref[3:4,cs]).astype(BF)
        for p in range(2):
            b=256*c+128*p
            o_ref[0,:,b:b+128]=attn_fwd(qkv_ref[0,:,b:b+128],qkv_ref[0,:,D+b:D+b+128],qkv_ref[0,:,2*D+b:2*D+b+128])

def img(n,dt=None): return pl.BlockSpec((1,RP,n),lambda i:(i,0,0))
def full(shape): return pl.BlockSpec(shape,lambda i:(0,)*len(shape))
PAR=pltpu.CompilerParams(vmem_limit_bytes=60*2**20)

def ka(h,w,vec):
    n=h.shape[0]
    return pl.pallas_call(ka_kernel,grid=(n,),in_specs=[img(D),full(w.shape),full(vec.shape)],
        out_specs=[img(3*D),img(D),img(D)],
        out_shape=[jax.ShapeDtypeStruct((n,RP,3*D),BF),jax.ShapeDtypeStruct((n,RP,D),BF),jax.ShapeDtypeStruct((n,RP,D),BF)],
        compiler_params=PAR)(h,w,vec)

def gelu_parts(u):
    c=0.5*(1.0+lax.erf(u*0.7071067811865476))
    g=c+u*(jnp.exp(-0.5*u*u)*0.3989422804014327)
    return u*c,g

def kb_kernel(FC,h_ref,o_ref,wo_ref,w1_ref,w2_ref,vec_ref,h1_ref,a_ref,e_ref,g_ref,h2_ref):
    h1=h_ref[0].astype(F32)+dot(o_ref[0],wo_ref[...])+vec_ref[4:5]
    h1_ref[0]=h1
    xc,rs=norm_stats(h1)
    a_ref[0]=(xc*rs*vec_ref[5:6]+vec_ref[6:7]).astype(BF)
    a=a_ref[0]
    h2_ref[0]=h1+vec_ref[7:8]
    for j in range(3072//FC):
        lo=FC*j
        u=dot(a,w1_ref[:,lo:lo+FC])+vec_ref[8+lo//D:9+lo//D,lo%D:lo%D+FC]
        e,g=gelu_parts(u)
        e_ref[0,:,lo:lo+FC]=e.astype(BF); g_ref[0,:,lo:lo+FC]=g.astype(BF)
        h2_ref[0]+=dot(e_ref[0,:,lo:lo+FC],w2_ref[lo:lo+FC,:])

def kb(h,o,wo,w1,w2,vec,FC=256):
    n=h.shape[0]
    S=jax.ShapeDtypeStruct
    return pl.pallas_call(functools.partial(kb_kernel,FC),grid=(n,),in_specs=[img(D),img(D),full(wo.shape),full(w1.shape),full(w2.shape),full(vec.shape)],
        out_specs=[img(D),img(D),img(3072),img(3072),img(D)],
        out_shape=[S((n,RP,D),F32),S((n,RP,D),BF),S((n,RP,3072),BF),S((n,RP,3072),BF),S((n,RP,D),F32)],
        compiler_params=PAR)(h,o,wo,w1,w2,vec)

def rsum(x): return jnp.sum(x,axis=0,keepdims=True)
def norm_back(x,gain,dy):
    xc,rs=norm_stats(x); xh=xc*rs
    dyg=dy*gain
    dx=rs*(dyg-jnp.mean(dyg,axis=-1,keepdims=True)-xh*jnp.mean(dyg*xh,axis=-1,keepdims=True))
    return dx, rsum(dy*xh), rsum(dy)

def kc_kernel(FC,d_ref,h1_ref,g_ref,wo_ref,w1_ref,w2_ref,vec_ref,db_ref,du_ref,dh1_ref,dh1b_ref,do_ref,dv_ref,acc_ref):
    @pl.when(pl.program_id(0)==0)
    def _(): dv_ref[...]=jnp.zeros_like(dv_ref)
    d=d_ref[0].astype(F32)
    db_ref[0]=d.astype(BF)
    db=db_ref[0]
    dv_ref[7:8]+=rsum(d)
    for j in range(3072//FC):
        lo=FC*j
        du=dot_t(db,w2_ref[lo:lo+FC,:])*g_ref[0,:,lo:lo+FC].astype(F32)
        dv_ref[8+lo//D:9+lo//D,lo%D:lo%D+FC]+=rsum(du)
        du_ref[0,:,lo:lo+FC]=du.astype(BF)
        t=dot_t(du_ref[0,:,lo:lo+FC],w1_ref[:,lo:lo+FC])
        if j==0: acc_ref[...]=t
        else: acc_ref[...]+=t
    dx,dg,dc=norm_back(h1_ref[0],vec_ref[5:6],acc_ref[...])
    dv_ref[5:6]+=dg; dv_ref[6:7]+=dc
    dh1=d_ref[0].astype(F32)+dx
    dh1_ref[0]=dh1
    dv_ref[4:5]+=rsum(dh1)
    dh1b_ref[0]=dh1.astype(BF)
    do_ref[0]=dot_t(dh1b_ref[0],wo_ref[...]).astype(BF)

def kc(d,h1,g,wo,w1,w2,vec,FC=256):
    n=d.shape[0]; S=jax.ShapeDtypeStruct
    return pl.pallas_call(functools.partial(kc_kernel,FC),grid=(n,),in_specs=[img(D),img(D),img(3072),full(wo.shape),full(w1.shape),full(w2.shape),full(vec.shape)],
        out_specs=[img(D),img(3072),img(D),img(D),img(D),full((16,D))],
        out_shape=[S((n,RP,D),BF),S((n,RP,3072),BF),S((n,RP,D),F32),S((n,RP,D),BF),S((n,RP,D),BF),S((16,D),F32)],
        scratch_shapes=[pltpu.VMEM((RP,D),F32)],
        compiler_params=PAR)(d,h1,g,wo,w1,w2,vec)

def kd_kernel(qkv_ref,do_ref,dz_ref,dv_ref):
    @pl.when(pl.program_id(0)==0)
    def _(): dv_ref[...]=jnp.zeros_like(dv_ref)
    for p in range(6):
        b=128*p
        dq,dk,dv=attn_bwd(qkv_ref[0,:,b:b+128],qkv_ref[0,:,D+b:D+b+128],qkv_ref[0,:,2*D+b:2*D+b+128],do_ref[0,:,b:b+128])
        dv_ref[2:3,b:b+128]+=rsum(dq); dv_ref[3:4,b:b+128]+=rsum(dv)
        dz_ref[0,:,b:b+128]=dq.astype(BF); dz_ref[0,:,D+b:D+b+128]=dk.astype(BF); dz_ref[0,:,2*D+b:2*D+b+128]=dv.astype(BF)

def kd(qkv,do):
    n=do.shape[0]; S=jax.ShapeDtypeStruct
    return pl.pallas_call(kd_kernel,grid=(n,),in_specs=[img(3*D),img(D)],out_specs=[img(3*D),full((16,D))],
        out_shape=[S((n,RP,3*D),BF),S((16,D),F32)],compiler_params=PAR)(qkv,do)

def kf_kernel(dz_ref,h_ref,dh1_ref,w_ref,vec_ref,dh_ref,dv_ref):
    @pl.when(pl.program_id(0)==0)
    def _(): dv_ref[...]=jnp.zeros_like(dv_ref)
    da=dot_t(dz_ref[0],w_ref[...])
    dx,dg,dc=norm_back(h_ref[0].astype(F32),vec_ref[0:1],da)
    dv_ref[0:1]+=dg; dv_ref[1:2]+=dc
    rows=dh_ref.shape[1]
    dh_ref[0]=(dh1_ref[0]+dx)[:rows]

def kf(dz,h,dh1,w,vec,rows=RP):
    n=dz.shape[0]; S=jax.ShapeDtypeStruct
    return pl.pallas_call(kf_kernel,grid=(n,),in_specs=[img(3*D),img(D),img(D),full(w.shape),full(vec.shape)],
        out_specs=[pl.BlockSpec((1,rows,D),lambda i:(i,0,0)),full((16,D))],
        out_shape=[S((n,rows,D),F32),S((16,D),F32)],compiler_params=PAR)(dz,h,dh1,w,vec)

def dw_kernel(l_ref,r_ref,o_ref):
    o_ref[...]=dot_0(l_ref[...],r_ref[...]).astype(BF)
def dw(l,r,MB=256):
    M=l.shape[-1]; N=r.shape[-1]; K=l.shape[0]*RP
    l=l.reshape(K,M); r=r.reshape(K,N)
    return pl.pallas_call(dw_kernel,grid=(M//MB,),in_specs=[pl.BlockSpec((K,MB),lambda i:(0,i)),pl.BlockSpec((K,N),lambda i:(0,0))],
       out_specs=pl.BlockSpec((MB,N),lambda i:(i,0)),out_shape=jax.ShapeDtypeStruct((M,N),BF),compiler_params=PAR)(l,r)


LAYERS = 2
STEP = 3
beta_one = 0.9
beta_two = 0.999
matrix_rate = 0.03
vector_rate = 0.2
matrix_decay = 0.05
adam_eps = 1e-8


def adam_update(master, gradient, moment_one, moment_two, rate, decay_rate):
    moment_one = beta_one * moment_one + (1.0 - beta_one) * gradient
    moment_two = beta_two * moment_two + (1.0 - beta_two) * gradient * gradient
    corr_one = 1.0 - beta_one**STEP
    corr_two = 1.0 - beta_two**STEP
    adam_move = moment_one / corr_one / (jnp.sqrt(moment_two / corr_two) + adam_eps)
    return (master - rate * (adam_move + decay_rate * master), moment_one, moment_two)


def swap(x, axis, size, mask):
    return lax.ppermute(x, axis, [(i, i ^ mask) for i in range(size)])


def halve(x, order, size):
    bits = size.bit_length() - 1
    me = lax.axis_index("fsdp")
    x = x.reshape((2,) * bits + x.shape[1:])
    left = list(range(bits))[::-1]
    for bit in order:
        at = left.index(bit)
        mine = (me >> bit) & 1
        keep = lax.dynamic_index_in_dim(x, mine, at, keepdims=False)
        send = lax.dynamic_index_in_dim(x, 1 - mine, at, keepdims=False)
        got = swap(send, "fsdp", size, 1 << bit)
        x = (keep.astype(F32) + got.astype(F32)).astype(BF)
        left.remove(bit)
    return x


def reduce_all(x, nf, nr):
    bits = nf.bit_length() - 1
    rows, cols = x.shape
    x = x.reshape(nf, rows // nf, cols)
    half = cols // 2 // 128 * 128
    up = [0] + list(range(1, bits))
    down = [0] + list(range(1, bits))[::-1]
    x = jnp.concatenate([halve(x[..., :half], up, nf), halve(x[..., half:], down, nf)], axis=-1)
    mask = 1
    while mask < nr:
        got = swap(x, "rep", nr, 2 * mask - 1)
        y = x.astype(F32) + got.astype(F32)
        x = y.astype(BF)
        mask *= 2
    return y


def make_shards(nf, nr):
    def shards(images, cotangent, weight_in, weight_out, vector_params, first_in, first_out, first_vec, second_in, second_out, second_vec):
        pad = lambda a: jnp.pad(a, ((0, 0), (0, RP - SEQ), (0, 0)))
        vec_all = lax.all_gather(vector_params.astype(BF), "fsdp", axis=1, tiled=True).astype(F32)
        h = pad(images)
        ct = pad(cotangent)
        saved = []
        for l in range(LAYERS):
            win = lax.all_gather(weight_in[l].astype(BF), "fsdp", axis=0, tiled=True)
            wout = lax.all_gather(weight_out[l].astype(BF), "fsdp", axis=0, tiled=True)
            vec = jnp.pad(vec_all[l].reshape(12, D), ((0, 4), (0, 0)))
            wqkv, w1, wo, w2 = win[:, : 3 * D], win[:, 3 * D :], wout[:D], wout[D:]
            qkv, o, a1 = ka(h, wqkv, vec)
            h1, a2, e, g, h2 = kb(h, o, wo, w1, w2, vec)
            saved.append((h, wqkv, w1, wo, w2, vec, qkv, o, a1, h1, a2, e, g))
            h = h2
        encoded = h[:, :SEQ].astype(BF)
        d = ct
        gin, gout, gvec = [None] * LAYERS, [None] * LAYERS, [None] * LAYERS
        for l in reversed(range(LAYERS)):
            h, wqkv, w1, wo, w2, vec, qkv, o, a1, h1, a2, e, g = saved[l]
            db, du, dh1, dh1b, do, dv1 = kc(d, h1, g, wo, w1, w2, vec)
            g1 = reduce_all(dw(a2, du), nf, nr)
            go = reduce_all(jnp.concatenate([dw(o, dh1b), dw(e, db)], axis=0), nf, nr)
            dz, dv2 = kd(qkv, do)
            gq = reduce_all(dw(a1, dz), nf, nr)
            d, dv3 = kf(dz, h, dh1, wqkv, vec, RP if l else SEQ)
            gin[l] = jnp.concatenate([gq, g1], axis=1)
            gout[l] = go
            gvec[l] = (dv1 + dv2 + dv3)[:12].reshape(-1)
        gv = lax.psum(jnp.stack(gvec), ("fsdp", "rep"))
        wide = gv.shape[1] // nf
        gv = lax.dynamic_slice_in_dim(gv, lax.axis_index("fsdp") * wide, wide, 1)
        gi, go = jnp.stack(gin), jnp.stack(gout)
        new_in, moment_in, square_in = adam_update(weight_in, gi, first_in, second_in, matrix_rate, matrix_decay)
        new_out, moment_out, square_out = adam_update(weight_out, go, first_out, second_out, matrix_rate, matrix_decay)
        new_vec, moment_vec, square_vec = adam_update(vector_params, gv, first_vec, second_vec, vector_rate, 0.0)
        return (encoded, d, gi, go, gv, new_in, new_out, new_vec, moment_in, moment_out, moment_vec, square_in, square_out, square_vec)

    return shards


def solution(mesh):
    tokens = P(("fsdp", "rep"), None, None)
    matrix = P(None, "fsdp", None)
    vector = P(None, "fsdp")
    in_specs = (tokens, tokens) + (matrix, matrix, vector) * 3
    out_specs = (tokens, tokens) + (matrix, matrix, vector) * 4
    return jax.shard_map(make_shards(mesh.shape["fsdp"], mesh.shape["rep"]), mesh=mesh, in_specs=in_specs, out_specs=out_specs, check_vma=False)
```

time: 1130 us -> 1030 us (0.912)
  Pallas kernels: 0 us -> 311 us
  matrix products: 307 us -> 0 us
  local copies, waits for them, and re-layouts: 196 us -> 80.9 us
  waiting for transfers between devices: 476 us -> 531 us
  other arithmetic: 94.5 us -> 41.2 us
  starting transfers between devices: 1.22 us -> 37.3 us
  blocking collectives: 27.4 us -> 9.09 us
    pallas_call x0 -> x18, Pallas kernels: none -> 311 us  [the longest x8 76.9 us: dw(): pl.pallas_call(dw_kernel, grid=(M // MB,), in_specs=[pl.BlockSpec((K, MB)...]
    dot_general x36 -> x0, matrix products: 307 us -> none  [the longest x8 81.8 us: back_product(): lax.dot_general(matrix_a, matrix_b, (((1,), (1,)), ((), ())), preferred_e...]
    ppermute x0 -> x48, waiting for transfers between devices: none -> 249 us  [swap(): return lax.ppermute(x, axis, [(i, i ^ mask) for i in range(size)])]
    reduce_scatter x4 -> x0, waiting for transfers between devices: 175 us -> none  [the longest x2 175 us: shards(): lax.psum_scatter(grad_in_w, 'fsdp', scatter_dimension=0, tiled=True)]
    all_gather x4, waiting for transfers between devices: 26.2 us -> 164 us  [the longest x2 93.7 us: shards(): win = lax.all_gather(weight_in[l].astype(BF), 'fsdp', axis=0, tiled=True)]
    psum x1, waiting for transfers between devices: 240 us -> 116 us  [shards(): gv = lax.psum(jnp.stack(gvec), ('fsdp', 'rep'))]
    reshape x24 -> x0, local copies, waits for them, and re-layouts: 122 us -> none  [the longest x16 87.1 us: heads_view(): return matrix_a.reshape(-1, SEQ, HEADS, HEAD_DIM)]
    slice x9 -> x18, local copies, waits for them, and re-layouts: 5.41 us -> 50.3 us  [the longest x8 30 us: shards(): wqkv, w1, wo, w2 = (win[:, :3 * D], win[:, 3 * D:], wout[:D], wout[D:])]
  transfers between devices with their start and end apart: 10 -> 53, of which waited for: 5 -> 29; matrix products, arithmetic and copies ran while one was open for 42% -> 9% of each run, Pallas kernels for 0% -> 16%
where the time goes in v1:
time: 1030 us
  waiting for transfers between devices  531 us (52%)
  Pallas kernels  311 us (30%)
  local copies, waits for them, and re-layouts  80.9 us (8%)
  other arithmetic  41.2 us (4%)
  starting transfers between devices  37.3 us (4%)
  between operations  15.2 us (1%)
    ppermute x48, waiting for transfers between devices, swap(): return lax.ppermute(x, axis, [(i, i ^ mask) for i in range(size)])  249 us
    psum x1, waiting for transfers between devices, shards(): gv = lax.psum(jnp.stack(gvec), ('fsdp', 'rep'))  116 us
    all_gather x2, waiting for transfers between devices, shards(): win = lax.all_gather(weight_in[l].astype(BF), 'fsdp', axis=0, tiled=True)  93.7 us
    pallas_call x8, Pallas kernels, dw(): pl.pallas_call(dw_kernel, grid=(M // MB,), in_specs=[pl.BlockSpec((K, MB)...  76.9 us
    all_gather x2, waiting for transfers between devices, shards(): wout = lax.all_gather(weight_out[l].astype(BF), 'fsdp', axis=0, tiled=True)  70.6 us
    pallas_call x2, Pallas kernels, kb(): pl.pallas_call(functools.partial(kb_kernel, FC), grid=(n,), in_specs=[img...  66.2 us
    pallas_call x2, Pallas kernels, kd(): pl.pallas_call(kd_kernel, grid=(n,), in_specs=[img(3 * D), img(D)], out_s...  48.9 us
    pallas_call x2, Pallas kernels, ka(): pl.pallas_call(ka_kernel, grid=(n,), in_specs=[img(D), full(w.shape), ful...  48.5 us
  transfers between devices with their start and end apart: 53, of which 29 were waited for; matrix products, arithmetic and copies ran while one was open for 9% of the time, Pallas kernels for 16%

profile of v1, /device:TPU:8, one launch (start us, length us, event | category | flops | bytes accessed | tf_op | source)
XLA Modules:
  0.0 1025.7 jit_solution(14425502363363729427)
XLA Ops:
  11.2 2.4 convert.47
  15.8 9.1 all_gather.16
  29.0 26.7 %all-gather.11.cloned.1.call-done = bf16[1,3840,768]{2,1,0:T(8,128)(2,1)} async-done(((bf16[1,480,768]{2,1,0:T(8,128)(2,1)}), bf16[1,3840,768]{2,1,0:T(8,128)(2,1)}) %all-gather.11.cloned.1.call-update) | async-done | bytes 5898256 | tf_op jit(solution)/shard_map/all_gather | solution.py:250
  55.6 2.4 slice_bitcast_fusion.3.wo_ref
  58.0 43.9 %all-gather.15.cloned.1.call-done = bf16[1,3840,768]{2,1,0:T(8,128)(2,1)} async-done(((bf16[1,480,768]{2,1,0:T(8,128)(2,1)}), bf16[1,3840,768]{2,1,0:T(8,128)(2,1)}) %all-gather.15.cloned.1.call-update) | async-done | bytes 5898256 | tf_op jit(solution)/shard_map/all_gather | solution.py:250
  102.0 2.6 slice_bitcast_fusion.2.wo_ref
  104.6 5.0 slice_bitcast_fusion.1.w2_ref
  109.6 2.4 slice_bitcast_fusion.w2_ref
  112.0 46.3 %all-gather.9.cloned.1.call-done = bf16[1,768,5376]{2,1,0:T(8,128)(2,1)} async-done(((bf16[1,96,5376]{2,1,0:T(8,128)(2,1)}), bf16[1,768,5376]{2,1,0:T(8,128)(2,1)}) %all-gather.9.cloned.1.call-update) | async-done | bytes 8257552 | tf_op jit(solution)/shard_map/all_gather | solution.py:249
  158.3 4.0 slice.126.w_ref
  162.4 4.7 slice.130.w1_ref
  167.1 47.4 %all-gather.13.cloned.1.call-done = bf16[1,768,5376]{2,1,0:T(8,128)(2,1)} async-done(((bf16[1,96,5376]{2,1,0:T(8,128)(2,1)}), bf16[1,768,5376]{2,1,0:T(8,128)(2,1)}) %all-gather.13.cloned.1.call-update) | async-done | bytes 8257552 | tf_op jit(solution)/shard_map/all_gather | solution.py:249
  214.5 4.0 slice.133.w_ref
  218.5 4.8 slice.137.w1_ref
  223.3 24.3 %shard_map.218 = (bf16[5,208,2304]{2,1,0:T(8,128)(2,1)}, bf16[5,208,768]{2,1,0:T(8,128)(2,1)}, bf16[5,208,768]{2,1,0:T(8,128)(2,1)}) custom-call(bf16[5,208,768]{2,1,0:T(8,128)(2,1)} %pad.14.h_ref, bf16[768,2304]{1,0:T(8,128)(2,1)} %slice.126.w_ref, f32[16,768]{1,0:T(8,128)} %pad.15.vec_ref), custom_call_target="tpu_custom_call" | custom-call | tf_op jit(solution)/shard_map/pallas_call | solution.py:77
  247.7 33.0 %shard_map.219 = (f32[5,208,768]{2,1,0:T(8,128)}, bf16[5,208,768]{2,1,0:T(8,128)(2,1)}, bf16[5,208,3072]{2,1,0:T(8,128)(2,1)}, bf16[5,208,3072]{2,1,0:T(8,128)(2,1)}, f32[5,208,768]{2,1,0:T(8,128)}) custom-call(bf16[5,208,768]{2,1,0:T(8,128)(2,1)} %pad.14.h_ref, bf16[5,208,768]{2,1,0:T(8,128)(2,1)} %get-tuple-element.50.o_ref, ...), custom_call_target="tpu_custom_call" | custom-call | tf_op jit(solution)/shard_map/pallas_call | solution.py:104
  280.7 24.2 %shard_map.220 = (bf16[5,208,2304]{2,1,0:T(8,128)(2,1)}, bf16[5,208,768]{2,1,0:T(8,128)(2,1)}, bf16[5,208,768]{2,1,0:T(8,128)(2,1)}) custom-call(f32[5,208,768]{2,1,0:T(8,128)} %get-tuple-element.51.h_ref, bf16[768,2304]{1,0:T(8,128)(2,1)} %slice.133.w_ref, f32[16,768]{1,0:T(8,128)} %pad.16.vec_ref), custom_call_target="tpu_custom_call" | custom-call | tf_op jit(solution)/shard_map/pallas_call | solution.py:77
  304.8 33.2 %shard_map.221 = (f32[5,208,768]{2,1,0:T(8,128)}, bf16[5,208,768]{2,1,0:T(8,128)(2,1)}, bf16[5,208,3072]{2,1,0:T(8,128)(2,1)}, bf16[5,208,3072]{2,1,0:T(8,128)(2,1)}, f32[5,208,768]{2,1,0:T(8,128)}) custom-call(f32[5,208,768]{2,1,0:T(8,128)} %get-tuple-element.51.h_ref, bf16[5,208,768]{2,1,0:T(8,128)(2,1)} %get-tuple-element.52.o_ref, ...), custom_call_target="tpu_custom_call" | custom-call | tf_op jit(solution)/shard_map/pallas_call | solution.py:104
  338.0 3.1 slice.179
  341.2 23.7 %shard_map.222 = (bf16[5,208,768]{2,1,0:T(8,128)(2,1)}, bf16[5,208,3072]{2,1,0:T(8,128)(2,1)}, f32[5,208,768]{2,1,0:T(8,128)}, bf16[5,208,768]{2,1,0:T(8,128)(2,...) custom-call(bf16[5,208,768]{2,1,0:T(8,128)(2,1)} %pad.17.d_ref, f32[5,208,768]{2,1,0:T(8,128)} %get-tuple-element.56.h1_ref, ...), custom_call_target="tpu_custom_call" | custom-call | tf_op jit(solution)/shard_map/pallas_call | solution.py:141
  364.9 11.0 %shard_map.231 = bf16[768,3072]{1,0:T(8,128)(2,1)} custom-call(bf16[1040,768]{1,0:T(8,128)(2,1)} %bitcast.307, bf16[1040,3072]{1,0:T(8,128)(2,1)} %bitcast.298), custom_call_target="tpu_custom_call" | custom-call | tf_op jit(solution)/shard_map/pallas_call | solution.py:181
  375.9 2.8 fusion.47
  382.9 24.6 %shard_map.223 = (bf16[5,208,2304]{2,1,0:T(8,128)(2,1)}, f32[16,768]{1,0:T(8,128)}) custom-call(bf16[5,208,2304]{2,1,0:T(8,128)(2,1)} %get-tuple-element.55.qkv_ref, bf16[5,208,768]{2,1,0:T(8,128)(2,1)} %get-tuple-element.58.do_ref), custom_call_target="tpu_custom_call" | custom-call | tf_op jit(solution)/shard_map/pallas_call | solution.py:158
  407.4 11.9 %shard_map.224 = (f32[5,208,768]{2,1,0:T(8,128)}, f32[16,768]{1,0:T(8,128)}) custom-call(bf16[5,208,2304]{2,1,0:T(8,128)(2,1)} %get-tuple-element.59.dz_ref, f32[5,208,768]{2,1,0:T(8,128)} %get-tuple-element.51.h_ref, f32[5,208,768]{2,1,0:T(8,128)} %get-tuple-element.60.dh1_ref, bf16[768,2304]{1,0:T(8,128)(2,1)} %slice.133.w_ref, f32[16,768]{1,0:T(8,128)} %pad.16.vec_ref), custom_call_target="tpu_custom_call" | custom-call | tf_op jit(solution)/shard_map/pallas_call | solution.py:172
  419.3 8.8 shard_map.230
  434.0 23.6 %shard_map.225 = (bf16[5,208,768]{2,1,0:T(8,128)(2,1)}, bf16[5,208,3072]{2,1,0:T(8,128)(2,1)}, f32[5,208,768]{2,1,0:T(8,128)}, bf16[5,208,768]{2,1,0:T(8,128)(2,...) custom-call(f32[5,208,768]{2,1,0:T(8,128)} %get-tuple-element.61.d_ref, f32[5,208,768]{2,1,0:T(8,128)} %get-tuple-element.62.h1_ref, ...), custom_call_target="tpu_custom_call" | custom-call | tf_op jit(solution)/shard_map/pallas_call | solution.py:141
  457.7 10.9 %shard_map.229 = bf16[768,3072]{1,0:T(8,128)(2,1)} custom-call(bf16[1040,768]{1,0:T(8,128)(2,1)} %bitcast.304, bf16[1040,3072]{1,0:T(8,128)(2,1)} %bitcast.299), custom_call_target="tpu_custom_call" | custom-call | tf_op jit(solution)/shard_map/pallas_call | solution.py:181
  468.6 2.8 fusion.46
  474.4 24.3 %shard_map.226 = (bf16[5,208,2304]{2,1,0:T(8,128)(2,1)}, f32[16,768]{1,0:T(8,128)}) custom-call(bf16[5,208,2304]{2,1,0:T(8,128)(2,1)} %get-tuple-element.54.qkv_ref, bf16[5,208,768]{2,1,0:T(8,128)(2,1)} %get-tuple-element.64.do_ref), custom_call_target="tpu_custom_call" | custom-call | tf_op jit(solution)/shard_map/pallas_call | solution.py:158
  498.7 11.4 %shard_map.227 = (f32[5,197,768]{2,1,0:T(8,128)}, f32[16,768]{1,0:T(8,128)}) custom-call(bf16[5,208,2304]{2,1,0:T(8,128)(2,1)} %get-tuple-element.65.dz_ref, bf16[5,208,768]{2,1,0:T(8,128)(2,1)} %pad.14.h_ref, f32[5,208,768]{2,1,0:T(8,128)} %get-tuple-element.66.dh1_ref, bf16[768,2304]{1,0:T(8,128)(2,1)} %slice.126.w_ref, f32[16,768]{1,0:T(8,128)} %pad.15.vec_ref), custom_call_target="tpu_custom_call" | custom-call | tf_op jit(solution)/shard_map/pallas_call | solution.py:172
  510.2 8.8 shard_map.228
  519.0 3.5 fusion.48
  524.9 13.6 %shard_map.235 = bf16[3072,768]{1,0:T(8,128)(2,1)} custom-call(bf16[1040,3072]{1,0:T(8,128)(2,1)} %bitcast.297, bf16[1040,768]{1,0:T(8,128)(2,1)} %bitcast.303), custom_call_target="tpu_custom_call" | custom-call | tf_op jit(solution)/shard_map/pallas_call | solution.py:181
  538.5 5.0 shard_map.234
  543.4 3.1 pad_maximum_fusion.1
  550.6 13.6 %shard_map.233 = bf16[3072,768]{1,0:T(8,128)(2,1)} custom-call(bf16[1040,3072]{1,0:T(8,128)(2,1)} %bitcast.296, bf16[1040,768]{1,0:T(8,128)(2,1)} %bitcast.305), custom_call_target="tpu_custom_call" | custom-call | tf_op jit(solution)/shard_map/pallas_call | solution.py:181
  564.2 5.2 shard_map.232
  569.4 3.1 pad_maximum_fusion
  575.6 2.6 dynamic-slice_bitcast_fusion.1
  583.7 116.0 %all-reduce.6.cloned.1.call-done = f32[2,9216]{1,0:T(2,128)} async-done(((f32[2,9216]{1,0:T(2,128)}), f32[2,9216]{1,0:T(2,128)}) %all-reduce.6.cloned.1.call-update) | async-done | bytes 73744 | tf_op jit(solution)/shard_map/psum | solution.py:271
  715.9 10.4 %collective-permute-done.20 = bf16[2,96,1152]{2,1,0:T(8,128)(2,1)S(1)} collective-permute-done((bf16[2,96,1152]{2,1,0:T(8,128)(2,1)S(1)}, bf16[2,96,1152]{2,1,0:T(8,128)(2,1)S(1)}, u32[]{:S(2)}, u32[]{:S(2)}) %collective-permute-start.20) | collective-permute-done | bytes 442400 | tf_op jit(solution)/shard_map/ppermute | solution.py:205
  727.9 9.9 collective-permute-done.4
  739.5 9.0 collective-permute-done.17
  750.0 8.0 collective-permute-done.1
  766.5 22.3 %collective-permute-done.21 = bf16[96,1152]{1,0:T(8,128)(2,1)S(1)} collective-permute-done((bf16[96,1152]{1,0:T(8,128)(2,1)S(1)}, bf16[96,1152]{1,0:T(8,128)(2,1)S(1)}, u32[]{:S(2)}, u32[]{:S(2)}) %collective-permute-start.21) | collective-permute-done | bytes 221216 | tf_op jit(solution)/shard_map/ppermute | solution.py:205
  789.6 5.2 collective-permute-done.18
  795.6 5.1 collective-permute-done.5
  801.5 7.6 collective-permute-done.2
  814.4 8.1 collective-permute-done.22
  822.7 8.0 collective-permute-done.6
  831.7 8.8 collective-permute-done.29
  841.7 5.5 collective-permute-done.26
  848.7 5.3 collective-permute-done.13
  855.4 5.3 collective-permute-done.10
  867.8 15.2 %collective-permute-done.23 = bf16[96,2304]{1,0:T(8,128)(2,1)S(1)} collective-permute-done((bf16[96,2304]{1,0:T(8,128)(2,1)S(1)}, bf16[96,2304]{1,0:T(8,128)(2,1)S(1)}, u32[]{:S(2)}, u32[]{:S(2)}) %collective-permute-start.23) | collective-permute-done | bytes 442400 | tf_op jit(solution)/shard_map/ppermute | solution.py:205
  884.5 5.9 collective-permute-done.7
  893.0 5.8 collective-permute-done.37
  903.0 13.5 %collective-permute-done.31 = bf16[96,3072]{1,0:T(8,128)(2,1)S(1)} collective-permute-done((bf16[96,3072]{1,0:T(8,128)(2,1)S(1)}, bf16[96,3072]{1,0:T(8,128)(2,1)S(1)}, u32[]{:S(2)}, u32[]{:S(2)}) %collective-permute-start.31) | collective-permute-done | bytes 589856 | tf_op jit(solution)/shard_map/ppermute | solution.py:205
  916.8 10.1 collective-permute-done.15
  927.5 6.9 collective-permute-done.38
  934.9 7.4 multiply_subtract_fusion
  942.4 58.2 %collective-permute-done.47 = bf16[480,768]{1,0:T(8,128)(2,1)S(1)} collective-permute-done((bf16[480,768]{1,0:T(8,128)(2,1)S(1)}, bf16[480,768]{1,0:T(8,128)(2,1)S(1)}, u32[]{:S(2)}, u32[]{:S(2)}) %collective-permute-start.47) | collective-permute-done | bytes 737312 | tf_op jit(solution)/shard_map/ppermute | solution.py:205
  1000.7 12.4 %collective-permute-done.39 = bf16[480,768]{1,0:T(8,128)(2,1)S(1)} collective-permute-done((bf16[480,768]{1,0:T(8,128)(2,1)S(1)}, bf16[480,768]{1,0:T(8,128)(2,1)S(1)}, u32[]{:S(2)}, u32[]{:S(2)}) %collective-permute-start.39) | collective-permute-done | bytes 737312 | tf_op jit(solution)/shard_map/ppermute | solution.py:205
  1013.3 5.5 multiply_subtract_fusion.1
  (282 shorter events, 96.9 us)
Async XLA Ops:
  7.2 48.5 %all-gather.11.cloned.1.call-start = ((), (), s32[]{:S(2)}) async-start(), calls=%async_computation.2 | async-start | bytes 6635520 | tf_op jit(solution)/shard_map/all_gather | solution.py:250
  10.4 91.6 %all-gather.15.cloned.1.call-start = ((), (), s32[]{:S(2)}) async-start(), calls=%async_computation.4 | async-start | bytes 6635520 | tf_op jit(solution)/shard_map/all_gather | solution.py:250
  11.2 147.1 %all-gather.9.cloned.1.call-start = ((), (), s32[]{:S(2)}) async-start(), calls=%async_computation.1 | async-start | bytes 9289728 | tf_op jit(solution)/shard_map/all_gather | solution.py:249
  15.1 11.3 %copy-start.23 = (bf16[5,197,768]{2,1,0:T(8,128)(2,1)S(1)}, bf16[5,197,768]{2,1,0:T(8,128)(2,1)}, u32[]{:S(2)}) copy-start(bf16[5,197,768]{2,1,0:T(8,128)(2,1)} %param.11) | copy-start | bytes 4538884
  15.1 199.4 %all-gather.13.cloned.1.call-start = ((), (), s32[]{:S(2)}) async-start(), calls=%async_computation.3 | async-start | bytes 9289728 | tf_op jit(solution)/shard_map/all_gather | solution.py:249
  15.7 684.0 %all-reduce.6.cloned.1.call-start = ((), (), s32[]{:S(2)}) async-start(), calls=%async_computation | async-start | bytes 147456 | tf_op jit(solution)/shard_map/psum | solution.py:271
  102.0 7.6 slice-start
  379.9 328.5 %collective-permute-start.27 = (bf16[2,2,96,1536]{3,2,1,0:T(8,128)(2,1)}, bf16[2,2,96,1536]{3,2,1,0:T(8,128)(2,1)}, u32[]{:S(2)}, u32[]{:S(2)}) collective-permute-start(bf16[2,2,96,1536]{3,2,1,0:T(8,128)(2,1)} %dynamic-slice_bitcast_fusion.3), channel_id=1, source_target_pairs={{0,4},{4,0},{8,12},{12,8},{16,20},{20,16},{24,28},{28,24},{1,5},{5... | collective-permute-start | bytes 3538952 | tf_op jit(solution)/shard_map/ppermute | solution.py:205
  382.6 328.2 %collective-permute-start.24 = (bf16[2,2,96,1536]{3,2,0,1:T(8,128)(2,1)}, bf16[2,2,96,1536]{3,2,0,1:T(8,128)(2,1)}, u32[]{:S(2)}, u32[]{:S(2)}) collective-permute-start(bf16[2,2,96,1536]{3,2,0,1:T(8,128)(2,1)} %bitcast.259), channel_id=1, source_target_pairs={{0,4},{4,0},{8,12},{12,8},{16,20},{20,16},{24,28},{28,24},{1,5},{5... | collective-permute-start | bytes 3538952 | tf_op jit(solution)/shard_map/ppermute | solution.py:205
  431.5 269.7 %collective-permute-start.19 = (bf16[2,2,96,1152]{3,2,1,0:T(8,128)(2,1)}, bf16[2,2,96,1152]{3,2,1,0:T(8,128)(2,1)}, u32[]{:S(2)}, u32[]{:S(2)}) collective-permute-start(bf16[2,2,96,1152]{3,2,1,0:T(8,128)(2,1)} %dynamic-slice_bitcast_fusion.6), channel_id=1, source_target_pairs={{0,4},{4,0},{8,12},{12,8},{16,20},{20,16},{24,28},{28,24},{1,5},{5... | collective-permute-start | bytes 2654216 | tf_op jit(solution)/shard_map/ppermute | solution.py:205
  433.8 271.8 %collective-permute-start.16 = (bf16[2,2,96,1152]{3,2,0,1:T(8,128)(2,1)}, bf16[2,2,96,1152]{3,2,0,1:T(8,128)(2,1)}, u32[]{:S(2)}, u32[]{:S(2)}) collective-permute-start(bf16[2,2,96,1152]{3,2,0,1:T(8,128)(2,1)} %bitcast.260), channel_id=1, source_target_pairs={{0,4},{4,0},{8,12},{12,8},{16,20},{20,16},{24,28},{28,24},{1,5},{5... | collective-permute-start | bytes 2654216 | tf_op jit(solution)/shard_map/ppermute | solution.py:205
  524.6 178.2 %collective-permute-start.3 = (bf16[2,2,96,1152]{3,2,1,0:T(8,128)(2,1)}, bf16[2,2,96,1152]{3,2,1,0:T(8,128)(2,1)}, u32[]{:S(2)}, u32[]{:S(2)}) collective-permute-start(bf16[2,2,96,1152]{3,2,1,0:T(8,128)(2,1)} %dynamic-slice_bitcast_fusion.7), channel_id=1, source_target_pairs={{0,4},{4,0},{8,12},{12,8},{16,20},{20,16},{24,28},{28,24},{1,5},{5... | collective-permute-start | bytes 2654216 | tf_op jit(solution)/shard_map/ppermute | solution.py:205
  581.7 118.0 %copy-start.37 = (f32[2,1152]{1,0:T(2,128)S(1)}, f32[2,1152]{1,0:T(2,128)}, u32[]{:S(2)}) copy-start(f32[2,1152]{1,0:T(2,128)} %param.18) | copy-start | bytes 27652
  581.7 118.0 %copy-start.38 = (f32[2,1152]{1,0:T(2,128)S(1)}, f32[2,1152]{1,0:T(2,128)}, u32[]{:S(2)}) copy-start(f32[2,1152]{1,0:T(2,128)} %param.21) | copy-start | bytes 27652
  701.2 4.0 collective-permute-start
  702.9 10.2 collective-permute-start.11
  705.2 8.8 collective-permute-start.8
  706.5 53.3 %collective-permute-start.43 = (bf16[2,2,480,384]{3,2,1,0:T(8,128)(2,1)S(1)}, bf16[2,2,480,384]{3,2,1,0:T(8,128)(2,1)S(1)}, u32[]{:S(2)}, u32[]{:S(2)}) collective-permute-start(bf16[2,2,480,384]{3,2,1,0:T(8,128)(2,1)S(1)} %copy-done.25), channel_id=1, source_target_pairs={{0,4},{4,0},{8,12},{12,8},{16,20},{20,16},{24,28},{28,24},{1,5},{5... | collective-permute-start | bytes 4423688 | tf_op jit(solution)/shard_map/ppermute | solution.py:205
  708.4 52.4 %collective-permute-start.40 = (bf16[2,2,480,384]{3,2,0,1:T(8,128)(2,1)S(1)}, bf16[2,2,480,384]{3,2,0,1:T(8,128)(2,1)S(1)}, u32[]{:S(2)}, u32[]{:S(2)}) collective-permute-start(bf16[2,2,480,384]{3,2,0,1:T(8,128)(2,1)S(1)} %bitcast.310), channel_id=1, source_target_pairs={{0,4},{4,0},{8,12},{12,8},{16,20},{20,16},{24,28},{28,24},{1,5},{5... | collective-permute-start | bytes 4423688 | tf_op jit(solution)/shard_map/ppermute | solution.py:205
  710.9 52.2 %collective-permute-start.35 = (bf16[2,2,480,384]{3,2,1,0:T(8,128)(2,1)S(1)}, bf16[2,2,480,384]{3,2,1,0:T(8,128)(2,1)S(1)}, u32[]{:S(2)}, u32[]{:S(2)}) collective-permute-start(bf16[2,2,480,384]{3,2,1,0:T(8,128)(2,1)S(1)} %copy-done.27), channel_id=1, source_target_pairs={{0,4},{4,0},{8,12},{12,8},{16,20},{20,16},{24,28},{28,24},{1,5},{5... | collective-permute-start | bytes 4423688 | tf_op jit(solution)/shard_map/ppermute | solution.py:205
  713.0 51.8 %collective-permute-start.32 = (bf16[2,2,480,384]{3,2,1,0:T(8,128)(2,1)S(1)}, bf16[2,2,480,384]{3,2,1,0:T(8,128)(2,1)S(1)}, u32[]{:S(2)}, u32[]{:S(2)}) collective-permute-start(bf16[2,2,480,384]{3,2,1,0:T(8,128)(2,1)S(1)} %copy-done.26), channel_id=1, source_target_pairs={{0,4},{4,0},{8,12},{12,8},{16,20},{20,16},{24,28},{28,24},{1,5},{5... | collective-permute-start | bytes 4423688 | tf_op jit(solution)/shard_map/ppermute | solution.py:205
  714.0 12.4 %collective-permute-start.20 = (bf16[2,96,1152]{2,1,0:T(8,128)(2,1)S(1)}, bf16[2,96,1152]{2,1,0:T(8,128)(2,1)S(1)}, u32[]{:S(2)}, u32[]{:S(2)}) collective-permute-start(bf16[2,96,1152]{2,1,0:T(8,128)(2,1)S(1)} %dynamic-slice_bitcast_fusion.17), channel_id=1, source_target_pairs={{0,16},{4,20},{8,24},{12,28},{16,0},{20,4},{24,8},{28,12},{1,17},{... | collective-permute-start | bytes 1327112 | tf_op jit(solution)/shard_map/ppermute | solution.py:205
  726.4 11.5 %collective-permute-start.4 = (bf16[2,96,1152]{2,1,0:T(8,128)(2,1)S(1)}, bf16[2,96,1152]{2,1,0:T(8,128)(2,1)S(1)}, u32[]{:S(2)}, u32[]{:S(2)}) collective-permute-start(bf16[2,96,1152]{2,1,0:T(8,128)(2,1)S(1)} %dynamic-slice_bitcast_fusion.19), channel_id=1, source_target_pairs={{0,16},{4,20},{8,24},{12,28},{16,0},{20,4},{24,8},{28,12},{1,17},{... | collective-permute-start | bytes 1327112 | tf_op jit(solution)/shard_map/ppermute | solution.py:205
  737.9 10.6 %collective-permute-start.17 = (bf16[2,96,1152]{2,1,0:T(8,128)(2,1)S(1)}, bf16[2,96,1152]{2,1,0:T(8,128)(2,1)S(1)}, u32[]{:S(2)}, u32[]{:S(2)}) collective-permute-start(bf16[2,96,1152]{2,1,0:T(8,128)(2,1)S(1)} %dynamic-slice_bitcast_fusion.18), channel_id=1, source_target_pairs={{0,8},{4,12},{8,0},{12,4},{16,24},{20,28},{24,16},{28,20},{1,9},{5... | collective-permute-start | bytes 1327112 | tf_op jit(solution)/shard_map/ppermute | solution.py:205
  748.4 9.6 collective-permute-start.1
  750.0 10.4 %copy-start.4 = (bf16[8,480,384]{2,1,0:T(8,128)(2,1)S(1)}, bf16[8,480,384]{2,1,0:T(8,128)(2,1)}, u32[]{:S(2)}) copy-start(bf16[8,480,384]{2,1,0:T(8,128)(2,1)} %copy-done.3) | copy-start | bytes 8847364
  758.1 51.8 %collective-permute-start.28 = (bf16[2,96,1536]{2,1,0:T(8,128)(2,1)S(1)}, bf16[2,96,1536]{2,1,0:T(8,128)(2,1)S(1)}, u32[]{:S(2)}, u32[]{:S(2)}) collective-permute-start(bf16[2,96,1536]{2,1,0:T(8,128)(2,1)S(1)} %dynamic-slice_bitcast_fusion.13), channel_id=1, source_target_pairs={{0,16},{4,20},{8,24},{12,28},{16,0},{20,4},{24,8},{28,12},{1,17},{... | collective-permute-start | bytes 1769480 | tf_op jit(solution)/shard_map/ppermute | solution.py:205
  759.8 51.7 %collective-permute-start.25 = (bf16[2,96,1536]{2,1,0:T(8,128)(2,1)S(1)}, bf16[2,96,1536]{2,1,0:T(8,128)(2,1)S(1)}, u32[]{:S(2)}, u32[]{:S(2)}) collective-permute-start(bf16[2,96,1536]{2,1,0:T(8,128)(2,1)S(1)} %dynamic-slice_bitcast_fusion.14), channel_id=1, source_target_pairs={{0,8},{4,12},{8,0},{12,4},{16,24},{20,28},{24,16},{28,20},{1,9},{5... | collective-permute-start | bytes 1769480 | tf_op jit(solution)/shard_map/ppermute | solution.py:205
  760.9 51.6 %collective-permute-start.12 = (bf16[2,96,1536]{2,1,0:T(8,128)(2,1)S(1)}, bf16[2,96,1536]{2,1,0:T(8,128)(2,1)S(1)}, u32[]{:S(2)}, u32[]{:S(2)}) collective-permute-start(bf16[2,96,1536]{2,1,0:T(8,128)(2,1)S(1)} %dynamic-slice_bitcast_fusion.15), channel_id=1, source_target_pairs={{0,16},{4,20},{8,24},{12,28},{16,0},{20,4},{24,8},{28,12},{1,17},{... | collective-permute-start | bytes 1769480 | tf_op jit(solution)/shard_map/ppermute | solution.py:205
  763.1 51.0 %collective-permute-start.9 = (bf16[2,96,1536]{2,1,0:T(8,128)(2,1)S(1)}, bf16[2,96,1536]{2,1,0:T(8,128)(2,1)S(1)}, u32[]{:S(2)}, u32[]{:S(2)}) collective-permute-start(bf16[2,96,1536]{2,1,0:T(8,128)(2,1)S(1)} %dynamic-slice_bitcast_fusion.16), channel_id=1, source_target_pairs={{0,8},{4,12},{8,0},{12,4},{16,24},{20,28},{24,16},{28,20},{1,9},{5... | collective-permute-start | bytes 1769480 | tf_op jit(solution)/shard_map/ppermute | solution.py:205
  764.8 24.0 %collective-permute-start.21 = (bf16[96,1152]{1,0:T(8,128)(2,1)S(1)}, bf16[96,1152]{1,0:T(8,128)(2,1)S(1)}, u32[]{:S(2)}, u32[]{:S(2)}) collective-permute-start(bf16[96,1152]{1,0:T(8,128)(2,1)S(1)} %dynamic-slice_bitcast_fusion.29), channel_id=1, source_target_pairs={{0,8},{4,12},{8,0},{12,4},{16,24},{20,28},{24,16},{28,20},{1,9},{5... | collective-permute-start | bytes 663560 | tf_op jit(solution)/shard_map/ppermute | solution.py:205
  788.8 5.9 collective-permute-start.18
  794.8 5.9 collective-permute-start.5
  800.7 8.4 collective-permute-start.2
  809.1 51.8 %collective-permute-start.44 = (bf16[2,480,384]{2,1,0:T(8,128)(2,1)S(1)}, bf16[2,480,384]{2,1,0:T(8,128)(2,1)S(1)}, u32[]{:S(2)}, u32[]{:S(2)}) collective-permute-start(bf16[2,480,384]{2,1,0:T(8,128)(2,1)S(1)} %dynamic-slice_bitcast_fusion.9), channel_id=1, source_target_pairs={{0,16},{4,20},{8,24},{12,28},{16,0},{20,4},{24,8},{28,12},{1,17},{... | collective-permute-start | bytes 2211848 | tf_op jit(solution)/shard_map/ppermute | solution.py:205
  809.9 53.3 %collective-permute-start.41 = (bf16[2,480,384]{2,1,0:T(8,128)(2,1)S(1)}, bf16[2,480,384]{2,1,0:T(8,128)(2,1)S(1)}, u32[]{:S(2)}, u32[]{:S(2)}) collective-permute-start(bf16[2,480,384]{2,1,0:T(8,128)(2,1)S(1)} %dynamic-slice_bitcast_fusion.10), channel_id=1, source_target_pairs={{0,8},{4,12},{8,0},{12,4},{16,24},{20,28},{24,16},{28,20},{1,9},{5... | collective-permute-start | bytes 2211848 | tf_op jit(solution)/shard_map/ppermute | solution.py:205
  811.5 52.9 %collective-permute-start.36 = (bf16[2,480,384]{2,1,0:T(8,128)(2,1)S(1)}, bf16[2,480,384]{2,1,0:T(8,128)(2,1)S(1)}, u32[]{:S(2)}, u32[]{:S(2)}) collective-permute-start(bf16[2,480,384]{2,1,0:T(8,128)(2,1)S(1)} %dynamic-slice_bitcast_fusion.11), channel_id=1, source_target_pairs={{0,16},{4,20},{8,24},{12,28},{16,0},{20,4},{24,8},{28,12},{1,17},{... | collective-permute-start | bytes 2211848 | tf_op jit(solution)/shard_map/ppermute | solution.py:205
  812.5 53.6 %collective-permute-start.33 = (bf16[2,480,384]{2,1,0:T(8,128)(2,1)S(1)}, bf16[2,480,384]{2,1,0:T(8,128)(2,1)S(1)}, u32[]{:S(2)}, u32[]{:S(2)}) collective-permute-start(bf16[2,480,384]{2,1,0:T(8,128)(2,1)S(1)} %dynamic-slice_bitcast_fusion.12), channel_id=1, source_target_pairs={{0,8},{4,12},{8,0},{12,4},{16,24},{20,28},{24,16},{28,20},{1,9},{5... | collective-permute-start | bytes 2211848 | tf_op jit(solution)/shard_map/ppermute | solution.py:205
  814.1 8.4 collective-permute-start.22
  822.4 8.3 collective-permute-start.6
  830.7 9.7 collective-permute-start.29
  840.5 6.8 collective-permute-start.26
  847.2 6.7 collective-permute-start.13
  854.0 6.7 collective-permute-start.10
  860.7 22.3 %collective-permute-start.23 = (bf16[96,2304]{1,0:T(8,128)(2,1)S(1)}, bf16[96,2304]{1,0:T(8,128)(2,1)S(1)}, u32[]{:S(2)}, u32[]{:S(2)}) collective-permute-start(bf16[96,2304]{1,0:T(8,128)(2,1)S(1)} %add_convert_fusion.4), channel_id=1, source_target_pairs={{0,3},{1,2},{2,1},{3,0},{4,7},{5,6},{6,5},{7,4},{8,11},{9,10},{10,... | collective-permute-start | bytes 1327112 | tf_op jit(solution)/shard_map/ppermute | solution.py:205
  860.9 29.5 %collective-permute-start.7 = (bf16[96,2304]{1,0:T(8,128)(2,1)S(1)}, bf16[96,2304]{1,0:T(8,128)(2,1)S(1)}, u32[]{:S(2)}, u32[]{:S(2)}) collective-permute-start(bf16[96,2304]{1,0:T(8,128)(2,1)S(1)} %add_convert_fusion.5), channel_id=1, source_target_pairs={{0,3},{1,2},{2,1},{3,0},{4,7},{5,6},{6,5},{7,4},{8,11},{9,10},{10,... | collective-permute-start | bytes 1327112 | tf_op jit(solution)/shard_map/ppermute | solution.py:205
  863.2 36.7 %collective-permute-start.30 = (bf16[96,3072]{1,0:T(8,128)(2,1)S(1)}, bf16[96,3072]{1,0:T(8,128)(2,1)S(1)}, u32[]{:S(2)}, u32[]{:S(2)}) collective-permute-start(bf16[96,3072]{1,0:T(8,128)(2,1)S(1)} %pad_maximum_fusion.7), channel_id=1, source_target_pairs={{0,1},{1,0},{2,3},{3,2},{4,5},{5,4},{6,7},{7,6},{8,9},{9,8},{10,11... | collective-permute-start | bytes 1769480 | tf_op jit(solution)/shard_map/ppermute | solution.py:205
  864.4 38.3 %collective-permute-start.14 = (bf16[96,3072]{1,0:T(8,128)(2,1)S(1)}, bf16[96,3072]{1,0:T(8,128)(2,1)S(1)}, u32[]{:S(2)}, u32[]{:S(2)}) collective-permute-start(bf16[96,3072]{1,0:T(8,128)(2,1)S(1)} %pad_maximum_fusion.6), channel_id=1, source_target_pairs={{0,1},{1,0},{2,3},{3,2},{4,5},{5,4},{6,7},{7,6},{8,9},{9,8},{10,11... | collective-permute-start | bytes 1769480 | tf_op jit(solution)/shard_map/ppermute | solution.py:205
  866.1 25.5 %collective-permute-start.45 = (bf16[480,384]{1,0:T(8,128)(2,1)S(1)}, bf16[480,384]{1,0:T(8,128)(2,1)S(1)}, u32[]{:S(2)}, u32[]{:S(2)}) collective-permute-start(bf16[480,384]{1,0:T(8,128)(2,1)S(1)} %dynamic-slice_bitcast_fusion.21), channel_id=1, source_target_pairs={{0,8},{4,12},{8,0},{12,4},{16,24},{20,28},{24,16},{28,20},{1,9},{5... | collective-permute-start | bytes 1105928 | tf_op jit(solution)/shard_map/ppermute | solution.py:205
  883.0 9.8 collective-permute-start.42
  890.4 8.5 collective-permute-start.37
  891.6 8.1 collective-permute-start.34
  892.9 34.3 %collective-permute-start.46 = (bf16[480,768]{1,0:T(8,128)(2,1)S(1)}, bf16[480,768]{1,0:T(8,128)(2,1)S(1)}, u32[]{:S(2)}, u32[]{:S(2)}) collective-permute-start(bf16[480,768]{1,0:T(8,128)(2,1)S(1)} %pad_maximum_fusion.5), channel_id=1, source_target_pairs={{0,1},{1,0},{2,3},{3,2},{4,5},{5,4},{6,7},{7,6},{8,9},{9,8},{10,11... | collective-permute-start | bytes 2211848 | tf_op jit(solution)/shard_map/ppermute | solution.py:205
  899.9 34.5 %collective-permute-start.38 = (bf16[480,768]{1,0:T(8,128)(2,1)S(1)}, bf16[480,768]{1,0:T(8,128)(2,1)S(1)}, u32[]{:S(2)}, u32[]{:S(2)}) collective-permute-start(bf16[480,768]{1,0:T(8,128)(2,1)S(1)} %pad_maximum_fusion.4), channel_id=1, source_target_pairs={{0,1},{1,0},{2,3},{3,2},{4,5},{5,4},{6,7},{7,6},{8,9},{9,8},{10,11... | collective-permute-start | bytes 2211848 | tf_op jit(solution)/shard_map/ppermute | solution.py:205
  900.1 16.3 %collective-permute-start.31 = (bf16[96,3072]{1,0:T(8,128)(2,1)S(1)}, bf16[96,3072]{1,0:T(8,128)(2,1)S(1)}, u32[]{:S(2)}, u32[]{:S(2)}) collective-permute-start(bf16[96,3072]{1,0:T(8,128)(2,1)S(1)} %add_convert_fusion.2), channel_id=1, source_target_pairs={{0,3},{1,2},{2,1},{3,0},{4,7},{5,6},{6,5},{7,4},{8,11},{9,10},{10,... | collective-permute-start | bytes 1769480 | tf_op jit(solution)/shard_map/ppermute | solution.py:205
  902.9 24.0 %collective-permute-start.15 = (bf16[96,3072]{1,0:T(8,128)(2,1)S(1)}, bf16[96,3072]{1,0:T(8,128)(2,1)S(1)}, u32[]{:S(2)}, u32[]{:S(2)}) collective-permute-start(bf16[96,3072]{1,0:T(8,128)(2,1)S(1)} %add_convert_fusion.3), channel_id=1, source_target_pairs={{0,3},{1,2},{2,1},{3,0},{4,7},{5,6},{6,5},{7,4},{8,11},{9,10},{10,... | collective-permute-start | bytes 1769480 | tf_op jit(solution)/shard_map/ppermute | solution.py:205
  916.6 18.3 %copy-start.19 = (f32[2,96,5376]{2,1,0:T(8,128)S(1)}, f32[2,96,5376]{2,1,0:T(8,128)}, u32[]{:S(2)}) copy-start(f32[2,96,5376]{2,1,0:T(8,128)} %param.19) | copy-start | bytes 12386308
  927.0 7.9 copy-start.18
  927.2 7.7 copy-start
  927.4 73.2 %collective-permute-start.47 = (bf16[480,768]{1,0:T(8,128)(2,1)S(1)}, bf16[480,768]{1,0:T(8,128)(2,1)S(1)}, u32[]{:S(2)}, u32[]{:S(2)}) collective-permute-start(bf16[480,768]{1,0:T(8,128)(2,1)S(1)} %add_convert_fusion), channel_id=1, source_target_pairs={{0,3},{1,2},{2,1},{3,0},{4,7},{5,6},{6,5},{7,4},{8,11},{9,10},{10,... | collective-permute-start | bytes 2211848 | tf_op jit(solution)/shard_map/ppermute | solution.py:205
  934.5 78.6 %collective-permute-start.39 = (bf16[480,768]{1,0:T(8,128)(2,1)S(1)}, bf16[480,768]{1,0:T(8,128)(2,1)S(1)}, u32[]{:S(2)}, u32[]{:S(2)}) collective-permute-start(bf16[480,768]{1,0:T(8,128)(2,1)S(1)} %add_convert_fusion.1), channel_id=1, source_target_pairs={{0,3},{1,2},{2,1},{3,0},{4,7},{5,6},{6,5},{7,4},{8,11},{9,10},{10,... | collective-permute-start | bytes 2211848 | tf_op jit(solution)/shard_map/ppermute | solution.py:205
  934.9 78.4 %copy-start.22 = (f32[2,480,768]{2,1,0:T(8,128)S(1)}, f32[2,480,768]{2,1,0:T(8,128)}, u32[]{:S(2)}) copy-start(f32[2,480,768]{2,1,0:T(8,128)} %param.20) | copy-start | bytes 8847364
  1000.6 12.7 %copy-start.21 = (f32[2,480,768]{2,1,0:T(8,128)S(1)}, f32[2,480,768]{2,1,0:T(8,128)}, u32[]{:S(2)}) copy-start(f32[2,480,768]{2,1,0:T(8,128)} %param.17) | copy-start | bytes 8847364
  1000.7 12.6 %copy-start.1 = (f32[2,480,768]{2,1,0:T(8,128)S(1)}, f32[2,480,768]{2,1,0:T(8,128)}, u32[]{:S(2)}) copy-start(f32[2,480,768]{2,1,0:T(8,128)} %param.14) | copy-start | bytes 8847364
  (30 other events, 70.9 us)
Sparse Core Ops, SparseCore 0:
  10.6 45.0 all-gather.10
  58.1 43.8 all-gather.14
  104.5 53.8 all-gather.8
  160.7 53.8 all-gather.12
  578.4 121.2 all-reduce.5

commit v2 on v1

--- a/solution.py
+++ b/solution.py
@@ -183,6 +183,223 @@
 
 
 LAYERS = 2
+MESH = pl.DeviceIdType.MESH
+CH = 96
+NC = 12
+
+
+def plane():
+    f = lax.axis_index("fsdp")
+    core, x, y = f % 2, (f // 2) % 2, f // 4
+    return f, core, x, y
+
+
+def chunk_rows(c, f):
+    layer, j = c // NC, c % NC
+    early = 1 - (j + 9) // 12
+    late = j // 8
+    mid = 1 - early - late
+    base = layer * NC * D
+    return pl.multiple_of(base + early * (j * D + CH * f) + late * ((j - 5) * D + CH * f)
+                          + mid * (7 * D + 5 * CH * f + CH * (j - 3)), 16)
+
+
+def fwd_kernel(img_ref, ws_ref, vs_ref, hs_ref, qkv_ref, a1_ref, o_ref, h1_ref, a2_ref, e_ref, g_ref, enc_ref, wo_ref, vo_ref,
+               w, hb, ob, ab, vg, vec, lsem, ssem, rsem, vssem, vrsem, osem, vosem):
+    l, s = pl.program_id(0), pl.program_id(1)
+    f, core, x, y = plane()
+    fc, fx, fy = f + 1 - 2 * core, f + 2 - 4 * x, f + 4 - 8 * y
+    fd = fx + fy - f
+
+    def wrow(c, who, lo=0, n=CH):
+        return w.at[pl.ds(pl.multiple_of(chunk_rows(c, who) + lo, 16), n)]
+
+    def send(c, kind, src, dst, to):
+        return pltpu.make_async_remote_copy(src_ref=src, dst_ref=dst, send_sem=ssem.at[c % 4, kind], recv_sem=rsem.at[c % 4, kind],
+                                            device_id={"fsdp": to}, device_id_type=MESH)
+
+    def kinds(c):
+        own, mine, half = ws_ref.at[c], wrow(c, f), CH // 2
+        return [lambda: send(c, 0, own, mine, fx), lambda: send(c, 1, own, mine, fy), lambda: send(c, 2, own, mine, fc),
+                lambda: send(c, 3, wrow(c, fx, 0, half), wrow(c, fx, 0, half), fy),
+                lambda: send(c, 4, wrow(c, fy, half, half), wrow(c, fy, half, half), fx),
+                lambda: send(c, 5, wrow(c, fx), wrow(c, fx), fc), lambda: send(c, 6, wrow(c, fy), wrow(c, fy), fc),
+                lambda: send(c, 7, wrow(c, fd), wrow(c, fd), fc), lambda: pltpu.make_async_copy(own, mine, lsem.at[c % 4])]
+
+    def start(c, which):
+        k = kinds(c)
+        for i in which:
+            k[i]().start()
+
+    def wait(c, which):
+        k = kinds(c)
+        for i in which:
+            k[i]().wait()
+
+    def tick(t):
+        @pl.when((t >= 3) & (t < 27))
+        def _():
+            wait(t - 3, (2, 5, 6, 7, 8))
+
+        @pl.when((t >= 2) & (t < 26))
+        def _():
+            wait(t - 2, (3, 4))
+            start(t - 2, (7,))
+
+        @pl.when((t >= 1) & (t < 25))
+        def _():
+            wait(t - 1, (0, 1))
+            start(t - 1, (3, 4, 5, 6))
+
+        @pl.when(t < 24)
+        def _():
+            start(t, (0, 1, 2, 8))
+
+    def out_copy(b, n):
+        return pltpu.make_async_copy(w.at[pl.ds(b, n)], wo_ref.at[pl.ds(b, n)], osem)
+
+    @pl.when((l == 0) & (s == 0))
+    def _():
+        bar = pltpu.get_barrier_semaphore()
+        for k in range(1, 8):
+            pl.semaphore_signal(bar, inc=1, device_id={"fsdp": (f + k) % 8}, device_id_type=MESH)
+        pl.semaphore_wait(bar, 7)
+
+        def vcopy(k):
+            return pltpu.make_async_remote_copy(src_ref=vs_ref, dst_ref=vg.at[f], send_sem=vssem.at[k - 1], recv_sem=vrsem.at[k - 1],
+                                                device_id={"fsdp": (f + k) % 8}, device_id_type=MESH)
+        for k in range(1, 8):
+            vcopy(k).start()
+        vg[f] = vs_ref[...]
+
+        @pl.loop(0, 6)
+        def _(t):
+            tick(t)
+        for k in range(1, 8):
+            vcopy(k).wait()
+        for layer in range(LAYERS):
+            for c in range(72):
+                vec[layer, c // 6:c // 6 + 1, 128 * (c % 6):128 * (c % 6) + 128] = vg[c // 9, layer, c % 9:c % 9 + 1, :]
+        hb[...] = jnp.zeros_like(hb)
+        cp = pltpu.make_async_copy(vec, vo_ref, vosem)
+        cp.start()
+        cp.wait()
+
+    early = (1 - l) * (s + 5) + l * (s + 17)
+    late = (1 - l) * (s + 1 + s // 11 + s // 13) + l * (s + 13)
+
+    @pl.when((s <= 5) & (l + s > 0))
+    def _():
+        tick(early)
+
+    @pl.when(s >= 10)
+    def _():
+        tick(late)
+
+    @pl.when(s < 5)
+    def _():
+        @pl.when(l == 0)
+        def _():
+            hb[s, 0:SEQ, :] = img_ref[s].astype(F32)
+        h = hb[s]
+        hs_ref[0, 0] = h
+        xc, rs = norm_stats(h)
+        a1_ref[0, 0] = (xc * rs * vec[l, 0:1] + vec[l, 1:2]).astype(BF)
+        a = a1_ref[0, 0]
+        wb = l * NC * D
+
+        def wq(part, c):
+            return w[pl.ds(pl.multiple_of(wb + part * D, 16), D), 256 * c:256 * c + 256]
+        for c in range(3):
+            cs = slice(256 * c, 256 * c + 256)
+            qkv_ref[0, 0, :, cs] = (dot(a, wq(0, c)) + vec[l, 2:3, cs]).astype(BF)
+            qkv_ref[0, 0, :, D + 256 * c:D + 256 * c + 256] = dot(a, wq(1, c)).astype(BF)
+            qkv_ref[0, 0, :, 2 * D + 256 * c:2 * D + 256 * c + 256] = (dot(a, wq(2, c)) + vec[l, 3:4, cs]).astype(BF)
+            for p in range(2):
+                b = 256 * c + 128 * p
+                o = attn_fwd(qkv_ref[0, 0, :, b:b + 128], qkv_ref[0, 0, :, D + b:D + b + 128], qkv_ref[0, 0, :, 2 * D + b:2 * D + b + 128])
+                o_ref[0, 0, :, b:b + 128] = o
+                ob[s, :, b:b + 128] = o
+
+    @pl.when((s >= 5) & (s < 10))
+    def _():
+        i = s - 5
+        wo = w[pl.ds(pl.multiple_of((l * NC + 7) * D, 16), D), :]
+        h1 = hb[i] + dot(ob[i], wo) + vec[l, 4:5]
+        h1_ref[0, 0] = h1
+        hb[i] = h1 + vec[l, 7:8]
+        xc, rs = norm_stats(h1)
+        a = (xc * rs * vec[l, 5:6] + vec[l, 6:7]).astype(BF)
+        a2_ref[0, 0] = a
+        ab[i] = a
+
+    @pl.when(s >= 10)
+    def _():
+        j = s - 10
+        up = pl.multiple_of((l * NC + 3 + j) * D, 16)
+        down = pl.multiple_of((l * NC + 8 + j) * D, 16)
+
+        @pl.loop(0, 5)
+        def _(i):
+            @pl.when((i == 3) & (l == 0) & ((s == 10) | (s == 12)))
+            def _():
+                tick(12 + 3 * ((s - 10) // 2))
+            for q in range(3):
+                cs = slice(256 * q, 256 * q + 256)
+                u = dot(ab[i], w[pl.ds(up, D), cs]) + vec[l, pl.ds(8 + j, 1), cs]
+                e, g = gelu_parts(u)
+                e_ref[0, i, :, cs] = e.astype(BF)
+                g_ref[0, i, :, cs] = g.astype(BF)
+                hb[i] += dot(e_ref[0, i, :, cs], w[pl.ds(pl.multiple_of(down + 256 * q, 16), 256), :])
+
+            @pl.when((l == 1) & (s == 13))
+            def _():
+                enc_ref[i] = hb[i, 0:SEQ, :].astype(BF)
+
+    for layer in range(LAYERS):
+        base = layer * NC * D
+
+        @pl.when((l == layer) & (s == 4))
+        def _():
+            out_copy(base, 3 * D).start()
+
+        @pl.when((l == layer) & (s == 9))
+        def _():
+            out_copy(base + 7 * D, 5 * D).start()
+
+        for j in range(4):
+            @pl.when((l == layer) & (s == 10 + j))
+            def _():
+                out_copy(base + (3 + j) * D, D).start()
+
+    @pl.when((l == 1) & (s == 13))
+    def _():
+        pltpu.make_async_copy(w, wo_ref, osem).wait()
+
+
+def fwd(images, shard, vshard):
+    n = images.shape[0]
+    S = jax.ShapeDtypeStruct
+    one = lambda cols: pl.BlockSpec((1, 1, RP, cols), lambda l, s: (l, jnp.minimum(s, 4), 0, 0))
+    two = lambda cols: pl.BlockSpec((1, 1, RP, cols), lambda l, s: (l, jnp.clip(s - 5, 0, 4), 0, 0))
+    wide = pl.BlockSpec((1, n, RP, D), lambda l, s: (l, 0, 0, jnp.clip(s - 10, 0, 3)))
+    anyw = pl.BlockSpec(memory_space=pl.ANY)
+    rows = LAYERS * NC * D
+    return pl.pallas_call(
+        fwd_kernel, grid=(LAYERS, 14),
+        in_specs=[pl.BlockSpec(images.shape, lambda l, s: (0, 0, 0)), anyw, pl.BlockSpec(vshard.shape, lambda l, s: (0, 0, 0))],
+        out_specs=[one(D), one(3 * D), one(D), one(D), two(D), two(D), wide, wide, pl.BlockSpec(images.shape, lambda l, s: (0, 0, 0)), anyw, anyw],
+        out_shape=[S((LAYERS, n, RP, D), F32), S((LAYERS, n, RP, 3 * D), BF), S((LAYERS, n, RP, D), BF), S((LAYERS, n, RP, D), BF),
+                   S((LAYERS, n, RP, D), F32), S((LAYERS, n, RP, D), BF), S((LAYERS, n, RP, 4 * D), BF), S((LAYERS, n, RP, 4 * D), BF),
+                   S(images.shape, BF), S((rows, D), BF), S((LAYERS, 16, D), F32)],
+        scratch_shapes=[pltpu.VMEM((rows, D), BF), pltpu.VMEM((n, RP, D), F32), pltpu.VMEM((n, RP, D), BF), pltpu.VMEM((n, RP, D), BF),
+                        pltpu.VMEM((8, LAYERS, 16, 128), F32), pltpu.VMEM((LAYERS, 16, D), F32),
+                        pltpu.SemaphoreType.DMA((4,)), pltpu.SemaphoreType.DMA((4, 8)), pltpu.SemaphoreType.DMA((4, 8)),
+                        pltpu.SemaphoreType.DMA((7,)), pltpu.SemaphoreType.DMA((7,)), pltpu.SemaphoreType.DMA, pltpu.SemaphoreType.DMA],
+        compiler_params=pltpu.CompilerParams(collective_id=0, has_side_effects=True, vmem_limit_bytes=62 * 2**20),
+    )(images, shard, vshard)
+
+
 STEP = 3
 beta_one = 0.9
 beta_two = 0.999
@@ -238,23 +455,45 @@
     return y
 
 
+def own_shard(weight_in, weight_out):
+    a = weight_in.astype(BF).reshape(LAYERS, CH, 7, D).transpose(0, 2, 1, 3)
+    b = weight_out.astype(BF).reshape(LAYERS, 5, CH, D)
+    return jnp.concatenate([a[:, :3], b, a[:, 3:]], axis=1).reshape(LAYERS * NC, CH, D)
+
+
+def fused_forward(images, weight_in, weight_out, vector_params):
+    vs = jnp.pad(vector_params.astype(BF).astype(F32).reshape(LAYERS, 9, 128), ((0, 0), (0, 7), (0, 0)))
+    hs, qkv, a1, o, h1, a2, e, g, encoded, w, vec = fwd(images, own_shard(weight_in, weight_out), vs)
+    saved = []
+    for l in range(LAYERS):
+        blk = lambda b, n: w[(l * NC + b) * D : (l * NC + b + n) * D]
+        wqkv = jnp.concatenate([blk(0, 1), blk(1, 1), blk(2, 1)], axis=1)
+        w1 = jnp.concatenate([blk(3 + j, 1) for j in range(4)], axis=1)
+        saved.append((hs[l], wqkv, w1, blk(7, 1), blk(8, 4), vec[l], qkv[l], o[l], a1[l], h1[l], a2[l], e[l], g[l]))
+    return encoded, saved
+
+
 def make_shards(nf, nr):
     def shards(images, cotangent, weight_in, weight_out, vector_params, first_in, first_out, first_vec, second_in, second_out, second_vec):
         pad = lambda a: jnp.pad(a, ((0, 0), (0, RP - SEQ), (0, 0)))
-        vec_all = lax.all_gather(vector_params.astype(BF), "fsdp", axis=1, tiled=True).astype(F32)
-        h = pad(images)
         ct = pad(cotangent)
-        saved = []
-        for l in range(LAYERS):
-            win = lax.all_gather(weight_in[l].astype(BF), "fsdp", axis=0, tiled=True)
-            wout = lax.all_gather(weight_out[l].astype(BF), "fsdp", axis=0, tiled=True)
-            vec = jnp.pad(vec_all[l].reshape(12, D), ((0, 4), (0, 0)))
-            wqkv, w1, wo, w2 = win[:, : 3 * D], win[:, 3 * D :], wout[:D], wout[D:]
-            qkv, o, a1 = ka(h, wqkv, vec)
-            h1, a2, e, g, h2 = kb(h, o, wo, w1, w2, vec)
-            saved.append((h, wqkv, w1, wo, w2, vec, qkv, o, a1, h1, a2, e, g))
-            h = h2
-        encoded = h[:, :SEQ].astype(BF)
+        if nf == 8:
+            encoded, saved = fused_forward(images, weight_in, weight_out, vector_params)
+        else:
+            vec_all = lax.all_gather(vector_params.astype(BF), "fsdp", axis=1, tiled=True).astype(F32)
+            h = pad(images)
+            ct = pad(cotangent)
+            saved = []
+            for l in range(LAYERS):
+                win = lax.all_gather(weight_in[l].astype(BF), "fsdp", axis=0, tiled=True)
+                wout = lax.all_gather(weight_out[l].astype(BF), "fsdp", axis=0, tiled=True)
+                vec = jnp.pad(vec_all[l].reshape(12, D), ((0, 4), (0, 0)))
+                wqkv, w1, wo, w2 = win[:, : 3 * D], win[:, 3 * D :], wout[:D], wout[D:]
+                qkv, o, a1 = ka(h, wqkv, vec)
+                h1, a2, e, g, h2 = kb(h, o, wo, w1, w2, vec)
+                saved.append((h, wqkv, w1, wo, w2, vec, qkv, o, a1, h1, a2, e, g))
+                h = h2
+            encoded = h[:, :SEQ].astype(BF)
         d = ct
         gin, gout, gvec = [None] * LAYERS, [None] * LAYERS, [None] * LAYERS
         for l in reversed(range(LAYERS)):

time: 1030 us -> 910 us (0.88)
  waiting for transfers between devices: 531 us -> 288 us
  Pallas kernels: 311 us -> 371 us
  local copies, waits for them, and re-layouts: 80.9 us -> 122 us
  other arithmetic: 41.2 us -> 67.1 us
    all_gather x4 -> x0, waiting for transfers between devices: 164 us -> none  [the longest x2 93.7 us: shards(): win = lax.all_gather(weight_in[l].astype(BF), 'fsdp', axis=0, tiled=True)]
    psum x1, waiting for transfers between devices: 116 us -> 38.2 us  [shards(): gv = lax.psum(jnp.stack(gvec), ('fsdp', 'rep'))]
    pallas_call x4 -> x1, Pallas kernels: 115 us -> 174 us  [fwd(): pl.pallas_call(fwd_kernel, grid=(LAYERS, 14), in_specs=[pl.BlockSpec(imag...]
    squeeze x0 -> x4, local copies, waits for them, and re-layouts: none -> 30 us  [the longest x1 11.5 us: fused_forward(): g[l]]
    concatenate x0 -> x3, other arithmetic: none -> 23.7 us  [the longest x1 14.8 us: fused_forward(): wqkv = jnp.concatenate([blk(0, 1), blk(1, 1), blk(2, 1)], axis=1)]
    slice x12 -> x9, local copies, waits for them, and re-layouts: 36 us -> 39.4 us  [the longest x2 19.9 us: fused_forward(): blk = lambda b, n: w[(l * NC + b) * D:(l * NC + b + n) * D]]
  transfers between devices with their start and end apart: 53 -> 49, of which waited for: 29 -> 25; matrix products, arithmetic and copies ran while one was open for 9% -> 11% of each run, Pallas kernels for 16% -> 18%
where the time goes in v2:
time: 910 us; the launch traced here: 900 us
  Pallas kernels  371 us (41%)
  waiting for transfers between devices  288 us (32%)
  local copies, waits for them, and re-layouts  122 us (13%)
  other arithmetic  67.1 us (7%)
  starting transfers between devices  36 us (4%)
  between operations  15.9 us (2%)
    ppermute x48, waiting for transfers between devices, swap(): return lax.ppermute(x, axis, [(i, i ^ mask) for i in range(size)])  250 us
    pallas_call x1, Pallas kernels, fwd(): pl.pallas_call(fwd_kernel, grid=(LAYERS, 14), in_specs=[pl.BlockSpec(imag...  174 us
    pallas_call x8, Pallas kernels, dw(): pl.pallas_call(dw_kernel, grid=(M // MB,), in_specs=[pl.BlockSpec((K, MB)...  76.9 us
    pallas_call x2, Pallas kernels, kd(): pl.pallas_call(kd_kernel, grid=(n,), in_specs=[img(3 * D), img(D)], out_s...  48.3 us
    pallas_call x2, Pallas kernels, kc(): pl.pallas_call(functools.partial(kc_kernel, FC), grid=(n,), in_specs=[img...  47.7 us
    psum x1, waiting for transfers between devices, shards(): gv = lax.psum(jnp.stack(gvec), ('fsdp', 'rep'))  38.2 us
    ppermute x48, starting transfers between devices, swap(): return lax.ppermute(x, axis, [(i, i ^ mask) for i in range(size)])  36 us
    pallas_call x2, Pallas kernels, kf(): pl.pallas_call(kf_kernel, grid=(n,), in_specs=[img(3 * D), img(D), img(D)...  23.7 us
  transfers between devices with their start and end apart: 49, of which 25 were waited for; matrix products, arithmetic and copies ran while one was open for 11% of the time, Pallas kernels for 18%

profile of v2, /device:TPU:8, one launch (start us, length us, event | category | flops | bytes accessed | tf_op | source)
XLA Modules:
  0.0 899.5 jit_solution(12332528582491517502)
XLA Ops:
  7.2 3.7 convert_element_type.536
  10.9 4.0 reshape.191
  21.4 2.0 pad_maximum_fusion.5
  23.4 174.1 %shard_map.218 = (f32[2,5,208,768]{3,2,1,0:T(8,128)}, bf16[2,5,208,2304]{3,2,1,0:T(8,128)(2,1)}, bf16[2,5,208,768]{3,2,1,0:T(8,128)(2,1)}, bf16[2,5,208,768]{3,2...) custom-call(bf16[5,197,768]{2,1,0:T(8,128)(2,1)} %img_ref.1, ...), custom_call_target="tpu_custom_call" | custom-call | tf_op jit(solution)/shard_map/pallas_call | solution.py:388
  197.5 11.9 %fusion.44 = (bf16[768,768]{1,0:T(8,128)(2,1)S(1)}, bf16[768,768]{1,0:T(8,128)(2,1)}, bf16[768,768]{1,0:T(8,128)(2,1)}, bf16[768,768]{1,0:T(8,128)(2,1)S(1)}, bf...) fusion(bf16[18432,768]{1,0:T(8,128)(2,1)} %get-tuple-element.49), kind=kLoop, calls=%fused_computation.177 | loop fusion | bytes 37748736 | tf_op jit(solution)/shard_map/slice | solution.py:469
  209.4 8.0 fusion.45
  217.4 11.5 %slice_bitcast_fusion = (bf16[5,208,3072]{2,1,0:T(8,128)(2,1)}, bf16[5,208,3072]{2,1,0:T(8,128)(2,1)}) fusion(bf16[2,5,208,3072]{3,2,1,0:T(8,128)(2,1)} %get-tuple-element.48), kind=kLoop, calls=%fused_computation | loop fusion | bytes 25559040 | tf_op jit(solution)/shard_map/squeeze | solution.py:472
  229.6 1.9 fusion.55
  232.9 9.7 %slice_bitcast_fusion.4 = (f32[5,208,768]{2,1,0:T(8,128)}, f32[5,208,768]{2,1,0:T(8,128)}, f32[5,208,768]{2,1,0:T(8,128)}, f32[5,208,768]{2,1,0:T(8,128)}) fusion(f32[2,5,208,768]{3,2,1,0:T(8,128)} %get-tuple-element.53, f32[2,5,208,768]{3,2,1,0:T(8,128)} %get-tuple-element.47), kind=kLoop, calls=%fused_computation.17 | loop fusion | bytes 25559040 | tf_op jit(solution)/shard_map/squeeze | solution.py:472
  242.5 6.9 pad_maximum_fusion.2
  249.5 23.9 %shard_map.219 = (bf16[5,208,768]{2,1,0:T(8,128)(2,1)}, bf16[5,208,3072]{2,1,0:T(8,128)(2,1)}, f32[5,208,768]{2,1,0:T(8,128)}, bf16[5,208,768]{2,1,0:T(8,128)(2,...) custom-call(bf16[5,208,768]{2,1,0:T(8,128)(2,1)} %pad.12.d_ref, f32[5,208,768]{2,1,0:T(8,128)} %get-tuple-element.142.h1_ref, ...), custom_call_target="tpu_custom_call" | custom-call | tf_op jit(solution)/shard_map/pallas_call | solution.py:141
  273.4 10.9 %shard_map.228 = bf16[768,3072]{1,0:T(8,128)(2,1)} custom-call(bf16[1040,768]{1,0:T(8,128)(2,1)} %bitcast.313, bf16[1040,3072]{1,0:T(8,128)(2,1)} %bitcast.315), custom_call_target="tpu_custom_call" | custom-call | tf_op jit(solution)/shard_map/pallas_call | solution.py:181
  284.4 4.2 fusion.50
  288.6 2.3 dynamic-slice_bitcast_fusion.3
  293.8 8.1 slice_bitcast_fusion.2
  301.9 24.2 %shard_map.220 = (bf16[5,208,2304]{2,1,0:T(8,128)(2,1)}, f32[16,768]{1,0:T(8,128)}) custom-call(bf16[5,208,2304]{2,1,0:T(8,128)(2,1)} %get-tuple-element.110.qkv_ref, bf16[5,208,768]{2,1,0:T(8,128)(2,1)} %get-tuple-element.51.do_ref), custom_call_target="tpu_custom_call" | custom-call | tf_op jit(solution)/shard_map/pallas_call | solution.py:158
  326.1 5.7 fusion.53
  331.8 8.8 shard_map.227
  340.6 2.3 fusion.52
  347.2 14.8 %pad_maximum_fusion.6 = (bf16[768,2304]{1,0:T(8,128)(2,1)}, bf16[768,2304]{1,0:T(8,128)(2,1)}) fusion(bf16[768,768]{1,0:T(8,128)(2,1)S(1)} %copy-done.20, bf16[768,768]{1,0:T(8,128)(2,1)S(1)} %copy-done.21, bf16[768,768]{1,0:T(8,128)(2,1)S(1)} %copy-done.22, bf16[768,768]{1,0:T(8,128)(2,1)S(1)} %copy-done.18, bf16[768,768]{1,0:T(8,128)(2,1)S(1)} %copy-done.19, ...), kind=kLoop, calls=%fused_computation.15 | loop fusion | flops 21233664 | bytes 14155776 | tf_op jit(solution)/shard_map/concatenate | solution.py:470
  362.0 11.9 %shard_map.221 = (f32[5,208,768]{2,1,0:T(8,128)}, f32[16,768]{1,0:T(8,128)}) custom-call(bf16[5,208,2304]{2,1,0:T(8,128)(2,1)} %get-tuple-element.52.dz_ref, f32[5,208,768]{2,1,0:T(8,128)} %get-tuple-element.113.h_ref, f32[5,208,768]{2,1,0:T(8,128)} %get-tuple-element.54.dh1_ref, bf16[768,2304]{1,0:T(8,128)(2,1)} %get-tuple-element.148.w_ref, ...), custom_call_target="tpu_custom_call" | custom-call | tf_op jit(solution)/shard_map/pallas_call | solution.py:172
  373.9 23.8 %shard_map.222 = (bf16[5,208,768]{2,1,0:T(8,128)(2,1)}, bf16[5,208,3072]{2,1,0:T(8,128)(2,1)}, f32[5,208,768]{2,1,0:T(8,128)}, bf16[5,208,768]{2,1,0:T(8,128)(2,...) custom-call(f32[5,208,768]{2,1,0:T(8,128)} %get-tuple-element.55.d_ref, f32[5,208,768]{2,1,0:T(8,128)} %get-tuple-element.143.h1_ref, ...), custom_call_target="tpu_custom_call" | custom-call | tf_op jit(solution)/shard_map/pallas_call | solution.py:141
  397.7 24.1 %shard_map.223 = (bf16[5,208,2304]{2,1,0:T(8,128)(2,1)}, f32[16,768]{1,0:T(8,128)}) custom-call(bf16[5,208,2304]{2,1,0:T(8,128)(2,1)} %get-tuple-element.111.qkv_ref, bf16[5,208,768]{2,1,0:T(8,128)(2,1)} %get-tuple-element.56.do_ref), custom_call_target="tpu_custom_call" | custom-call | tf_op jit(solution)/shard_map/pallas_call | solution.py:158
  421.8 8.8 shard_map.225
  430.6 3.5 fusion.51
  436.7 11.8 %shard_map.224 = (f32[5,197,768]{2,1,0:T(8,128)}, f32[16,768]{1,0:T(8,128)}) custom-call(bf16[5,208,2304]{2,1,0:T(8,128)(2,1)} %get-tuple-element.57.dz_ref, f32[5,208,768]{2,1,0:T(8,128)} %get-tuple-element.112.h_ref, f32[5,208,768]{2,1,0:T(8,128)} %get-tuple-element.58.dh1_ref, bf16[768,2304]{1,0:T(8,128)(2,1)} %get-tuple-element.149.w_ref, ...), custom_call_target="tpu_custom_call" | custom-call | tf_op jit(solution)/shard_map/pallas_call | solution.py:172
  450.2 11.0 %shard_map.226 = bf16[768,3072]{1,0:T(8,128)(2,1)} custom-call(bf16[1040,768]{1,0:T(8,128)(2,1)} %bitcast.310, bf16[1040,3072]{1,0:T(8,128)(2,1)} %bitcast.314), custom_call_target="tpu_custom_call" | custom-call | tf_op jit(solution)/shard_map/pallas_call | solution.py:181
  461.1 2.8 fusion.49
  466.9 10.8 %fusion.46 = (bf16[1,5,208,3072]{3,2,1,0:T(8,128)(2,1)}, bf16[1,5,208,3072]{3,2,1,0:T(8,128)(2,1)}) fusion(bf16[2,5,208,3072]{3,2,1,0:T(8,128)(2,1)} %get-tuple-element.66), kind=kLoop, calls=%fused_computation.179 | loop fusion | bytes 25559040 | tf_op jit(solution)/shard_map/slice | solution.py:472
  477.7 13.6 %shard_map.232 = bf16[3072,768]{1,0:T(8,128)(2,1)} custom-call(bf16[1040,3072]{1,0:T(8,128)(2,1)} %bitcast.275, bf16[1040,768]{1,0:T(8,128)(2,1)} %bitcast.317), custom_call_target="tpu_custom_call" | custom-call | tf_op jit(solution)/shard_map/pallas_call | solution.py:181
  491.3 5.0 shard_map.231
  496.3 3.1 pad_maximum_fusion.1
  501.4 2.0 constant_dynamic-slice_fusion.2
  503.4 13.6 %shard_map.230 = bf16[3072,768]{1,0:T(8,128)(2,1)} custom-call(bf16[1040,3072]{1,0:T(8,128)(2,1)} %bitcast.274, bf16[1040,768]{1,0:T(8,128)(2,1)} %bitcast.318), custom_call_target="tpu_custom_call" | custom-call | tf_op jit(solution)/shard_map/pallas_call | solution.py:181
  517.1 5.2 shard_map.229
  522.2 3.1 pad_maximum_fusion
  531.1 2.7 copy.63
  533.7 38.2 %all-reduce.4.cloned.1.call-done = f32[2,9216]{1,0:T(2,128)} async-done(((f32[2,9216]{1,0:T(2,128)}), f32[2,9216]{1,0:T(2,128)}) %all-reduce.4.cloned.1.call-update) | async-done | bytes 73744 | tf_op jit(solution)/shard_map/psum | solution.py:510
  588.1 10.4 %collective-permute-done.20 = bf16[2,96,1152]{2,1,0:T(8,128)(2,1)S(1)} collective-permute-done((bf16[2,96,1152]{2,1,0:T(8,128)(2,1)S(1)}, bf16[2,96,1152]{2,1,0:T(8,128)(2,1)S(1)}, u32[]{:S(2)}, u32[]{:S(2)}) %collective-permute-start.20) | collective-permute-done | bytes 442400 | tf_op jit(solution)/shard_map/ppermute | solution.py:422
  600.1 9.9 %collective-permute-done.4 = bf16[2,96,1152]{2,1,0:T(8,128)(2,1)S(1)} collective-permute-done((bf16[2,96,1152]{2,1,0:T(8,128)(2,1)S(1)}, bf16[2,96,1152]{2,1,0:T(8,128)(2,1)S(1)}, u32[]{:S(2)}, u32[]{:S(2)}) %collective-permute-start.4) | collective-permute-done | bytes 442400 | tf_op jit(solution)/shard_map/ppermute | solution.py:422
  611.7 9.0 collective-permute-done.17
  622.2 8.1 collective-permute-done.1
  638.3 22.7 %collective-permute-done.21 = bf16[96,1152]{1,0:T(8,128)(2,1)S(1)} collective-permute-done((bf16[96,1152]{1,0:T(8,128)(2,1)S(1)}, bf16[96,1152]{1,0:T(8,128)(2,1)S(1)}, u32[]{:S(2)}, u32[]{:S(2)}) %collective-permute-start.21) | collective-permute-done | bytes 221216 | tf_op jit(solution)/shard_map/ppermute | solution.py:422
  661.8 5.2 collective-permute-done.18
  667.7 5.1 collective-permute-done.5
  673.6 7.6 collective-permute-done.2
  686.5 8.1 collective-permute-done.22
  694.9 8.0 collective-permute-done.6
  703.9 8.8 collective-permute-done.29
  713.9 5.5 collective-permute-done.26
  720.9 5.2 collective-permute-done.13
  727.6 5.3 collective-permute-done.10
  733.1 2.1 collective-permute-start.7
  740.1 15.1 %collective-permute-done.23 = bf16[96,2304]{1,0:T(8,128)(2,1)S(1)} collective-permute-done((bf16[96,2304]{1,0:T(8,128)(2,1)S(1)}, bf16[96,2304]{1,0:T(8,128)(2,1)S(1)}, u32[]{:S(2)}, u32[]{:S(2)}) %collective-permute-start.23) | collective-permute-done | bytes 442400 | tf_op jit(solution)/shard_map/ppermute | solution.py:422
  756.6 5.9 collective-permute-done.7
  765.2 5.8 collective-permute-done.37
  773.1 1.8 collective-permute-done.14
  775.2 13.5 %collective-permute-done.31 = bf16[96,3072]{1,0:T(8,128)(2,1)S(1)} collective-permute-done((bf16[96,3072]{1,0:T(8,128)(2,1)S(1)}, bf16[96,3072]{1,0:T(8,128)(2,1)S(1)}, u32[]{:S(2)}, u32[]{:S(2)}) %collective-permute-start.31) | collective-permute-done | bytes 589856 | tf_op jit(solution)/shard_map/ppermute | solution.py:422
  789.0 10.2 %collective-permute-done.15 = bf16[96,3072]{1,0:T(8,128)(2,1)S(1)} collective-permute-done((bf16[96,3072]{1,0:T(8,128)(2,1)S(1)}, bf16[96,3072]{1,0:T(8,128)(2,1)S(1)}, u32[]{:S(2)}, u32[]{:S(2)}) %collective-permute-start.15) | collective-permute-done | bytes 589856 | tf_op jit(solution)/shard_map/ppermute | solution.py:422
  799.7 6.8 collective-permute-done.38
  807.1 7.4 multiply_subtract_fusion
  814.6 58.2 %collective-permute-done.47 = bf16[480,768]{1,0:T(8,128)(2,1)S(1)} collective-permute-done((bf16[480,768]{1,0:T(8,128)(2,1)S(1)}, bf16[480,768]{1,0:T(8,128)(2,1)S(1)}, u32[]{:S(2)}, u32[]{:S(2)}) %collective-permute-start.47) | collective-permute-done | bytes 737312 | tf_op jit(solution)/shard_map/ppermute | solution.py:422
  873.0 12.4 %collective-permute-done.39 = bf16[480,768]{1,0:T(8,128)(2,1)S(1)} collective-permute-done((bf16[480,768]{1,0:T(8,128)(2,1)S(1)}, bf16[480,768]{1,0:T(8,128)(2,1)S(1)}, u32[]{:S(2)}, u32[]{:S(2)}) %collective-permute-start.39) | collective-permute-done | bytes 737312 | tf_op jit(solution)/shard_map/ppermute | solution.py:422
  885.6 5.5 multiply_subtract_fusion.1
  (277 shorter events, 86.0 us)
Async XLA Ops:
  7.2 564.7 %all-reduce.4.cloned.1.call-start = ((), (), s32[]{:S(2)}) async-start(), calls=%async_computation | async-start | bytes 147456 | tf_op jit(solution)/shard_map/psum | solution.py:510
  217.4 11.5 %copy-start.37 = (f32[2,16,768]{2,1,0:T(8,128)S(1)}, f32[2,16,768]{2,1,0:T(8,128)}, u32[]{:S(2)}) copy-start(f32[2,16,768]{2,1,0:T(8,128)} %get-tuple-element.50) | copy-start | bytes 294916
  217.4 12.2 %copy-start.27 = (bf16[2,5,208,768]{3,2,1,0:T(8,128)(2,1)S(1)}, bf16[2,5,208,768]{3,2,1,0:T(8,128)(2,1)}, u32[]{:S(2)}) copy-start(bf16[2,5,208,768]{3,2,1,0:T(8,128)(2,1)} %get-tuple-element.61) | copy-start | bytes 9584644
  290.9 289.7 %collective-permute-start.27 = (bf16[2,2,96,1536]{3,2,1,0:T(8,128)(2,1)}, bf16[2,2,96,1536]{3,2,1,0:T(8,128)(2,1)}, u32[]{:S(2)}, u32[]{:S(2)}) collective-permute-start(bf16[2,2,96,1536]{3,2,1,0:T(8,128)(2,1)} %dynamic-slice_bitcast_fusion.3), channel_id=1, source_target_pairs={{0,4},{4,0},{8,12},{12,8},{16,20},{20,16},{24,28},{28,24},{1,5},{5... | collective-permute-start | bytes 3538952 | tf_op jit(solution)/shard_map/ppermute | solution.py:422
  293.3 289.8 %collective-permute-start.24 = (bf16[2,2,96,1536]{3,2,0,1:T(8,128)(2,1)}, bf16[2,2,96,1536]{3,2,0,1:T(8,128)(2,1)}, u32[]{:S(2)}, u32[]{:S(2)}) collective-permute-start(bf16[2,2,96,1536]{3,2,0,1:T(8,128)(2,1)} %bitcast.272), channel_id=1, source_target_pairs={{0,4},{4,0},{8,12},{12,8},{16,20},{20,16},{24,28},{28,24},{1,5},{5... | collective-permute-start | bytes 3538952 | tf_op jit(solution)/shard_map/ppermute | solution.py:422
  343.9 229.5 %collective-permute-start.19 = (bf16[2,2,96,1152]{3,2,1,0:T(8,128)(2,1)}, bf16[2,2,96,1152]{3,2,1,0:T(8,128)(2,1)}, u32[]{:S(2)}, u32[]{:S(2)}) collective-permute-start(bf16[2,2,96,1152]{3,2,1,0:T(8,128)(2,1)} %dynamic-slice_bitcast_fusion.6), channel_id=1, source_target_pairs={{0,4},{4,0},{8,12},{12,8},{16,20},{20,16},{24,28},{28,24},{1,5},{5... | collective-permute-start | bytes 2654216 | tf_op jit(solution)/shard_map/ppermute | solution.py:422
  346.0 231.8 %collective-permute-start.16 = (bf16[2,2,96,1152]{3,2,0,1:T(8,128)(2,1)}, bf16[2,2,96,1152]{3,2,0,1:T(8,128)(2,1)}, u32[]{:S(2)}, u32[]{:S(2)}) collective-permute-start(bf16[2,2,96,1152]{3,2,0,1:T(8,128)(2,1)} %bitcast.273), channel_id=1, source_target_pairs={{0,4},{4,0},{8,12},{12,8},{16,20},{20,16},{24,28},{28,24},{1,5},{5... | collective-permute-start | bytes 2654216 | tf_op jit(solution)/shard_map/ppermute | solution.py:422
  430.6 6.0 copy-start.39
  430.6 6.0 copy-start.41
  436.4 138.7 %collective-permute-start.3 = (bf16[2,2,96,1152]{3,2,1,0:T(8,128)(2,1)}, bf16[2,2,96,1152]{3,2,1,0:T(8,128)(2,1)}, u32[]{:S(2)}, u32[]{:S(2)}) collective-permute-start(bf16[2,2,96,1152]{3,2,1,0:T(8,128)(2,1)} %dynamic-slice_bitcast_fusion.7), channel_id=1, source_target_pairs={{0,4},{4,0},{8,12},{12,8},{16,20},{20,16},{24,28},{28,24},{1,5},{5... | collective-permute-start | bytes 2654216 | tf_op jit(solution)/shard_map/ppermute | solution.py:422
  436.7 11.9 %copy-start.40 = (f32[16,768]{1,0:T(8,128)S(1)}, f32[16,768]{1,0:T(8,128)}, u32[]{:S(2)}) copy-start(f32[16,768]{1,0:T(8,128)} %get-tuple-element.70) | copy-start | bytes 147460
  436.7 11.8 %copy-start.42 = (f32[16,768]{1,0:T(8,128)S(1)}, f32[16,768]{1,0:T(8,128)}, u32[]{:S(2)}) copy-start(f32[16,768]{1,0:T(8,128)} %get-tuple-element.71) | copy-start | bytes 147460
  531.1 40.9 %copy-start.44 = (f32[2,1152]{1,0:T(2,128)S(1)}, f32[2,1152]{1,0:T(2,128)}, u32[]{:S(2)}) copy-start(f32[2,1152]{1,0:T(2,128)} %param.18) | copy-start | bytes 27652
  531.1 40.9 %copy-start.45 = (f32[2,1152]{1,0:T(2,128)S(1)}, f32[2,1152]{1,0:T(2,128)}, u32[]{:S(2)}) copy-start(f32[2,1152]{1,0:T(2,128)} %param.21) | copy-start | bytes 27652
  573.4 4.0 collective-permute-start
  575.1 10.1 %collective-permute-start.11 = (bf16[2,2,96,1536]{3,2,1,0:T(8,128)(2,1)}, bf16[2,2,96,1536]{3,2,1,0:T(8,128)(2,1)S(1)}, u32[]{:S(2)}, u32[]{:S(2)}) collective-permute-start(bf16[2,2,96,1536]{3,2,1,0:T(8,128)(2,1)} %dynamic-slice_bitcast_fusion.4), channel_id=1, source_target_pairs={{0,4},{4,0},{8,12},{12,8},{16,20},{20,16},{24,28},{28,24},{1,5},{5... | collective-permute-start | bytes 3538952 | tf_op jit(solution)/shard_map/ppermute | solution.py:422
  577.4 8.8 collective-permute-start.8
  578.7 53.3 %collective-permute-start.43 = (bf16[2,2,480,384]{3,2,1,0:T(8,128)(2,1)S(1)}, bf16[2,2,480,384]{3,2,1,0:T(8,128)(2,1)S(1)}, u32[]{:S(2)}, u32[]{:S(2)}) collective-permute-start(bf16[2,2,480,384]{3,2,1,0:T(8,128)(2,1)S(1)} %copy-done.34), channel_id=1, source_target_pairs={{0,4},{4,0},{8,12},{12,8},{16,20},{20,16},{24,28},{28,24},{1,5},{5... | collective-permute-start | bytes 4423688 | tf_op jit(solution)/shard_map/ppermute | solution.py:422
  580.6 52.5 %collective-permute-start.40 = (bf16[2,2,480,384]{3,2,0,1:T(8,128)(2,1)S(1)}, bf16[2,2,480,384]{3,2,0,1:T(8,128)(2,1)S(1)}, u32[]{:S(2)}, u32[]{:S(2)}) collective-permute-start(bf16[2,2,480,384]{3,2,0,1:T(8,128)(2,1)S(1)} %bitcast.321), channel_id=1, source_target_pairs={{0,4},{4,0},{8,12},{12,8},{16,20},{20,16},{24,28},{28,24},{1,5},{5... | collective-permute-start | bytes 4423688 | tf_op jit(solution)/shard_map/ppermute | solution.py:422
  583.1 52.2 %collective-permute-start.35 = (bf16[2,2,480,384]{3,2,1,0:T(8,128)(2,1)S(1)}, bf16[2,2,480,384]{3,2,1,0:T(8,128)(2,1)S(1)}, u32[]{:S(2)}, u32[]{:S(2)}) collective-permute-start(bf16[2,2,480,384]{3,2,1,0:T(8,128)(2,1)S(1)} %copy-done.33), channel_id=1, source_target_pairs={{0,4},{4,0},{8,12},{12,8},{16,20},{20,16},{24,28},{28,24},{1,5},{5... | collective-permute-start | bytes 4423688 | tf_op jit(solution)/shard_map/ppermute | solution.py:422
  585.2 51.7 %collective-permute-start.32 = (bf16[2,2,480,384]{3,2,1,0:T(8,128)(2,1)S(1)}, bf16[2,2,480,384]{3,2,1,0:T(8,128)(2,1)S(1)}, u32[]{:S(2)}, u32[]{:S(2)}) collective-permute-start(bf16[2,2,480,384]{3,2,1,0:T(8,128)(2,1)S(1)} %copy-done.32), channel_id=1, source_target_pairs={{0,4},{4,0},{8,12},{12,8},{16,20},{20,16},{24,28},{28,24},{1,5},{5... | collective-permute-start | bytes 4423688 | tf_op jit(solution)/shard_map/ppermute | solution.py:422
  586.2 12.4 %collective-permute-start.20 = (bf16[2,96,1152]{2,1,0:T(8,128)(2,1)S(1)}, bf16[2,96,1152]{2,1,0:T(8,128)(2,1)S(1)}, u32[]{:S(2)}, u32[]{:S(2)}) collective-permute-start(bf16[2,96,1152]{2,1,0:T(8,128)(2,1)S(1)} %dynamic-slice_bitcast_fusion.17), channel_id=1, source_target_pairs={{0,16},{4,20},{8,24},{12,28},{16,0},{20,4},{24,8},{28,12},{1,17},{... | collective-permute-start | bytes 1327112 | tf_op jit(solution)/shard_map/ppermute | solution.py:422
  598.6 11.5 %collective-permute-start.4 = (bf16[2,96,1152]{2,1,0:T(8,128)(2,1)S(1)}, bf16[2,96,1152]{2,1,0:T(8,128)(2,1)S(1)}, u32[]{:S(2)}, u32[]{:S(2)}) collective-permute-start(bf16[2,96,1152]{2,1,0:T(8,128)(2,1)S(1)} %dynamic-slice_bitcast_fusion.19), channel_id=1, source_target_pairs={{0,16},{4,20},{8,24},{12,28},{16,0},{20,4},{24,8},{28,12},{1,17},{... | collective-permute-start | bytes 1327112 | tf_op jit(solution)/shard_map/ppermute | solution.py:422
  610.1 10.6 %collective-permute-start.17 = (bf16[2,96,1152]{2,1,0:T(8,128)(2,1)S(1)}, bf16[2,96,1152]{2,1,0:T(8,128)(2,1)S(1)}, u32[]{:S(2)}, u32[]{:S(2)}) collective-permute-start(bf16[2,96,1152]{2,1,0:T(8,128)(2,1)S(1)} %dynamic-slice_bitcast_fusion.18), channel_id=1, source_target_pairs={{0,8},{4,12},{8,0},{12,4},{16,24},{20,28},{24,16},{28,20},{1,9},{5... | collective-permute-start | bytes 1327112 | tf_op jit(solution)/shard_map/ppermute | solution.py:422
  611.6 21.0 %copy-start.6 = (bf16[8,480,384]{2,1,0:T(8,128)(2,1)S(1)}, bf16[8,480,384]{2,1,0:T(8,128)(2,1)}, u32[]{:S(2)}) copy-start(bf16[8,480,384]{2,1,0:T(8,128)(2,1)} %copy-done.5) | copy-start | bytes 8847364
  620.6 9.6 %collective-permute-start.1 = (bf16[2,96,1152]{2,1,0:T(8,128)(2,1)S(1)}, bf16[2,96,1152]{2,1,0:T(8,128)(2,1)S(1)}, u32[]{:S(2)}, u32[]{:S(2)}) collective-permute-start(bf16[2,96,1152]{2,1,0:T(8,128)(2,1)S(1)} %dynamic-slice_bitcast_fusion.20), channel_id=1, source_target_pairs={{0,8},{4,12},{8,0},{12,4},{16,24},{20,28},{24,16},{28,20},{1,9},{5... | collective-permute-start | bytes 1327112 | tf_op jit(solution)/shard_map/ppermute | solution.py:422
  630.3 51.8 %collective-permute-start.28 = (bf16[2,96,1536]{2,1,0:T(8,128)(2,1)S(1)}, bf16[2,96,1536]{2,1,0:T(8,128)(2,1)S(1)}, u32[]{:S(2)}, u32[]{:S(2)}) collective-permute-start(bf16[2,96,1536]{2,1,0:T(8,128)(2,1)S(1)} %dynamic-slice_bitcast_fusion.13), channel_id=1, source_target_pairs={{0,16},{4,20},{8,24},{12,28},{16,0},{20,4},{24,8},{28,12},{1,17},{... | collective-permute-start | bytes 1769480 | tf_op jit(solution)/shard_map/ppermute | solution.py:422
  632.0 51.7 %collective-permute-start.25 = (bf16[2,96,1536]{2,1,0:T(8,128)(2,1)S(1)}, bf16[2,96,1536]{2,1,0:T(8,128)(2,1)S(1)}, u32[]{:S(2)}, u32[]{:S(2)}) collective-permute-start(bf16[2,96,1536]{2,1,0:T(8,128)(2,1)S(1)} %dynamic-slice_bitcast_fusion.14), channel_id=1, source_target_pairs={{0,8},{4,12},{8,0},{12,4},{16,24},{20,28},{24,16},{28,20},{1,9},{5... | collective-permute-start | bytes 1769480 | tf_op jit(solution)/shard_map/ppermute | solution.py:422
  633.1 51.6 %collective-permute-start.12 = (bf16[2,96,1536]{2,1,0:T(8,128)(2,1)S(1)}, bf16[2,96,1536]{2,1,0:T(8,128)(2,1)S(1)}, u32[]{:S(2)}, u32[]{:S(2)}) collective-permute-start(bf16[2,96,1536]{2,1,0:T(8,128)(2,1)S(1)} %dynamic-slice_bitcast_fusion.15), channel_id=1, source_target_pairs={{0,16},{4,20},{8,24},{12,28},{16,0},{20,4},{24,8},{28,12},{1,17},{... | collective-permute-start | bytes 1769480 | tf_op jit(solution)/shard_map/ppermute | solution.py:422
  635.2 51.0 %collective-permute-start.9 = (bf16[2,96,1536]{2,1,0:T(8,128)(2,1)S(1)}, bf16[2,96,1536]{2,1,0:T(8,128)(2,1)S(1)}, u32[]{:S(2)}, u32[]{:S(2)}) collective-permute-start(bf16[2,96,1536]{2,1,0:T(8,128)(2,1)S(1)} %dynamic-slice_bitcast_fusion.16), channel_id=1, source_target_pairs={{0,8},{4,12},{8,0},{12,4},{16,24},{20,28},{24,16},{28,20},{1,9},{5... | collective-permute-start | bytes 1769480 | tf_op jit(solution)/shard_map/ppermute | solution.py:422
  637.0 24.1 %collective-permute-start.21 = (bf16[96,1152]{1,0:T(8,128)(2,1)S(1)}, bf16[96,1152]{1,0:T(8,128)(2,1)S(1)}, u32[]{:S(2)}, u32[]{:S(2)}) collective-permute-start(bf16[96,1152]{1,0:T(8,128)(2,1)S(1)} %dynamic-slice_bitcast_fusion.29), channel_id=1, source_target_pairs={{0,8},{4,12},{8,0},{12,4},{16,24},{20,28},{24,16},{28,20},{1,9},{5... | collective-permute-start | bytes 663560 | tf_op jit(solution)/shard_map/ppermute | solution.py:422
  661.0 5.9 collective-permute-start.18
  667.0 5.9 collective-permute-start.5
  672.9 8.4 collective-permute-start.2
  681.3 51.8 %collective-permute-start.44 = (bf16[2,480,384]{2,1,0:T(8,128)(2,1)S(1)}, bf16[2,480,384]{2,1,0:T(8,128)(2,1)S(1)}, u32[]{:S(2)}, u32[]{:S(2)}) collective-permute-start(bf16[2,480,384]{2,1,0:T(8,128)(2,1)S(1)} %dynamic-slice_bitcast_fusion.9), channel_id=1, source_target_pairs={{0,16},{4,20},{8,24},{12,28},{16,0},{20,4},{24,8},{28,12},{1,17},{... | collective-permute-start | bytes 2211848 | tf_op jit(solution)/shard_map/ppermute | solution.py:422
  682.1 53.3 %collective-permute-start.41 = (bf16[2,480,384]{2,1,0:T(8,128)(2,1)S(1)}, bf16[2,480,384]{2,1,0:T(8,128)(2,1)S(1)}, u32[]{:S(2)}, u32[]{:S(2)}) collective-permute-start(bf16[2,480,384]{2,1,0:T(8,128)(2,1)S(1)} %dynamic-slice_bitcast_fusion.10), channel_id=1, source_target_pairs={{0,8},{4,12},{8,0},{12,4},{16,24},{20,28},{24,16},{28,20},{1,9},{5... | collective-permute-start | bytes 2211848 | tf_op jit(solution)/shard_map/ppermute | solution.py:422
  683.7 52.9 %collective-permute-start.36 = (bf16[2,480,384]{2,1,0:T(8,128)(2,1)S(1)}, bf16[2,480,384]{2,1,0:T(8,128)(2,1)S(1)}, u32[]{:S(2)}, u32[]{:S(2)}) collective-permute-start(bf16[2,480,384]{2,1,0:T(8,128)(2,1)S(1)} %dynamic-slice_bitcast_fusion.11), channel_id=1, source_target_pairs={{0,16},{4,20},{8,24},{12,28},{16,0},{20,4},{24,8},{28,12},{1,17},{... | collective-permute-start | bytes 2211848 | tf_op jit(solution)/shard_map/ppermute | solution.py:422
  684.7 53.4 %collective-permute-start.33 = (bf16[2,480,384]{2,1,0:T(8,128)(2,1)S(1)}, bf16[2,480,384]{2,1,0:T(8,128)(2,1)S(1)}, u32[]{:S(2)}, u32[]{:S(2)}) collective-permute-start(bf16[2,480,384]{2,1,0:T(8,128)(2,1)S(1)} %dynamic-slice_bitcast_fusion.12), channel_id=1, source_target_pairs={{0,8},{4,12},{8,0},{12,4},{16,24},{20,28},{24,16},{28,20},{1,9},{5... | collective-permute-start | bytes 2211848 | tf_op jit(solution)/shard_map/ppermute | solution.py:422
  686.2 8.4 collective-permute-start.22
  694.6 8.3 collective-permute-start.6
  702.9 9.7 %collective-permute-start.29 = (bf16[96,1536]{1,0:T(8,128)(2,1)S(1)}, bf16[96,1536]{1,0:T(8,128)(2,1)S(1)}, u32[]{:S(2)}, u32[]{:S(2)}) collective-permute-start(bf16[96,1536]{1,0:T(8,128)(2,1)S(1)} %dynamic-slice_bitcast_fusion.25), channel_id=1, source_target_pairs={{0,8},{4,12},{8,0},{12,4},{16,24},{20,28},{24,16},{28,20},{1,9},{5... | collective-permute-start | bytes 884744 | tf_op jit(solution)/shard_map/ppermute | solution.py:422
  712.6 6.8 collective-permute-start.26
  719.4 6.7 collective-permute-start.13
  726.2 6.7 collective-permute-start.10
  732.9 22.3 %collective-permute-start.23 = (bf16[96,2304]{1,0:T(8,128)(2,1)S(1)}, bf16[96,2304]{1,0:T(8,128)(2,1)S(1)}, u32[]{:S(2)}, u32[]{:S(2)}) collective-permute-start(bf16[96,2304]{1,0:T(8,128)(2,1)S(1)} %add_convert_fusion.4), channel_id=1, source_target_pairs={{0,3},{1,2},{2,1},{3,0},{4,7},{5,6},{6,5},{7,4},{8,11},{9,10},{10,... | collective-permute-start | bytes 1327112 | tf_op jit(solution)/shard_map/ppermute | solution.py:422
  733.1 29.5 %collective-permute-start.7 = (bf16[96,2304]{1,0:T(8,128)(2,1)S(1)}, bf16[96,2304]{1,0:T(8,128)(2,1)S(1)}, u32[]{:S(2)}, u32[]{:S(2)}) collective-permute-start(bf16[96,2304]{1,0:T(8,128)(2,1)S(1)} %add_convert_fusion.5), channel_id=1, source_target_pairs={{0,3},{1,2},{2,1},{3,0},{4,7},{5,6},{6,5},{7,4},{8,11},{9,10},{10,... | collective-permute-start | bytes 1327112 | tf_op jit(solution)/shard_map/ppermute | solution.py:422
  735.4 36.8 %collective-permute-start.30 = (bf16[96,3072]{1,0:T(8,128)(2,1)S(1)}, bf16[96,3072]{1,0:T(8,128)(2,1)S(1)}, u32[]{:S(2)}, u32[]{:S(2)}) collective-permute-start(bf16[96,3072]{1,0:T(8,128)(2,1)S(1)} %pad_maximum_fusion.12), channel_id=1, source_target_pairs={{0,1},{1,0},{2,3},{3,2},{4,5},{5,4},{6,7},{7,6},{8,9},{9,8},{10,11... | collective-permute-start | bytes 1769480 | tf_op jit(solution)/shard_map/ppermute | solution.py:422
  736.6 38.3 %collective-permute-start.14 = (bf16[96,3072]{1,0:T(8,128)(2,1)S(1)}, bf16[96,3072]{1,0:T(8,128)(2,1)S(1)}, u32[]{:S(2)}, u32[]{:S(2)}) collective-permute-start(bf16[96,3072]{1,0:T(8,128)(2,1)S(1)} %pad_maximum_fusion.11), channel_id=1, source_target_pairs={{0,1},{1,0},{2,3},{3,2},{4,5},{5,4},{6,7},{7,6},{8,9},{9,8},{10,11... | collective-permute-start | bytes 1769480 | tf_op jit(solution)/shard_map/ppermute | solution.py:422
  738.3 25.5 %collective-permute-start.45 = (bf16[480,384]{1,0:T(8,128)(2,1)S(1)}, bf16[480,384]{1,0:T(8,128)(2,1)S(1)}, u32[]{:S(2)}, u32[]{:S(2)}) collective-permute-start(bf16[480,384]{1,0:T(8,128)(2,1)S(1)} %dynamic-slice_bitcast_fusion.21), channel_id=1, source_target_pairs={{0,8},{4,12},{8,0},{12,4},{16,24},{20,28},{24,16},{28,20},{1,9},{5... | collective-permute-start | bytes 1105928 | tf_op jit(solution)/shard_map/ppermute | solution.py:422
  755.2 9.8 %collective-permute-start.42 = (bf16[480,384]{1,0:T(8,128)(2,1)S(1)}, bf16[480,384]{1,0:T(8,128)(2,1)S(1)}, u32[]{:S(2)}, u32[]{:S(2)}) collective-permute-start(bf16[480,384]{1,0:T(8,128)(2,1)S(1)} %dynamic-slice_bitcast_fusion.22), channel_id=1, source_target_pairs={{0,16},{4,20},{8,24},{12,28},{16,0},{20,4},{24,8},{28,12},{1,17},{... | collective-permute-start | bytes 1105928 | tf_op jit(solution)/shard_map/ppermute | solution.py:422
  762.5 8.5 collective-permute-start.37
  763.9 8.1 collective-permute-start.34
  765.1 34.3 %collective-permute-start.46 = (bf16[480,768]{1,0:T(8,128)(2,1)S(1)}, bf16[480,768]{1,0:T(8,128)(2,1)S(1)}, u32[]{:S(2)}, u32[]{:S(2)}) collective-permute-start(bf16[480,768]{1,0:T(8,128)(2,1)S(1)} %pad_maximum_fusion.10), channel_id=1, source_target_pairs={{0,1},{1,0},{2,3},{3,2},{4,5},{5,4},{6,7},{7,6},{8,9},{9,8},{10,11... | collective-permute-start | bytes 2211848 | tf_op jit(solution)/shard_map/ppermute | solution.py:422
  772.1 34.4 %collective-permute-start.38 = (bf16[480,768]{1,0:T(8,128)(2,1)S(1)}, bf16[480,768]{1,0:T(8,128)(2,1)S(1)}, u32[]{:S(2)}, u32[]{:S(2)}) collective-permute-start(bf16[480,768]{1,0:T(8,128)(2,1)S(1)} %pad_maximum_fusion.9), channel_id=1, source_target_pairs={{0,1},{1,0},{2,3},{3,2},{4,5},{5,4},{6,7},{7,6},{8,9},{9,8},{10,11... | collective-permute-start | bytes 2211848 | tf_op jit(solution)/shard_map/ppermute | solution.py:422
  772.4 16.3 %collective-permute-start.31 = (bf16[96,3072]{1,0:T(8,128)(2,1)S(1)}, bf16[96,3072]{1,0:T(8,128)(2,1)S(1)}, u32[]{:S(2)}, u32[]{:S(2)}) collective-permute-start(bf16[96,3072]{1,0:T(8,128)(2,1)S(1)} %add_convert_fusion.2), channel_id=1, source_target_pairs={{0,3},{1,2},{2,1},{3,0},{4,7},{5,6},{6,5},{7,4},{8,11},{9,10},{10,... | collective-permute-start | bytes 1769480 | tf_op jit(solution)/shard_map/ppermute | solution.py:422
  775.1 24.1 %collective-permute-start.15 = (bf16[96,3072]{1,0:T(8,128)(2,1)S(1)}, bf16[96,3072]{1,0:T(8,128)(2,1)S(1)}, u32[]{:S(2)}, u32[]{:S(2)}) collective-permute-start(bf16[96,3072]{1,0:T(8,128)(2,1)S(1)} %add_convert_fusion.3), channel_id=1, source_target_pairs={{0,3},{1,2},{2,1},{3,0},{4,7},{5,6},{6,5},{7,4},{8,11},{9,10},{10,... | collective-permute-start | bytes 1769480 | tf_op jit(solution)/shard_map/ppermute | solution.py:422
  788.8 18.3 %copy-start.25 = (f32[2,96,5376]{2,1,0:T(8,128)S(1)}, f32[2,96,5376]{2,1,0:T(8,128)}, u32[]{:S(2)}) copy-start(f32[2,96,5376]{2,1,0:T(8,128)} %param.19) | copy-start | bytes 12386308
  799.3 7.8 copy-start.24
  799.4 7.7 copy-start
  799.7 73.1 %collective-permute-start.47 = (bf16[480,768]{1,0:T(8,128)(2,1)S(1)}, bf16[480,768]{1,0:T(8,128)(2,1)S(1)}, u32[]{:S(2)}, u32[]{:S(2)}) collective-permute-start(bf16[480,768]{1,0:T(8,128)(2,1)S(1)} %add_convert_fusion), channel_id=1, source_target_pairs={{0,3},{1,2},{2,1},{3,0},{4,7},{5,6},{6,5},{7,4},{8,11},{9,10},{10,... | collective-permute-start | bytes 2211848 | tf_op jit(solution)/shard_map/ppermute | solution.py:422
  806.7 78.7 %collective-permute-start.39 = (bf16[480,768]{1,0:T(8,128)(2,1)S(1)}, bf16[480,768]{1,0:T(8,128)(2,1)S(1)}, u32[]{:S(2)}, u32[]{:S(2)}) collective-permute-start(bf16[480,768]{1,0:T(8,128)(2,1)S(1)} %add_convert_fusion.1), channel_id=1, source_target_pairs={{0,3},{1,2},{2,1},{3,0},{4,7},{5,6},{6,5},{7,4},{8,11},{9,10},{10,... | collective-permute-start | bytes 2211848 | tf_op jit(solution)/shard_map/ppermute | solution.py:422
  807.1 78.4 %copy-start.29 = (f32[2,480,768]{2,1,0:T(8,128)S(1)}, f32[2,480,768]{2,1,0:T(8,128)}, u32[]{:S(2)}) copy-start(f32[2,480,768]{2,1,0:T(8,128)} %param.20) | copy-start | bytes 8847364
  872.8 12.7 %copy-start.28 = (f32[2,480,768]{2,1,0:T(8,128)S(1)}, f32[2,480,768]{2,1,0:T(8,128)}, u32[]{:S(2)}) copy-start(f32[2,480,768]{2,1,0:T(8,128)} %param.17) | copy-start | bytes 8847364
  872.9 12.6 %copy-start.2 = (f32[2,480,768]{2,1,0:T(8,128)S(1)}, f32[2,480,768]{2,1,0:T(8,128)}, u32[]{:S(2)}) copy-start(f32[2,480,768]{2,1,0:T(8,128)} %param.14) | copy-start | bytes 8847364
  (31 other events, 82.7 us)
Sparse Core Ops, SparseCore 0:
  450.3 121.6 all-reduce.3

commit v3 on v2

--- a/solution.py
+++ b/solution.py
@@ -400,6 +400,335 @@
     )(images, shard, vshard)
 
 
+def bwd_kernel(cot_ref, w_ref, vec_ref, hs_ref, h1_ref, g_ref, e_ref, qkv_ref, a2_ref, o_ref, a1_ref,
+               di_ref, gin_ref, gout_ref, gv_ref,
+               wk, d, db, dhb, do, du, ab, gb, dv, rc, s2, ra, rb, s3a, s3b, r3a, r3b, s4, rz, s5, ry, fin,
+               vs, vr, vz, wsem, asem, ssem, rsem, osem, vssem, vrsem):
+    lr, s = pl.program_id(0), pl.program_id(1)
+    l = LAYERS - 1 - lr
+    f, core, x, y = plane()
+    z = lax.axis_index("rep")
+    fc, fx, fy = f + 1 - 2 * core, f + 2 - 4 * x, f + 4 - 8 * y
+    z1, z3 = z + 1 - 2 * (z % 2), 3 - z
+    half = CH // 2
+    rows = d.shape[0] * RP
+
+    def load(layer, block, n, at):
+        return pltpu.make_async_copy(w_ref.at[pl.ds(pl.multiple_of((layer * NC + block) * D, 16), n * D)], wk.at[pl.ds(at * D, n * D)], wsem.at[0 if at else 1])
+
+    def fetch(src, slot):
+        return pltpu.make_async_copy(src.at[l], ab.at[slot], asem.at[slot])
+
+    def remote(kind, p, src, dst, **to):
+        return pltpu.make_async_remote_copy(src_ref=src, dst_ref=dst, send_sem=ssem.at[p, kind], recv_sem=rsem.at[p, kind],
+                                            device_id=to, device_id_type=MESH)
+
+    def chunk(v):
+        return v - 6 * (v // 18)
+
+    def live(v):
+        return ((v >= 0) & (v < 12)) | ((v >= 18) & (v < 30))
+
+    def kind(n, v):
+        p = v % 2
+        if n == 0:
+            lc = chunk(v) % NC
+            return remote(0, p, gb.at[lc - 9 * (lc // 9), :, 1 - core], rc.at[p], fsdp=fc)
+        if n == 1:
+            return remote(1, p, s2.at[p, :, 1 - x, pl.ds(0, half)], ra.at[p], fsdp=fx)
+        if n == 2:
+            return remote(2, p, s2.at[p, 1 - y, :, pl.ds(half, half)], rb.at[p], fsdp=fy)
+        if n == 3:
+            return remote(3, p, s3a.at[p, 1 - y], r3a.at[p], fsdp=fy)
+        if n == 4:
+            return remote(4, p, s3b.at[p, 1 - x], r3b.at[p], fsdp=fx)
+        if n == 5:
+            return remote(5, p, s4.at[p], rz.at[p], rep=z1)
+        return remote(6, p, s5.at[p], ry.at[p], rep=z3)
+
+    def put(v, act):
+        c = chunk(v)
+        lc, layer = c % NC, LAYERS - 1 - c // NC
+        p = v % 2
+        out = (lc >= 4) & (lc < 9)
+
+        @pl.when(out)
+        def _():
+            act(pltpu.make_async_copy(fin.at[p], gout_ref.at[layer, pl.ds(pl.multiple_of((lc - 4) * CH, 8), CH)], osem.at[p]))
+
+        @pl.when(jnp.logical_not(out))
+        def _():
+            j = lc + 3 - 9 * (lc // 9)
+            j = j - 3 * (lc // 9)
+            act(pltpu.make_async_copy(fin.at[p], gin_ref.at[layer, :, pl.ds(pl.multiple_of(j * D, 128), D)], osem.at[p]))
+
+    def add(a, b):
+        return a.astype(F32) + b.astype(F32)
+
+    def tick(t):
+        @pl.when(live(t - 6))
+        def _():
+            put(t - 6, lambda a: a.wait())
+
+        @pl.when(live(t - 5))
+        def _():
+            v = t - 5
+            p = v % 2
+            kind(6, v).wait()
+            fin[p] = add(s5[p], ry[p])
+            put(v, lambda a: a.start())
+
+        @pl.when(live(t - 4))
+        def _():
+            v = t - 4
+            p = v % 2
+            kind(5, v).wait()
+            s5[p] = add(s4[p], rz[p]).astype(BF)
+            kind(6, v).start()
+
+        @pl.when(live(t - 3))
+        def _():
+            v = t - 3
+            p = v % 2
+            kind(3, v).wait()
+            kind(4, v).wait()
+            s4[p, 0:half] = add(s3a[p, y], r3a[p]).astype(BF)
+            s4[p, half:CH] = add(s3b[p, x], r3b[p]).astype(BF)
+            kind(5, v).start()
+
+        @pl.when(live(t - 2))
+        def _():
+            v = t - 2
+            p = v % 2
+            kind(1, v).wait()
+            kind(2, v).wait()
+            for i in range(2):
+                s3a[p, i] = add(s2[p, i, x, 0:half], ra[p, i]).astype(BF)
+                s3b[p, i] = add(s2[p, y, i, half:CH], rb[p, i]).astype(BF)
+            kind(3, v).start()
+            kind(4, v).start()
+
+        @pl.when(live(t - 1))
+        def _():
+            v = t - 1
+            p = v % 2
+            kind(0, v).wait()
+            lc = chunk(v) % NC
+            for i in range(4):
+                s2[p, i // 2, i % 2] = add(gb[lc - 9 * (lc // 9), i, core], rc[p, i]).astype(BF)
+            kind(1, v).start()
+            kind(2, v).start()
+
+        @pl.when(live(t))
+        def _():
+            kind(0, t).start()
+
+    @pl.when((lr == 0) & (s == 0))
+    def _():
+        load(l, 3, 9, 0).start()
+        bar = pltpu.get_barrier_semaphore()
+        for k in range(1, 8):
+            pl.semaphore_signal(bar, inc=1, device_id={"fsdp": (f + k) % 8}, device_id_type=MESH)
+        for k in range(1, 4):
+            pl.semaphore_signal(bar, inc=1, device_id={"rep": (z + k) % 4}, device_id_type=MESH)
+        pl.semaphore_wait(bar, 10)
+        dv[...] = jnp.zeros_like(dv)
+        load(l, 3, 9, 0).wait()
+
+    @pl.when((lr == 1) & (s == 0))
+    def _():
+        load(l, 3, 3, 0).start()
+        load(l, 3, 3, 0).wait()
+        load(l, 6, 6, 3).wait()
+
+    @pl.when(s == 0)
+    def _():
+        fetch(a2_ref, 0).start()
+        fetch(o_ref, 1).start()
+
+    @pl.when(s == 5)
+    def _():
+        fetch(a2_ref, 0).wait()
+        load(l, 0, 3, 0).start()
+
+        @pl.when(lr == 0)
+        def _():
+            load(l - 1, 6, 6, 3).start()
+
+    @pl.when(s == 9)
+    def _():
+        fetch(o_ref, 1).wait()
+
+    @pl.when(s == 10)
+    def _():
+        fetch(a1_ref, 0).start()
+
+    @pl.when(s == 19)
+    def _():
+        fetch(a1_ref, 0).wait()
+
+    @pl.when(s == 22)
+    def _():
+        load(l, 0, 3, 0).wait()
+
+    even = 1 - s % 2
+    first = (s >= 6) & (s <= 12) & (even == 1)
+    second = (s >= 14) & (s <= 18)
+    third = (s >= 20) & ((even == 1) | (lr == 1))
+    start = (s <= 4) & (lr == 1)
+    t = jnp.where(first, 18 * lr + (s - 6) // 2, jnp.where(second, 18 * lr + s - 10, jnp.where(start, 13 + s, lr * (s + 7) + (1 - lr) * ((s - 20) // 2 + 9))))
+
+    @pl.when(first | second | third | start)
+    def _():
+        tick(t)
+
+    @pl.when(s < 5)
+    def _():
+        i = s
+
+        @pl.when(lr == 0)
+        def _():
+            d[i] = jnp.zeros((RP, D), F32)
+            d[i, 0:SEQ, :] = cot_ref[0].astype(F32)
+        up = d[i]
+        db[i] = up.astype(BF)
+        dv[l, 7:8] += rsum(up)
+        acc = None
+        for j in range(12):
+            cs = slice(256 * j, 256 * j + 256)
+            r = (5 * D + 256 * j)
+            t1 = dot_t(db[i], wk[r:r + 256, :]) * g_ref[0, 0, :, cs].astype(F32)
+            dv[l, 8 + j // 3:9 + j // 3, 256 * (j % 3):256 * (j % 3) + 256] += rsum(t1)
+            du[i, :, cs] = t1.astype(BF)
+            t2 = dot_t(du[i, :, cs], wk[(j // 3) * D:(j // 3) * D + D, 256 * (j % 3):256 * (j % 3) + 256])
+            acc = t2 if acc is None else acc + t2
+        dx, dg, dc = norm_back(h1_ref[0, 0], vec_ref[l, 5:6], acc)
+        dv[l, 5:6] += dg
+        dv[l, 6:7] += dc
+        dh1 = d[i] + dx
+        d[i] = dh1
+        dv[l, 4:5] += rsum(dh1)
+        dhb[i] = dh1.astype(BF)
+        do[i] = dot_t(dhb[i], wk[4 * D:5 * D, :]).astype(BF)
+
+    def grad(lhs, rhs, store):
+        for m in range(2):
+            r = dot_0(lhs(384 * m), rhs).astype(BF).reshape(4, CH, D)
+            store(4 * m, r)
+
+    def inner(slot, j):
+        def store(m, r):
+            gb[slot, m // 2, 0] = r[0]
+            gb[slot, m // 2, 1] = r[1]
+            gb[slot, m // 2 + 1, 0] = r[2]
+            gb[slot, m // 2 + 1, 1] = r[3]
+        grad(lambda m: ab[0, :, :, m:m + 384].reshape(rows, 384), du[:, :, pl.ds(pl.multiple_of(D * j, 128), D)].reshape(rows, D), store)
+
+    def outer(step, lhs, rhs):
+        def store(m, r):
+            for q in range(4):
+                b = 8 * step + m + q
+                gb[4 + b % 5, b // 10, (b // 5) % 2] = r[q]
+        grad(lhs, rhs[...].reshape(rows, D), store)
+
+    @pl.when((s >= 5) & (s < 9))
+    def _():
+        inner(s - 5, s - 5)
+
+    @pl.when(s == 9)
+    def _():
+        outer(0, lambda m: ab[1, :, :, m:m + 384].reshape(rows, 384), dhb)
+
+    @pl.when((s >= 10) & (s < 14))
+    def _():
+        outer(s - 9, lambda m: e_ref[0, :, :, m:m + 384].reshape(rows, 384), db)
+
+    @pl.when((s >= 14) & (s < 19))
+    def _():
+        i = s - 14
+        for p in range(6):
+            b = 128 * p
+            dq, dk, dvv = attn_bwd(qkv_ref[0, 0, :, b:b + 128], qkv_ref[0, 0, :, D + b:D + b + 128], qkv_ref[0, 0, :, 2 * D + b:2 * D + b + 128],
+                                   do[i, :, b:b + 128])
+            dv[l, 2:3, b:b + 128] += rsum(dq)
+            dv[l, 3:4, b:b + 128] += rsum(dvv)
+            du[i, :, b:b + 128] = dq.astype(BF)
+            du[i, :, D + b:D + b + 128] = dk.astype(BF)
+            du[i, :, 2 * D + b:2 * D + b + 128] = dvv.astype(BF)
+
+    @pl.when((s >= 19) & (s < 22))
+    def _():
+        inner(s - 19, s - 19)
+
+    @pl.when(s >= 22)
+    def _():
+        i = s - 22
+        da = dot_t(du[i, :, 0:D], wk[0:D, :]) + dot_t(du[i, :, D:2 * D], wk[D:2 * D, :]) + dot_t(du[i, :, 2 * D:3 * D], wk[2 * D:3 * D, :])
+        dx, dg, dc = norm_back(hs_ref[0, 0], vec_ref[l, 0:1], da)
+        dv[l, 0:1] += dg
+        dv[l, 1:2] += dc
+        dh = d[i] + dx
+        d[i] = dh
+        di_ref[0] = dh[0:SEQ]
+
+    @pl.when((lr == 1) & (s == 26))
+    def _():
+        for layer in range(LAYERS):
+            for c in range(72):
+                vs[c // 9, layer, c % 9:c % 9 + 1, :] = dv[layer, c // 6:c // 6 + 1, 128 * (c % 6):128 * (c % 6) + 128]
+
+        def vcopy(k):
+            to = (f + k) % 8
+            return pltpu.make_async_remote_copy(src_ref=vs.at[to], dst_ref=vr.at[k - 1], send_sem=vssem.at[k - 1], recv_sem=vrsem.at[k - 1],
+                                                device_id={"fsdp": to}, device_id_type=MESH)
+
+        def zcopy(k):
+            return pltpu.make_async_remote_copy(src_ref=vz.at[z], dst_ref=vz.at[z], send_sem=vssem.at[6 + k], recv_sem=vrsem.at[6 + k],
+                                                device_id={"rep": (z + k) % 4}, device_id_type=MESH)
+        for k in range(1, 8):
+            vcopy(k).start()
+        tick(34)
+        for k in range(1, 8):
+            vcopy(k).wait()
+        total = vs[f]
+        for k in range(7):
+            total = total + vr[k]
+        vz[z] = total
+        for k in range(1, 4):
+            zcopy(k).start()
+        for k in range(1, 4):
+            zcopy(k).wait()
+        gv_ref[...] = (vz[0] + vz[1]) + (vz[2] + vz[3])
+        put(29, lambda a: a.wait())
+
+
+def bwd(cotangent, w, vec, hs, h1, g, e, qkv, a2, o, a1, shard_in, shard_out):
+    n = cotangent.shape[0]
+    S = jax.ShapeDtypeStruct
+    anyw = pl.BlockSpec(memory_space=pl.ANY)
+    row = lambda cols, at: pl.BlockSpec((1, 1, RP, cols), lambda lr, s: (LAYERS - 1 - lr, jnp.clip(s - at, 0, 4), 0, 0))
+    tok = lambda index: pl.BlockSpec((1, SEQ, D), index)
+    VB = lambda *shape: pltpu.VMEM(shape, BF)
+    half = CH // 2
+    return pl.pallas_call(
+        bwd_kernel, grid=(LAYERS, 27),
+        in_specs=[tok(lambda lr, s: (jnp.minimum(s + 4 * lr, 4), 0, 0)), anyw, pl.BlockSpec(vec.shape, lambda lr, s: (0, 0, 0)),
+                  row(D, 22), row(D, 0), row(4 * D, 0),
+                  pl.BlockSpec((1, n, RP, D), lambda lr, s: (LAYERS - 1 - lr, 0, 0, jnp.clip(s - 10, 0, 3))),
+                  row(3 * D, 14), anyw, anyw, anyw],
+        out_specs=[tok(lambda lr, s: (lr * jnp.clip(s - 22, 0, 4), 0, 0)), anyw, anyw, pl.BlockSpec((LAYERS, 16, 128), lambda lr, s: (0, 0, 0))],
+        out_shape=[S(cotangent.shape, F32), S(shard_in, F32), S(shard_out, F32), S((LAYERS, 16, 128), F32)],
+        scratch_shapes=[VB(9 * D, D), pltpu.VMEM((n, RP, D), F32), VB(n, RP, D), VB(n, RP, D), VB(n, RP, D), VB(n, RP, 4 * D), VB(2, n, RP, D),
+                        VB(9, 4, 2, CH, D), pltpu.VMEM((LAYERS, 16, D), F32),
+                        VB(2, 4, CH, D), VB(2, 2, 2, CH, D), VB(2, 2, half, D), VB(2, 2, half, D), VB(2, 2, half, D), VB(2, 2, half, D),
+                        VB(2, half, D), VB(2, half, D), VB(2, CH, D), VB(2, CH, D), VB(2, CH, D), VB(2, CH, D), pltpu.VMEM((2, CH, D), F32),
+                        pltpu.VMEM((8, LAYERS, 16, 128), F32), pltpu.VMEM((7, LAYERS, 16, 128), F32), pltpu.VMEM((4, LAYERS, 16, 128), F32),
+                        pltpu.SemaphoreType.DMA((2,)), pltpu.SemaphoreType.DMA((2,)), pltpu.SemaphoreType.DMA((2, 7)), pltpu.SemaphoreType.DMA((2, 7)),
+                        pltpu.SemaphoreType.DMA((2,)), pltpu.SemaphoreType.DMA((10,)), pltpu.SemaphoreType.DMA((10,))],
+        compiler_params=pltpu.CompilerParams(collective_id=1, has_side_effects=True, vmem_limit_bytes=63 * 2**20),
+    )(cotangent, w, vec, hs, h1, g, e, qkv, a2, o, a1)
+
+
 STEP = 3
 beta_one = 0.9
 beta_two = 0.999
@@ -461,56 +790,54 @@
     return jnp.concatenate([a[:, :3], b, a[:, 3:]], axis=1).reshape(LAYERS * NC, CH, D)
 
 
-def fused_forward(images, weight_in, weight_out, vector_params):
+def fused_step(images, cotangent, weight_in, weight_out, vector_params):
     vs = jnp.pad(vector_params.astype(BF).astype(F32).reshape(LAYERS, 9, 128), ((0, 0), (0, 7), (0, 0)))
     hs, qkv, a1, o, h1, a2, e, g, encoded, w, vec = fwd(images, own_shard(weight_in, weight_out), vs)
+    dimg, gi, go, gv = bwd(cotangent, w, vec, hs, h1, g, e, qkv, a2, o, a1, weight_in.shape, weight_out.shape)
+    return encoded, dimg, gi, go, gv[:, :9].reshape(vector_params.shape)
+
+
+def plain_step(nf, nr, images, cotangent, weight_in, weight_out, vector_params):
+    pad = lambda a: jnp.pad(a, ((0, 0), (0, RP - SEQ), (0, 0)))
+    vec_all = lax.all_gather(vector_params.astype(BF), "fsdp", axis=1, tiled=True).astype(F32)
+    h = pad(images)
+    ct = pad(cotangent)
     saved = []
     for l in range(LAYERS):
-        blk = lambda b, n: w[(l * NC + b) * D : (l * NC + b + n) * D]
-        wqkv = jnp.concatenate([blk(0, 1), blk(1, 1), blk(2, 1)], axis=1)
-        w1 = jnp.concatenate([blk(3 + j, 1) for j in range(4)], axis=1)
-        saved.append((hs[l], wqkv, w1, blk(7, 1), blk(8, 4), vec[l], qkv[l], o[l], a1[l], h1[l], a2[l], e[l], g[l]))
-    return encoded, saved
+        win = lax.all_gather(weight_in[l].astype(BF), "fsdp", axis=0, tiled=True)
+        wout = lax.all_gather(weight_out[l].astype(BF), "fsdp", axis=0, tiled=True)
+        vec = jnp.pad(vec_all[l].reshape(12, D), ((0, 4), (0, 0)))
+        wqkv, w1, wo, w2 = win[:, : 3 * D], win[:, 3 * D :], wout[:D], wout[D:]
+        qkv, o, a1 = ka(h, wqkv, vec)
+        h1, a2, e, g, h2 = kb(h, o, wo, w1, w2, vec)
+        saved.append((h, wqkv, w1, wo, w2, vec, qkv, o, a1, h1, a2, e, g))
+        h = h2
+    encoded = h[:, :SEQ].astype(BF)
+    d = ct
+    gin, gout, gvec = [None] * LAYERS, [None] * LAYERS, [None] * LAYERS
+    for l in reversed(range(LAYERS)):
+        h, wqkv, w1, wo, w2, vec, qkv, o, a1, h1, a2, e, g = saved[l]
+        db, du, dh1, dh1b, do, dv1 = kc(d, h1, g, wo, w1, w2, vec)
+        g1 = reduce_all(dw(a2, du), nf, nr)
+        go = reduce_all(jnp.concatenate([dw(o, dh1b), dw(e, db)], axis=0), nf, nr)
+        dz, dv2 = kd(qkv, do)
+        gq = reduce_all(dw(a1, dz), nf, nr)
+        d, dv3 = kf(dz, h, dh1, wqkv, vec, RP if l else SEQ)
+        gin[l] = jnp.concatenate([gq, g1], axis=1)
+        gout[l] = go
+        gvec[l] = (dv1 + dv2 + dv3)[:12].reshape(-1)
+    gv = lax.psum(jnp.stack(gvec), ("fsdp", "rep"))
+    wide = gv.shape[1] // nf
+    gv = lax.dynamic_slice_in_dim(gv, lax.axis_index("fsdp") * wide, wide, 1)
+    return encoded, d, jnp.stack(gin), jnp.stack(gout), gv
 
 
 def make_shards(nf, nr):
     def shards(images, cotangent, weight_in, weight_out, vector_params, first_in, first_out, first_vec, second_in, second_out, second_vec):
-        pad = lambda a: jnp.pad(a, ((0, 0), (0, RP - SEQ), (0, 0)))
-        ct = pad(cotangent)
-        if nf == 8:
-            encoded, saved = fused_forward(images, weight_in, weight_out, vector_params)
+        if nf == 8 and nr == 4:
+            encoded, d, gi, go, gv = fused_step(images, cotangent, weight_in, weight_out, vector_params)
         else:
-            vec_all = lax.all_gather(vector_params.astype(BF), "fsdp", axis=1, tiled=True).astype(F32)
-            h = pad(images)
-            ct = pad(cotangent)
-            saved = []
-            for l in range(LAYERS):
-                win = lax.all_gather(weight_in[l].astype(BF), "fsdp", axis=0, tiled=True)
-                wout = lax.all_gather(weight_out[l].astype(BF), "fsdp", axis=0, tiled=True)
-                vec = jnp.pad(vec_all[l].reshape(12, D), ((0, 4), (0, 0)))
-                wqkv, w1, wo, w2 = win[:, : 3 * D], win[:, 3 * D :], wout[:D], wout[D:]
-                qkv, o, a1 = ka(h, wqkv, vec)
-                h1, a2, e, g, h2 = kb(h, o, wo, w1, w2, vec)
-                saved.append((h, wqkv, w1, wo, w2, vec, qkv, o, a1, h1, a2, e, g))
-                h = h2
-            encoded = h[:, :SEQ].astype(BF)
-        d = ct
-        gin, gout, gvec = [None] * LAYERS, [None] * LAYERS, [None] * LAYERS
-        for l in reversed(range(LAYERS)):
-            h, wqkv, w1, wo, w2, vec, qkv, o, a1, h1, a2, e, g = saved[l]
-            db, du, dh1, dh1b, do, dv1 = kc(d, h1, g, wo, w1, w2, vec)
-            g1 = reduce_all(dw(a2, du), nf, nr)
-            go = reduce_all(jnp.concatenate([dw(o, dh1b), dw(e, db)], axis=0), nf, nr)
-            dz, dv2 = kd(qkv, do)
-            gq = reduce_all(dw(a1, dz), nf, nr)
-            d, dv3 = kf(dz, h, dh1, wqkv, vec, RP if l else SEQ)
-            gin[l] = jnp.concatenate([gq, g1], axis=1)
-            gout[l] = go
-            gvec[l] = (dv1 + dv2 + dv3)[:12].reshape(-1)
-        gv = lax.psum(jnp.stack(gvec), ("fsdp", "rep"))
-        wide = gv.shape[1] // nf
-        gv = lax.dynamic_slice_in_dim(gv, lax.axis_index("fsdp") * wide, wide, 1)
-        gi, go = jnp.stack(gin), jnp.stack(gout)
+            encoded, d, gi, go, gv = plain_step(nf, nr, images, cotangent, weight_in, weight_out, vector_params)
         new_in, moment_in, square_in = adam_update(weight_in, gi, first_in, second_in, matrix_rate, matrix_decay)
         new_out, moment_out, square_out = adam_update(weight_out, go, first_out, second_out, matrix_rate, matrix_decay)
         new_vec, moment_vec, square_vec = adam_update(vector_params, gv, first_vec, second_vec, vector_rate, 0.0)

time: 910 us -> 503 us (0.55)
  waiting for transfers between devices: 288 us -> 0 us
  local copies, waits for them, and re-layouts: 122 us -> 20 us
  Pallas kernels: 371 us -> 457 us
  other arithmetic: 67.1 us -> 22.4 us
  starting transfers between devices: 36 us -> 0 us
  between operations: 15.9 us -> 0.76 us
    ppermute x48 -> x0, waiting for transfers between devices: 250 us -> none  [swap(): return lax.ppermute(x, axis, [(i, i ^ mask) for i in range(size)])]
    pallas_call x14 -> x1, Pallas kernels: 197 us -> 283 us  [bwd(): pl.pallas_call(bwd_kernel, grid=(LAYERS, 27), in_specs=[tok(lambda lr, s:...]
    slice x11 -> x0, local copies, waits for them, and re-layouts: 52.3 us -> none  [the longest x2 19.9 us: fused_forward(): blk = lambda b, n: w[(l * NC + b) * D:(l * NC + b + n) * D]]
    squeeze x37 -> x0, local copies, waits for them, and re-layouts: 43.4 us -> none  [the longest x33 13.4 us: halve(): send = lax.dynamic_index_in_dim(x, 1 - mine, at, keepdims=False)]
    psum x1 -> x0, waiting for transfers between devices: 38.2 us -> none  [shards(): gv = lax.psum(jnp.stack(gvec), ('fsdp', 'rep'))]
    ppermute x48 -> x0, starting transfers between devices: 36 us -> none  [swap(): return lax.ppermute(x, axis, [(i, i ^ mask) for i in range(size)])]
    concatenate x10 -> x0, other arithmetic: 28.2 us -> none  [the longest x1 14.8 us: fused_forward(): wqkv = jnp.concatenate([blk(0, 1), blk(1, 1), blk(2, 1)], axis=1)]
    convert_element_type x43 -> x1, other arithmetic: 14.8 us -> 0.71 us  [fused_step(): vector_params.astype(BF).astype(F32).reshape(LAYERS, 9, 128)]
  transfers between devices with their start and end apart: 49 -> 0, of which waited for: 25 -> 0; matrix products, arithmetic and copies ran while one was open for 11% -> 0% of each run, Pallas kernels for 18% -> 0%
where the time goes in v3:
time: 503 us; the launch traced here: 500 us
  Pallas kernels  457 us (91%)
  other arithmetic  22.4 us (4%)
  local copies, waits for them, and re-layouts  20 us (4%)
    pallas_call x1, Pallas kernels, bwd(): pl.pallas_call(bwd_kernel, grid=(LAYERS, 27), in_specs=[tok(lambda lr, s:...  283 us
    pallas_call x1, Pallas kernels, fwd(): pl.pallas_call(fwd_kernel, grid=(LAYERS, 14), in_specs=[pl.BlockSpec(imag...  174 us
    unnamed x29, local copies, waits for them, and re-layouts  14.8 us
    sub x3, other arithmetic, adam_update(): master - rate * (adam_move + decay_rate * master)  14.2 us

profile of v3, /device:TPU:8, one launch (start us, length us, event | category | flops | bytes accessed | tf_op | source)
XLA Modules:
  0.0 500.4 jit_solution(7081391138787181757)
XLA Ops:
  0.6 0.7 convert_element_type.14
  1.4 0.0 copy-start
  1.4 0.6 pad_convert_fusion.vs_ref
  2.0 3.4 convert_element_type.13
  5.4 0.0 copy-done
  5.4 1.5 convert_element_type.12
  6.9 4.0 reshape.44
  10.9 0.6 slice.13
  11.5 0.0 copy-start.4
  11.5 0.3 slice.12
  11.8 0.1 copy.26
  11.9 0.1 copy.27
  12.1 0.8 copy-done.4
  12.9 2.0 pad_maximum_fusion
  14.9 174.3 %shard_map.218 = (f32[2,5,208,768]{3,2,1,0:T(8,128)}, bf16[2,5,208,2304]{3,2,1,0:T(8,128)(2,1)}, bf16[2,5,208,768]{3,2,1,0:T(8,128)(2,1)}, bf16[2,5,208,768]{3,2...) custom-call(bf16[5,197,768]{2,1,0:T(8,128)(2,1)} %img_ref.1, ...), custom_call_target="tpu_custom_call" | custom-call | tf_op jit(solution)/shard_map/pallas_call | solution.py:388
  189.2 0.0 copy-start.9
  189.2 0.0 copy-start.10
  189.2 0.0 copy-start.11
  189.2 283.0 %shard_map.219 = (f32[5,197,768]{2,1,0:T(8,128)}, f32[2,96,5376]{2,1,0:T(8,128)}, f32[2,480,768]{2,1,0:T(8,128)}, f32[2,16,128]{2,1,0:T(8,128)}) custom-call(bf16[5,197,768]{2,1,0:T(8,128)(2,1)} %cot_ref.1, bf16[18432,768]{1,0:T(8,128)(2,1)} %get-tuple-element.30.w_ref, f32[2,16,768]{2,1,0:T(8,128)} %get-tuple-element.31.vec_ref, ...), custom_call_target="tpu_custom_call" | custom-call | tf_op jit(solution)/shard_map/pallas_call | solution.py:713
  472.2 0.7 slice_bitcast_fusion
  472.9 0.0 copy-done.9
  472.9 0.0 copy-done.10
  473.0 0.0 copy-done.11
  473.0 0.6 multiply_subtract_fusion.2
  473.6 0.0 copy-start.1
  473.6 0.0 copy-start.2
  473.6 0.0 copy-start.5
  473.6 0.0 copy-start.6
  473.6 8.0 %multiply_subtract_fusion.1 = (f32[2,480,768]{2,1,0:T(8,128)}, f32[2,480,768]{2,1,0:T(8,128)}, f32[2,480,768]{2,1,0:T(8,128)}) fusion(f32[2,480,768]{2,1,0:T(8,128)} %param.14, f32[2,480,768]{2,1,0:T(8,128)} %get-tuple-element.71, f32[2,480,768]{2,1,0:T(8,128)} %param.17, f32[2,480,768]{2,1,0:T(8,128)} %param.20), kind=kLoop, calls=%fused_computation.7 | loop fusion | flops 11059200 | bytes 20643840 | tf_op jit(solution)/shard_map/sub | solution.py:747
  481.6 0.4 copy-done.1
  482.0 1.6 copy-done.2
  483.5 1.2 copy-done.5
  484.7 1.2 copy-done.6
  485.9 0.0 copy-start.8
  485.9 5.6 %multiply_subtract_fusion = (f32[2,96,5376]{2,1,0:T(8,128)}, f32[2,96,5376]{2,1,0:T(8,128)}, f32[2,96,5376]{2,1,0:T(8,128)}) fusion(f32[2,96,5376]{2,1,0:T(8,128)S(1)} %copy-done.1, f32[2,96,5376]{2,1,0:T(8,128)S(1)} %copy-done.2, f32[2,96,5376]{2,1,0:T(8,128)S(1)} %copy-done.5, f32[2,96,5376]{2,1,0:T(8,128)S(1)} %copy-done.6), kind=kLoop, calls=%fused_computation.3 | loop fusion | flops 15482880 | bytes 28901376 | tf_op jit(solution)/shard_map/sub | solution.py:747
  491.4 0.0 copy-start.7
  491.4 0.0 copy-done.8
  491.5 1.1 copy.35
  492.6 1.3 copy-done.7
  493.9 1.6 copy.36
  495.5 0.0 copy-start.3
  495.5 2.1 copy.37
  497.6 1.2 copy-done.3
  498.8 1.6 copy.38
  (1 shorter events, 0.0 us)
Async XLA Ops:
  1.4 4.0 copy-start
  11.5 1.4 copy-start.4
  189.2 283.7 %copy-start.9 = (f32[2,1152]{1,0:T(2,128)S(1)}, f32[2,1152]{1,0:T(2,128)}, u32[]{:S(2)}) copy-start(f32[2,1152]{1,0:T(2,128)} %param.15) | copy-start | bytes 27652
  189.2 283.7 %copy-start.10 = (f32[2,1152]{1,0:T(2,128)S(1)}, f32[2,1152]{1,0:T(2,128)}, u32[]{:S(2)}) copy-start(f32[2,1152]{1,0:T(2,128)} %param.18) | copy-start | bytes 27652
  189.2 283.7 %copy-start.11 = (f32[2,1152]{1,0:T(2,128)S(1)}, f32[2,1152]{1,0:T(2,128)}, u32[]{:S(2)}) copy-start(f32[2,1152]{1,0:T(2,128)} %param.21) | copy-start | bytes 27652
  473.6 8.4 %copy-start.1 = (f32[2,96,5376]{2,1,0:T(8,128)S(1)}, f32[2,96,5376]{2,1,0:T(8,128)}, u32[]{:S(2)}) copy-start(f32[2,96,5376]{2,1,0:T(8,128)} %param.13) | copy-start | bytes 12386308
  473.6 9.9 %copy-start.2 = (f32[2,96,5376]{2,1,0:T(8,128)S(1)}, f32[2,96,5376]{2,1,0:T(8,128)}, u32[]{:S(2)}) copy-start(f32[2,96,5376]{2,1,0:T(8,128)} %get-tuple-element.70) | copy-start | bytes 12386308
  473.6 11.1 %copy-start.5 = (f32[2,96,5376]{2,1,0:T(8,128)S(1)}, f32[2,96,5376]{2,1,0:T(8,128)}, u32[]{:S(2)}) copy-start(f32[2,96,5376]{2,1,0:T(8,128)} %param.16) | copy-start | bytes 12386308
  473.6 12.3 %copy-start.6 = (f32[2,96,5376]{2,1,0:T(8,128)S(1)}, f32[2,96,5376]{2,1,0:T(8,128)}, u32[]{:S(2)}) copy-start(f32[2,96,5376]{2,1,0:T(8,128)} %param.19) | copy-start | bytes 12386308
  485.9 5.6 %copy-start.8 = (bf16[5,197,768]{2,1,0:T(8,128)(2,1)S(1)}, bf16[5,197,768]{2,1,0:T(8,128)(2,1)}, u32[]{:S(2)}) copy-start(bf16[5,197,768]{2,1,0:T(8,128)(2,1)} %get-tuple-element.68) | copy-start | bytes 4538884
  491.4 2.4 copy-start.7
  495.5 3.3 copy-start.3

commit v4 on v3

--- a/solution.py
+++ b/solution.py
@@ -215,7 +215,7 @@
         return w.at[pl.ds(pl.multiple_of(chunk_rows(c, who) + lo, 16), n)]
 
     def send(c, kind, src, dst, to):
-        return pltpu.make_async_remote_copy(src_ref=src, dst_ref=dst, send_sem=ssem.at[c % 4, kind], recv_sem=rsem.at[c % 4, kind],
+        return pltpu.make_async_remote_copy(src_ref=src, dst_ref=dst, send_sem=ssem.at[c % 8, kind], recv_sem=rsem.at[c % 8, kind],
                                             device_id={"fsdp": to}, device_id_type=MESH)
 
     def kinds(c):
@@ -224,7 +224,7 @@
                 lambda: send(c, 3, wrow(c, fx, 0, half), wrow(c, fx, 0, half), fy),
                 lambda: send(c, 4, wrow(c, fy, half, half), wrow(c, fy, half, half), fx),
                 lambda: send(c, 5, wrow(c, fx), wrow(c, fx), fc), lambda: send(c, 6, wrow(c, fy), wrow(c, fy), fc),
-                lambda: send(c, 7, wrow(c, fd), wrow(c, fd), fc), lambda: pltpu.make_async_copy(own, mine, lsem.at[c % 4])]
+                lambda: send(c, 7, wrow(c, fd), wrow(c, fd), fc), lambda: pltpu.make_async_copy(own, mine, lsem.at[c % 8])]
 
     def start(c, which):
         k = kinds(c)
@@ -237,19 +237,19 @@
             k[i]().wait()
 
     def tick(t):
+        @pl.when((t >= 4) & (t < 28))
+        def _():
+            wait(t - 4, (2, 5, 6, 7, 8))
+
         @pl.when((t >= 3) & (t < 27))
         def _():
-            wait(t - 3, (2, 5, 6, 7, 8))
+            wait(t - 3, (3, 4))
+            start(t - 3, (7,))
 
         @pl.when((t >= 2) & (t < 26))
         def _():
-            wait(t - 2, (3, 4))
-            start(t - 2, (7,))
-
-        @pl.when((t >= 1) & (t < 25))
-        def _():
-            wait(t - 1, (0, 1))
-            start(t - 1, (3, 4, 5, 6))
+            wait(t - 2, (0, 1))
+            start(t - 2, (3, 4, 5, 6))
 
         @pl.when(t < 24)
         def _():
@@ -272,7 +272,7 @@
             vcopy(k).start()
         vg[f] = vs_ref[...]
 
-        @pl.loop(0, 6)
+        @pl.loop(0, 7)
         def _(t):
             tick(t)
         for k in range(1, 8):
@@ -285,8 +285,8 @@
         cp.start()
         cp.wait()
 
-    early = (1 - l) * (s + 5) + l * (s + 17)
-    late = (1 - l) * (s + 1 + s // 11 + s // 13) + l * (s + 13)
+    early = (1 - l) * (s + 6) + l * (s + 18)
+    late = (1 - l) * (s + 2 + s // 11 + s // 13) + l * (s + 14)
 
     @pl.when((s <= 5) & (l + s > 0))
     def _():
@@ -343,7 +343,7 @@
         def _(i):
             @pl.when((i == 3) & (l == 0) & ((s == 10) | (s == 12)))
             def _():
-                tick(12 + 3 * ((s - 10) // 2))
+                tick(13 + 3 * ((s - 10) // 2))
             for q in range(3):
                 cs = slice(256 * q, 256 * q + 256)
                 u = dot(ab[i], w[pl.ds(up, D), cs]) + vec[l, pl.ds(8 + j, 1), cs]
@@ -394,7 +394,7 @@
                    S(images.shape, BF), S((rows, D), BF), S((LAYERS, 16, D), F32)],
         scratch_shapes=[pltpu.VMEM((rows, D), BF), pltpu.VMEM((n, RP, D), F32), pltpu.VMEM((n, RP, D), BF), pltpu.VMEM((n, RP, D), BF),
                         pltpu.VMEM((8, LAYERS, 16, 128), F32), pltpu.VMEM((LAYERS, 16, D), F32),
-                        pltpu.SemaphoreType.DMA((4,)), pltpu.SemaphoreType.DMA((4, 8)), pltpu.SemaphoreType.DMA((4, 8)),
+                        pltpu.SemaphoreType.DMA((8,)), pltpu.SemaphoreType.DMA((8, 8)), pltpu.SemaphoreType.DMA((8, 8)),
                         pltpu.SemaphoreType.DMA((7,)), pltpu.SemaphoreType.DMA((7,)), pltpu.SemaphoreType.DMA, pltpu.SemaphoreType.DMA],
         compiler_params=pltpu.CompilerParams(collective_id=0, has_side_effects=True, vmem_limit_bytes=62 * 2**20),
     )(images, shard, vshard)
@@ -402,7 +402,7 @@
 
 def bwd_kernel(cot_ref, w_ref, vec_ref, hs_ref, h1_ref, g_ref, e_ref, qkv_ref, a2_ref, o_ref, a1_ref,
                di_ref, gin_ref, gout_ref, gv_ref,
-               wk, d, db, dhb, do, du, ab, gb, dv, rc, s2, ra, rb, s3a, s3b, r3a, r3b, s4, rz, s5, ry, fin,
+               wk, d, db, dhb, do, du, ab, gb, dv, rc, s2, ra, rb, s3a, s3b, r3a, r3b, s4, rz, s5, ry, s6, rw, fin,
                vs, vr, vz, wsem, asem, ssem, rsem, osem, vssem, vrsem):
     lr, s = pl.program_id(0), pl.program_id(1)
     l = LAYERS - 1 - lr
@@ -411,6 +411,8 @@
     fc, fx, fy = f + 1 - 2 * core, f + 2 - 4 * x, f + 4 - 8 * y
     z1, z3 = z + 1 - 2 * (z % 2), 3 - z
     half = CH // 2
+    mine = pl.multiple_of(((z + 1) // 2 % 2) * half, 16)
+    theirs = pl.multiple_of(half - (z + 1) // 2 % 2 * half, 16)
     rows = d.shape[0] * RP
 
     def load(layer, block, n, at):
@@ -423,32 +425,30 @@
         return pltpu.make_async_remote_copy(src_ref=src, dst_ref=dst, send_sem=ssem.at[p, kind], recv_sem=rsem.at[p, kind],
                                             device_id=to, device_id_type=MESH)
 
-    def chunk(v):
-        return v - 6 * (v // 18)
-
     def live(v):
-        return ((v >= 0) & (v < 12)) | ((v >= 18) & (v < 30))
+        return (v >= 0) & (v < 24)
 
     def kind(n, v):
-        p = v % 2
+        p, q = v % 2, v % 4
         if n == 0:
-            lc = chunk(v) % NC
-            return remote(0, p, gb.at[lc - 9 * (lc // 9), :, 1 - core], rc.at[p], fsdp=fc)
+            lc = v % NC
+            return remote(0, q, gb.at[lc - 9 * (lc // 9), :, 1 - core], rc.at[p], fsdp=fc)
         if n == 1:
-            return remote(1, p, s2.at[p, :, 1 - x, pl.ds(0, half)], ra.at[p], fsdp=fx)
+            return remote(1, q, s2.at[p, :, 1 - x, pl.ds(0, half)], ra.at[q], fsdp=fx)
         if n == 2:
-            return remote(2, p, s2.at[p, 1 - y, :, pl.ds(half, half)], rb.at[p], fsdp=fy)
+            return remote(2, q, s2.at[p, 1 - y, :, pl.ds(half, half)], rb.at[q], fsdp=fy)
         if n == 3:
-            return remote(3, p, s3a.at[p, 1 - y], r3a.at[p], fsdp=fy)
+            return remote(3, q, s3a.at[p, 1 - y], r3a.at[p], fsdp=fy)
         if n == 4:
-            return remote(4, p, s3b.at[p, 1 - x], r3b.at[p], fsdp=fx)
+            return remote(4, q, s3b.at[p, 1 - x], r3b.at[p], fsdp=fx)
         if n == 5:
-            return remote(5, p, s4.at[p], rz.at[p], rep=z1)
-        return remote(6, p, s5.at[p], ry.at[p], rep=z3)
+            return remote(5, q, s4.at[p, pl.ds(theirs, half)], rz.at[q], rep=z1)
+        if n == 6:
+            return remote(6, q, s5.at[p], ry.at[q], rep=z3)
+        return remote(7, q, s6.at[p], rw.at[p], rep=z1)
 
     def put(v, act):
-        c = chunk(v)
-        lc, layer = c % NC, LAYERS - 1 - c // NC
+        lc, layer = v % NC, LAYERS - 1 - v // NC
         p = v % 2
         out = (lc >= 4) & (lc < 9)
 
@@ -466,29 +466,38 @@
         return a.astype(F32) + b.astype(F32)
 
     def tick(t):
-        @pl.when(live(t - 6))
-        def _():
-            put(t - 6, lambda a: a.wait())
-
-        @pl.when(live(t - 5))
-        def _():
-            v = t - 5
+        @pl.when(live(t - 10))
+        def _():
+            put(t - 10, lambda a: a.wait())
+
+        @pl.when(live(t - 9))
+        def _():
+            v = t - 9
+            p = v % 2
+            kind(7, v).wait()
+            fin[p, pl.ds(mine, half)] = s6[p].astype(F32)
+            fin[p, pl.ds(theirs, half)] = rw[p].astype(F32)
+            put(v, lambda a: a.start())
+
+        @pl.when(live(t - 8))
+        def _():
+            v = t - 8
             p = v % 2
             kind(6, v).wait()
-            fin[p] = add(s5[p], ry[p])
-            put(v, lambda a: a.start())
-
-        @pl.when(live(t - 4))
-        def _():
-            v = t - 4
+            s6[p] = add(s5[p], ry[v % 4]).astype(BF)
+            kind(7, v).start()
+
+        @pl.when(live(t - 6))
+        def _():
+            v = t - 6
             p = v % 2
             kind(5, v).wait()
-            s5[p] = add(s4[p], rz[p]).astype(BF)
+            s5[p] = add(s4[p, pl.ds(mine, half)], rz[v % 4]).astype(BF)
             kind(6, v).start()
 
-        @pl.when(live(t - 3))
-        def _():
-            v = t - 3
+        @pl.when(live(t - 4))
+        def _():
+            v = t - 4
             p = v % 2
             kind(3, v).wait()
             kind(4, v).wait()
@@ -496,15 +505,15 @@
             s4[p, half:CH] = add(s3b[p, x], r3b[p]).astype(BF)
             kind(5, v).start()
 
-        @pl.when(live(t - 2))
-        def _():
-            v = t - 2
-            p = v % 2
+        @pl.when(live(t - 3))
+        def _():
+            v = t - 3
+            p, q = v % 2, v % 4
             kind(1, v).wait()
             kind(2, v).wait()
             for i in range(2):
-                s3a[p, i] = add(s2[p, i, x, 0:half], ra[p, i]).astype(BF)
-                s3b[p, i] = add(s2[p, y, i, half:CH], rb[p, i]).astype(BF)
+                s3a[p, i] = add(s2[p, i, x, 0:half], ra[q, i]).astype(BF)
+                s3b[p, i] = add(s2[p, y, i, half:CH], rb[q, i]).astype(BF)
             kind(3, v).start()
             kind(4, v).start()
 
@@ -513,7 +522,7 @@
             v = t - 1
             p = v % 2
             kind(0, v).wait()
-            lc = chunk(v) % NC
+            lc = v % NC
             for i in range(4):
                 s2[p, i // 2, i % 2] = add(gb[lc - 9 * (lc // 9), i, core], rc[p, i]).astype(BF)
             kind(1, v).start()
@@ -571,12 +580,12 @@
     def _():
         load(l, 0, 3, 0).wait()
 
-    even = 1 - s % 2
-    first = (s >= 6) & (s <= 12) & (even == 1)
+    odd = s % 2
+    first = (s >= 6) & (s <= 13) & (odd == 1 - lr)
     second = (s >= 14) & (s <= 18)
-    third = (s >= 20) & ((even == 1) | (lr == 1))
-    start = (s <= 4) & (lr == 1)
-    t = jnp.where(first, 18 * lr + (s - 6) // 2, jnp.where(second, 18 * lr + s - 10, jnp.where(start, 13 + s, lr * (s + 7) + (1 - lr) * ((s - 20) // 2 + 9))))
+    third = (s >= 20) & (lr == 1)
+    start = (s <= 4) & (odd == 0) & (lr == 1)
+    t = jnp.where(first, 12 * lr + (s - 6) // 2, jnp.where(second, 12 * lr + s - 10, jnp.where(start, 9 + s // 2, s + 1)))
 
     @pl.when(first | second | third | start)
     def _():
@@ -687,7 +696,8 @@
                                                 device_id={"rep": (z + k) % 4}, device_id_type=MESH)
         for k in range(1, 8):
             vcopy(k).start()
-        tick(34)
+        for t in range(28, 34):
+            tick(jnp.int32(t))
         for k in range(1, 8):
             vcopy(k).wait()
         total = vs[f]
@@ -699,7 +709,6 @@
         for k in range(1, 4):
             zcopy(k).wait()
         gv_ref[...] = (vz[0] + vz[1]) + (vz[2] + vz[3])
-        put(29, lambda a: a.wait())
 
 
 def bwd(cotangent, w, vec, hs, h1, g, e, qkv, a2, o, a1, shard_in, shard_out):
@@ -720,10 +729,11 @@
         out_shape=[S(cotangent.shape, F32), S(shard_in, F32), S(shard_out, F32), S((LAYERS, 16, 128), F32)],
         scratch_shapes=[VB(9 * D, D), pltpu.VMEM((n, RP, D), F32), VB(n, RP, D), VB(n, RP, D), VB(n, RP, D), VB(n, RP, 4 * D), VB(2, n, RP, D),
                         VB(9, 4, 2, CH, D), pltpu.VMEM((LAYERS, 16, D), F32),
-                        VB(2, 4, CH, D), VB(2, 2, 2, CH, D), VB(2, 2, half, D), VB(2, 2, half, D), VB(2, 2, half, D), VB(2, 2, half, D),
-                        VB(2, half, D), VB(2, half, D), VB(2, CH, D), VB(2, CH, D), VB(2, CH, D), VB(2, CH, D), pltpu.VMEM((2, CH, D), F32),
+                        VB(2, 4, CH, D), VB(2, 2, 2, CH, D), VB(4, 2, half, D), VB(4, 2, half, D), VB(2, 2, half, D), VB(2, 2, half, D),
+                        VB(2, half, D), VB(2, half, D), VB(2, CH, D), VB(4, half, D), VB(2, half, D), VB(4, half, D), VB(2, half, D), VB(2, half, D),
+                        pltpu.VMEM((2, CH, D), F32),
                         pltpu.VMEM((8, LAYERS, 16, 128), F32), pltpu.VMEM((7, LAYERS, 16, 128), F32), pltpu.VMEM((4, LAYERS, 16, 128), F32),
-                        pltpu.SemaphoreType.DMA((2,)), pltpu.SemaphoreType.DMA((2,)), pltpu.SemaphoreType.DMA((2, 7)), pltpu.SemaphoreType.DMA((2, 7)),
+                        pltpu.SemaphoreType.DMA((2,)), pltpu.SemaphoreType.DMA((2,)), pltpu.SemaphoreType.DMA((4, 8)), pltpu.SemaphoreType.DMA((4, 8)),
                         pltpu.SemaphoreType.DMA((2,)), pltpu.SemaphoreType.DMA((10,)), pltpu.SemaphoreType.DMA((10,))],
         compiler_params=pltpu.CompilerParams(collective_id=1, has_side_effects=True, vmem_limit_bytes=63 * 2**20),
     )(cotangent, w, vec, hs, h1, g, e, qkv, a2, o, a1)

time: 503 us -> 419 us (0.83)
  Pallas kernels: 457 us -> 373 us
    pallas_call x1, Pallas kernels: 283 us -> 232 us  [bwd(): pl.pallas_call(bwd_kernel, grid=(LAYERS, 27), in_specs=[tok(lambda lr, s:...]
    pallas_call x1, Pallas kernels: 174 us -> 141 us  [fwd(): pl.pallas_call(fwd_kernel, grid=(LAYERS, 14), in_specs=[pl.BlockSpec(imag...]
where the time goes in v4:
time: 419 us; the launch traced here: 416 us
  Pallas kernels  373 us (89%)
  other arithmetic  22.4 us (5%)
  local copies, waits for them, and re-layouts  20 us (5%)
    pallas_call x1, Pallas kernels, bwd(): pl.pallas_call(bwd_kernel, grid=(LAYERS, 27), in_specs=[tok(lambda lr, s:...  232 us
    pallas_call x1, Pallas kernels, fwd(): pl.pallas_call(fwd_kernel, grid=(LAYERS, 14), in_specs=[pl.BlockSpec(imag...  141 us
    unnamed x29, local copies, waits for them, and re-layouts  14.8 us
    sub x3, other arithmetic, adam_update(): master - rate * (adam_move + decay_rate * master)  14.2 us

profile of v4, /device:TPU:8, one launch (start us, length us, event | category | flops | bytes accessed | tf_op | source)
XLA Modules:
  0.0 416.1 jit_solution(6278806850278833992)
XLA Ops:
  0.6 0.7 convert_element_type.14
  1.4 0.0 copy-start
  1.4 0.6 pad_convert_fusion.vs_ref
  2.0 3.4 convert_element_type.13
  5.4 0.0 copy-done
  5.4 1.5 convert_element_type.12
  6.9 4.0 reshape.44
  10.9 0.6 slice.13
  11.5 0.0 copy-start.4
  11.5 0.3 slice.12
  11.8 0.1 copy.26
  11.9 0.1 copy.27
  12.1 0.8 copy-done.4
  12.9 2.0 pad_maximum_fusion
  14.9 141.0 %shard_map.218 = (f32[2,5,208,768]{3,2,1,0:T(8,128)}, bf16[2,5,208,2304]{3,2,1,0:T(8,128)(2,1)}, bf16[2,5,208,768]{3,2,1,0:T(8,128)(2,1)}, bf16[2,5,208,768]{3,2...) custom-call(bf16[5,197,768]{2,1,0:T(8,128)(2,1)} %img_ref.1, ...), custom_call_target="tpu_custom_call" | custom-call | tf_op jit(solution)/shard_map/pallas_call | solution.py:388
  155.9 0.0 copy-start.9
  155.9 0.0 copy-start.10
  155.9 0.0 copy-start.11
  155.9 231.9 %shard_map.219 = (f32[5,197,768]{2,1,0:T(8,128)}, f32[2,96,5376]{2,1,0:T(8,128)}, f32[2,480,768]{2,1,0:T(8,128)}, f32[2,16,128]{2,1,0:T(8,128)}) custom-call(bf16[5,197,768]{2,1,0:T(8,128)(2,1)} %cot_ref.1, bf16[18432,768]{1,0:T(8,128)(2,1)} %get-tuple-element.30.w_ref, f32[2,16,768]{2,1,0:T(8,128)} %get-tuple-element.31.vec_ref, ...), custom_call_target="tpu_custom_call" | custom-call | tf_op jit(solution)/shard_map/pallas_call | solution.py:722
  387.9 0.7 slice_bitcast_fusion
  388.6 0.0 copy-done.9
  388.6 0.0 copy-done.10
  388.6 0.0 copy-done.11
  388.6 0.6 multiply_subtract_fusion.2
  389.3 0.0 copy-start.1
  389.3 0.0 copy-start.2
  389.3 0.0 copy-start.5
  389.3 0.0 copy-start.6
  389.3 8.0 %multiply_subtract_fusion.1 = (f32[2,480,768]{2,1,0:T(8,128)}, f32[2,480,768]{2,1,0:T(8,128)}, f32[2,480,768]{2,1,0:T(8,128)}) fusion(f32[2,480,768]{2,1,0:T(8,128)} %param.14, f32[2,480,768]{2,1,0:T(8,128)} %get-tuple-element.71, f32[2,480,768]{2,1,0:T(8,128)} %param.17, f32[2,480,768]{2,1,0:T(8,128)} %param.20), kind=kLoop, calls=%fused_computation.7 | loop fusion | flops 11059200 | bytes 20643840 | tf_op jit(solution)/shard_map/sub | solution.py:757
  397.3 0.4 copy-done.1
  397.6 1.6 copy-done.2
  399.2 1.2 copy-done.5
  400.4 1.2 copy-done.6
  401.5 0.0 copy-start.8
  401.5 5.6 %multiply_subtract_fusion = (f32[2,96,5376]{2,1,0:T(8,128)}, f32[2,96,5376]{2,1,0:T(8,128)}, f32[2,96,5376]{2,1,0:T(8,128)}) fusion(f32[2,96,5376]{2,1,0:T(8,128)S(1)} %copy-done.1, f32[2,96,5376]{2,1,0:T(8,128)S(1)} %copy-done.2, f32[2,96,5376]{2,1,0:T(8,128)S(1)} %copy-done.5, f32[2,96,5376]{2,1,0:T(8,128)S(1)} %copy-done.6), kind=kLoop, calls=%fused_computation.3 | loop fusion | flops 15482880 | bytes 28901376 | tf_op jit(solution)/shard_map/sub | solution.py:757
  407.1 0.0 copy-start.7
  407.1 0.0 copy-done.8
  407.1 1.1 copy.35
  408.2 1.3 copy-done.7
  409.5 1.6 copy.36
  411.2 0.0 copy-start.3
  411.2 2.1 copy.37
  413.3 1.2 copy-done.3
  414.5 1.6 copy.38
  (1 shorter events, 0.0 us)
Async XLA Ops:
  1.4 4.0 copy-start
  11.5 1.4 copy-start.4
  155.9 232.7 %copy-start.9 = (f32[2,1152]{1,0:T(2,128)S(1)}, f32[2,1152]{1,0:T(2,128)}, u32[]{:S(2)}) copy-start(f32[2,1152]{1,0:T(2,128)} %param.15) | copy-start | bytes 27652
  155.9 232.7 %copy-start.10 = (f32[2,1152]{1,0:T(2,128)S(1)}, f32[2,1152]{1,0:T(2,128)}, u32[]{:S(2)}) copy-start(f32[2,1152]{1,0:T(2,128)} %param.18) | copy-start | bytes 27652
  155.9 232.7 %copy-start.11 = (f32[2,1152]{1,0:T(2,128)S(1)}, f32[2,1152]{1,0:T(2,128)}, u32[]{:S(2)}) copy-start(f32[2,1152]{1,0:T(2,128)} %param.21) | copy-start | bytes 27652
  389.3 8.4 %copy-start.1 = (f32[2,96,5376]{2,1,0:T(8,128)S(1)}, f32[2,96,5376]{2,1,0:T(8,128)}, u32[]{:S(2)}) copy-start(f32[2,96,5376]{2,1,0:T(8,128)} %param.13) | copy-start | bytes 12386308
  389.3 9.9 %copy-start.2 = (f32[2,96,5376]{2,1,0:T(8,128)S(1)}, f32[2,96,5376]{2,1,0:T(8,128)}, u32[]{:S(2)}) copy-start(f32[2,96,5376]{2,1,0:T(8,128)} %get-tuple-element.70) | copy-start | bytes 12386308
  389.3 11.1 %copy-start.5 = (f32[2,96,5376]{2,1,0:T(8,128)S(1)}, f32[2,96,5376]{2,1,0:T(8,128)}, u32[]{:S(2)}) copy-start(f32[2,96,5376]{2,1,0:T(8,128)} %param.16) | copy-start | bytes 12386308
  389.3 12.3 %copy-start.6 = (f32[2,96,5376]{2,1,0:T(8,128)S(1)}, f32[2,96,5376]{2,1,0:T(8,128)}, u32[]{:S(2)}) copy-start(f32[2,96,5376]{2,1,0:T(8,128)} %param.19) | copy-start | bytes 12386308
  401.5 5.6 %copy-start.8 = (bf16[5,197,768]{2,1,0:T(8,128)(2,1)S(1)}, bf16[5,197,768]{2,1,0:T(8,128)(2,1)}, u32[]{:S(2)}) copy-start(bf16[5,197,768]{2,1,0:T(8,128)(2,1)} %get-tuple-element.68) | copy-start | bytes 4538884
  407.1 2.4 copy-start.7
  411.2 3.3 copy-start.3

commit v5 on v4

--- a/solution.py
+++ b/solution.py
@@ -16,43 +16,42 @@
     var=jnp.mean(xc*xc,axis=-1,keepdims=True)
     return xc, lax.rsqrt(var+EPS)
 
-def attn_fwd(q,k,v):
-    lane=lax.broadcasted_iota(jnp.int32,(1,128),1)
-    col=lax.broadcasted_iota(jnp.int32,(1,RP),1)
-    os=[]
-    for half in range(2):
-        m=jnp.where((lane<64) if half==0 else (lane>=64),0.125,0.0).astype(BF)
-        s=dot_t(q*m,k)
-        s=jnp.where(col<SEQ,s,-1e30)
-        mx=jnp.max(s,axis=-1,keepdims=True)
-        e=jnp.exp(s-mx)
-        p=(e*(1.0/jnp.sum(e,axis=-1,keepdims=True))).astype(BF)
-        os.append(dot(p,v))
-    return jnp.where(lane<64,os[0],os[1]).astype(BF)
-
-def attn_bwd(q,k,v,do):
-    lane=lax.broadcasted_iota(jnp.int32,(1,128),1)
-    row=lax.broadcasted_iota(jnp.int32,(RP,1),0)
-    r=[]
-    for half in range(2):
-        sel=(lane<64) if half==0 else (lane>=64)
-        m=jnp.where(sel,0.125,0.0).astype(BF)
-        m1=jnp.where(sel,1.0,0.0).astype(BF)
-        qs=q*m
-        s=dot_t(k,qs)
-        s=jnp.where(row<SEQ,s,-1e30)
-        mx=jnp.max(s,axis=0,keepdims=True)
-        e=jnp.exp(s-mx)
-        p=e*(1.0/jnp.sum(e,axis=0,keepdims=True))
-        pb=p.astype(BF)
-        dp=dot_t(v,do*m1)
-        dl=jnp.sum(p*dp,axis=0,keepdims=True)
-        ds=(p*(dp-dl)).astype(BF)
-        dv=dot(pb,do)
-        dk=dot(ds,qs)
-        dq=dot_0(ds,k)*0.125
-        r.append((dq,dk,dv))
-    return tuple(jnp.where(lane<64,a,b) for a,b in zip(*r))
+def head_masks(scale):
+    lane = lax.broadcasted_iota(jnp.int32, (1, 128), 1)
+    return jnp.where(lane < 64, scale, 0.0).astype(BF), jnp.where(lane < 64, 0.0, scale).astype(BF)
+
+
+def weights_t(q, k, masks):
+    row = lax.broadcasted_iota(jnp.int32, (RP, 1), 0)
+    s = [jnp.where(row < SEQ, dot_t(k, q * m), -1e30) for m in masks]
+    e = [jnp.exp(x - jnp.max(x, axis=0, keepdims=True)) for x in s]
+    return [x * (1.0 / jnp.sum(x, axis=0, keepdims=True)) for x in e]
+
+
+def attn_fwd(q, k, v):
+    ones = head_masks(1.0)
+    row = lax.broadcasted_iota(jnp.int32, (16, 1), 0)
+    ps = []
+    for m in head_masks(0.125):
+        s = dot_t(k, q * m)
+        s = jnp.concatenate([s[:RP - 16], jnp.where(row < SEQ - RP + 16, s[RP - 16:], -1e30)], axis=0)
+        e = jnp.exp(s - jnp.max(s, axis=0, keepdims=True))
+        ps.append((e * (1.0 / jnp.sum(e, axis=0, keepdims=True))).astype(BF))
+    return (dot_0(ps[0], v * ones[0]) + dot_0(ps[1], v * ones[1])).astype(BF)
+
+
+def attn_bwd(q, k, v, do):
+    scaled, ones = head_masks(0.125), head_masks(1.0)
+    p = weights_t(q, k, scaled)
+    dos = [do * m for m in ones]
+    dp = [dot_t(v, x) for x in dos]
+    pb = [x.astype(BF) for x in p]
+    ds = [(a * (b - jnp.sum(a * b, axis=0, keepdims=True))).astype(BF) for a, b in zip(p, dp)]
+    dv = dot(pb[0], dos[0]) + dot(pb[1], dos[1])
+    dk = dot(ds[0], q * scaled[0]) + dot(ds[1], q * scaled[1])
+    dq = dot_0(ds[0], k * scaled[0]) + dot_0(ds[1], k * scaled[1])
+    return dq, dk, dv
+
 
 def ka_kernel(h_ref,w_ref,vec_ref,qkv_ref,o_ref,a_ref):
     h=h_ref[0].astype(F32)
@@ -204,8 +203,8 @@
                           + mid * (7 * D + 5 * CH * f + CH * (j - 3)), 16)
 
 
-def fwd_kernel(img_ref, ws_ref, vs_ref, hs_ref, qkv_ref, a1_ref, o_ref, h1_ref, a2_ref, e_ref, g_ref, enc_ref, wo_ref, vo_ref,
-               w, hb, ob, ab, vg, vec, lsem, ssem, rsem, vssem, vrsem, osem, vosem):
+def fwd_kernel(img_ref, win_ref, wout_ref, vs_ref, hs_ref, qkv_ref, a1_ref, o_ref, h1_ref, a2_ref, e_ref, g_ref, enc_ref, wo_ref, vo_ref,
+               w, hb, ob, ab, vg, vec, st, lsem, ssem, rsem, vssem, vrsem, osem, vosem):
     l, s = pl.program_id(0), pl.program_id(1)
     f, core, x, y = plane()
     fc, fx, fy = f + 1 - 2 * core, f + 2 - 4 * x, f + 4 - 8 * y
@@ -218,13 +217,25 @@
         return pltpu.make_async_remote_copy(src_ref=src, dst_ref=dst, send_sem=ssem.at[c % 8, kind], recv_sem=rsem.at[c % 8, kind],
                                             device_id={"fsdp": to}, device_id_type=MESH)
 
+    def fetch(c, act):
+        layer, j = c // NC, c % NC
+        mid = (j >= 3) & (j < 8)
+
+        @pl.when(mid)
+        def _():
+            act(pltpu.make_async_copy(wout_ref.at[layer, pl.ds(pl.multiple_of((j - 3) * CH, 8), CH)], st.at[c % 4], lsem.at[c % 4]))
+
+        @pl.when(jnp.logical_not(mid))
+        def _():
+            act(pltpu.make_async_copy(win_ref.at[layer, :, pl.ds(pl.multiple_of((j - 5 * (j // 8)) * D, 128), D)], st.at[c % 4], lsem.at[c % 4]))
+
     def kinds(c):
-        own, mine, half = ws_ref.at[c], wrow(c, f), CH // 2
-        return [lambda: send(c, 0, own, mine, fx), lambda: send(c, 1, own, mine, fy), lambda: send(c, 2, own, mine, fc),
+        mine, half = wrow(c, f), CH // 2
+        return [lambda: send(c, 0, mine, mine, fx), lambda: send(c, 1, mine, mine, fy), lambda: send(c, 2, mine, mine, fc),
                 lambda: send(c, 3, wrow(c, fx, 0, half), wrow(c, fx, 0, half), fy),
                 lambda: send(c, 4, wrow(c, fy, half, half), wrow(c, fy, half, half), fx),
                 lambda: send(c, 5, wrow(c, fx), wrow(c, fx), fc), lambda: send(c, 6, wrow(c, fy), wrow(c, fy), fc),
-                lambda: send(c, 7, wrow(c, fd), wrow(c, fd), fc), lambda: pltpu.make_async_copy(own, mine, lsem.at[c % 8])]
+                lambda: send(c, 7, wrow(c, fd), wrow(c, fd), fc)]
 
     def start(c, which):
         k = kinds(c)
@@ -239,7 +250,7 @@
     def tick(t):
         @pl.when((t >= 4) & (t < 28))
         def _():
-            wait(t - 4, (2, 5, 6, 7, 8))
+            wait(t - 4, (2, 5, 6, 7))
 
         @pl.when((t >= 3) & (t < 27))
         def _():
@@ -253,13 +264,21 @@
 
         @pl.when(t < 24)
         def _():
-            start(t, (0, 1, 2, 8))
+            fetch(t, lambda a: a.wait())
+            w[pl.ds(chunk_rows(t, f), CH)] = st[t % 4].astype(BF)
+            start(t, (0, 1, 2))
+
+        @pl.when(t < 21)
+        def _():
+            fetch(t + 3, lambda a: a.start())
 
     def out_copy(b, n):
         return pltpu.make_async_copy(w.at[pl.ds(b, n)], wo_ref.at[pl.ds(b, n)], osem)
 
     @pl.when((l == 0) & (s == 0))
     def _():
+        for c in range(3):
+            fetch(jnp.int32(c), lambda a: a.start())
         bar = pltpu.get_barrier_semaphore()
         for k in range(1, 8):
             pl.semaphore_signal(bar, inc=1, device_id={"fsdp": (f + k) % 8}, device_id_type=MESH)
@@ -286,7 +305,12 @@
         cp.wait()
 
     early = (1 - l) * (s + 6) + l * (s + 18)
-    late = (1 - l) * (s + 2 + s // 11 + s // 13) + l * (s + 14)
+    late = (1 - l) * (s + 2) + l * (s + 14)
+
+    @pl.when((s == 0) & (l == 1))
+    def _():
+        tick(16)
+        tick(17)
 
     @pl.when((s <= 5) & (l + s > 0))
     def _():
@@ -339,21 +363,21 @@
         up = pl.multiple_of((l * NC + 3 + j) * D, 16)
         down = pl.multiple_of((l * NC + 8 + j) * D, 16)
 
-        @pl.loop(0, 5)
-        def _(i):
-            @pl.when((i == 3) & (l == 0) & ((s == 10) | (s == 12)))
-            def _():
-                tick(13 + 3 * ((s - 10) // 2))
-            for q in range(3):
-                cs = slice(256 * q, 256 * q + 256)
-                u = dot(ab[i], w[pl.ds(up, D), cs]) + vec[l, pl.ds(8 + j, 1), cs]
-                e, g = gelu_parts(u)
-                e_ref[0, i, :, cs] = e.astype(BF)
-                g_ref[0, i, :, cs] = g.astype(BF)
-                hb[i] += dot(e_ref[0, i, :, cs], w[pl.ds(pl.multiple_of(down + 256 * q, 16), 256), :])
-
-            @pl.when((l == 1) & (s == 13))
-            def _():
+        bias = vec[l, pl.ds(8 + j, 1), :]
+        n = hb.shape[0]
+        u = dot(ab[0], w[pl.ds(up, D), :])
+        for i in range(n):
+            later = dot(ab[i + 1], w[pl.ds(up, D), :]) if i < n - 1 else None
+            e, g = gelu_parts(u + bias)
+            e = e.astype(BF)
+            e_ref[0, i] = e
+            g_ref[0, i] = g.astype(BF)
+            hb[i] += dot(e, w[pl.ds(down, D), :])
+            u = later
+
+        @pl.when((l == 1) & (s == 13))
+        def _():
+            for i in range(n):
                 enc_ref[i] = hb[i, 0:SEQ, :].astype(BF)
 
     for layer in range(LAYERS):
@@ -377,7 +401,7 @@
         pltpu.make_async_copy(w, wo_ref, osem).wait()
 
 
-def fwd(images, shard, vshard):
+def fwd(images, weight_in, weight_out, vshard):
     n = images.shape[0]
     S = jax.ShapeDtypeStruct
     one = lambda cols: pl.BlockSpec((1, 1, RP, cols), lambda l, s: (l, jnp.minimum(s, 4), 0, 0))
@@ -387,22 +411,22 @@
     rows = LAYERS * NC * D
     return pl.pallas_call(
         fwd_kernel, grid=(LAYERS, 14),
-        in_specs=[pl.BlockSpec(images.shape, lambda l, s: (0, 0, 0)), anyw, pl.BlockSpec(vshard.shape, lambda l, s: (0, 0, 0))],
+        in_specs=[pl.BlockSpec(images.shape, lambda l, s: (0, 0, 0)), anyw, anyw, pl.BlockSpec(vshard.shape, lambda l, s: (0, 0, 0))],
         out_specs=[one(D), one(3 * D), one(D), one(D), two(D), two(D), wide, wide, pl.BlockSpec(images.shape, lambda l, s: (0, 0, 0)), anyw, anyw],
         out_shape=[S((LAYERS, n, RP, D), F32), S((LAYERS, n, RP, 3 * D), BF), S((LAYERS, n, RP, D), BF), S((LAYERS, n, RP, D), BF),
                    S((LAYERS, n, RP, D), F32), S((LAYERS, n, RP, D), BF), S((LAYERS, n, RP, 4 * D), BF), S((LAYERS, n, RP, 4 * D), BF),
                    S(images.shape, BF), S((rows, D), BF), S((LAYERS, 16, D), F32)],
         scratch_shapes=[pltpu.VMEM((rows, D), BF), pltpu.VMEM((n, RP, D), F32), pltpu.VMEM((n, RP, D), BF), pltpu.VMEM((n, RP, D), BF),
-                        pltpu.VMEM((8, LAYERS, 16, 128), F32), pltpu.VMEM((LAYERS, 16, D), F32),
-                        pltpu.SemaphoreType.DMA((8,)), pltpu.SemaphoreType.DMA((8, 8)), pltpu.SemaphoreType.DMA((8, 8)),
+                        pltpu.VMEM((8, LAYERS, 16, 128), F32), pltpu.VMEM((LAYERS, 16, D), F32), pltpu.VMEM((4, CH, D), F32),
+                        pltpu.SemaphoreType.DMA((4,)), pltpu.SemaphoreType.DMA((8, 8)), pltpu.SemaphoreType.DMA((8, 8)),
                         pltpu.SemaphoreType.DMA((7,)), pltpu.SemaphoreType.DMA((7,)), pltpu.SemaphoreType.DMA, pltpu.SemaphoreType.DMA],
         compiler_params=pltpu.CompilerParams(collective_id=0, has_side_effects=True, vmem_limit_bytes=62 * 2**20),
-    )(images, shard, vshard)
+    )(images, weight_in, weight_out, vshard)
 
 
 def bwd_kernel(cot_ref, w_ref, vec_ref, hs_ref, h1_ref, g_ref, e_ref, qkv_ref, a2_ref, o_ref, a1_ref,
                di_ref, gin_ref, gout_ref, gv_ref,
-               wk, d, db, dhb, do, du, ab, gb, dv, rc, s2, ra, rb, s3a, s3b, r3a, r3b, s4, rz, s5, ry, s6, rw, fin,
+               wk, d, acc, db, dhb, du, ab, gb, dv, rc, s2, ra, rb, s3a, s3b, r3a, r3b, s4, rz, s5, ry, s6, rw, fin,
                vs, vr, vz, wsem, asem, ssem, rsem, osem, vssem, vrsem):
     lr, s = pl.program_id(0), pl.program_id(1)
     l = LAYERS - 1 - lr
@@ -413,13 +437,14 @@
     half = CH // 2
     mine = pl.multiple_of(((z + 1) // 2 % 2) * half, 16)
     theirs = pl.multiple_of(half - (z + 1) // 2 % 2 * half, 16)
-    rows = d.shape[0] * RP
+    n = d.shape[0]
+    rows = n * RP
 
     def load(layer, block, n, at):
         return pltpu.make_async_copy(w_ref.at[pl.ds(pl.multiple_of((layer * NC + block) * D, 16), n * D)], wk.at[pl.ds(at * D, n * D)], wsem.at[0 if at else 1])
 
-    def fetch(src, slot):
-        return pltpu.make_async_copy(src.at[l], ab.at[slot], asem.at[slot])
+    def fetch(src, slot, layer):
+        return pltpu.make_async_copy(src.at[layer], ab.at[slot], asem.at[slot])
 
     def remote(kind, p, src, dst, **to):
         return pltpu.make_async_remote_copy(src_ref=src, dst_ref=dst, send_sem=ssem.at[p, kind], recv_sem=rsem.at[p, kind],
@@ -463,7 +488,7 @@
             act(pltpu.make_async_copy(fin.at[p], gin_ref.at[layer, :, pl.ds(pl.multiple_of(j * D, 128), D)], osem.at[p]))
 
     def add(a, b):
-        return a.astype(F32) + b.astype(F32)
+        return a + b
 
     def tick(t):
         @pl.when(live(t - 10))
@@ -542,83 +567,96 @@
             pl.semaphore_signal(bar, inc=1, device_id={"rep": (z + k) % 4}, device_id_type=MESH)
         pl.semaphore_wait(bar, 10)
         dv[...] = jnp.zeros_like(dv)
+        fetch(a2_ref, 0, l).start()
+        for i in range(n):
+            d[i] = jnp.zeros((RP, D), F32)
+            d[i, 0:SEQ, :] = cot_ref[i].astype(F32)
         load(l, 3, 9, 0).wait()
 
     @pl.when((lr == 1) & (s == 0))
     def _():
-        load(l, 3, 3, 0).start()
         load(l, 3, 3, 0).wait()
         load(l, 6, 6, 3).wait()
 
     @pl.when(s == 0)
     def _():
-        fetch(a2_ref, 0).start()
-        fetch(o_ref, 1).start()
-
-    @pl.when(s == 5)
-    def _():
-        fetch(a2_ref, 0).wait()
+        fetch(o_ref, 1, l).start()
+
+    @pl.when(s == 1)
+    def _():
+        fetch(a2_ref, 0, l).wait()
+
+    @pl.when(s == 8)
+    def _():
+        fetch(a1_ref, 0, l).start()
+
+    @pl.when(s == 13)
+    def _():
+        fetch(o_ref, 1, l).wait()
         load(l, 0, 3, 0).start()
 
         @pl.when(lr == 0)
         def _():
             load(l - 1, 6, 6, 3).start()
 
-    @pl.when(s == 9)
-    def _():
-        fetch(o_ref, 1).wait()
-
-    @pl.when(s == 10)
-    def _():
-        fetch(a1_ref, 0).start()
-
-    @pl.when(s == 19)
-    def _():
-        fetch(a1_ref, 0).wait()
-
-    @pl.when(s == 22)
+    @pl.when(s == 23)
+    def _():
+        fetch(a1_ref, 0, l).wait()
+
+    @pl.when(s == 26)
     def _():
         load(l, 0, 3, 0).wait()
 
-    odd = s % 2
-    first = (s >= 6) & (s <= 13) & (odd == 1 - lr)
-    second = (s >= 14) & (s <= 18)
-    third = (s >= 20) & (lr == 1)
-    start = (s <= 4) & (odd == 0) & (lr == 1)
-    t = jnp.where(first, 12 * lr + (s - 6) // 2, jnp.where(second, 12 * lr + s - 10, jnp.where(start, 9 + s // 2, s + 1)))
-
-    @pl.when(first | second | third | start)
+    @pl.when((s == 27) & (lr == 0))
+    def _():
+        fetch(a2_ref, 0, l - 1).start()
+        load(l - 1, 3, 3, 0).start()
+
+    one = (s >= 2) & (s <= 8) & (s % 2 == 0)
+    two = (s >= 18) & (s <= 22) & (s != 20)
+    three = s == 24
+    four = (lr == 0) & ((s == 26) | (s == 28))
+    five = (lr == 1) & (s >= 25)
+    six = (lr == 1) & (s == 0)
+    back = s - 18
+    t = jnp.where(one, 12 * lr + s // 2 - 1, jnp.where(two, 12 * lr + 4 + back - back // 3, jnp.where(three, 12 * lr + 8, jnp.where(
+        four, 9 + (s - 26) // 2, jnp.where(five, s - 4, 11)))))
+
+    @pl.when(one | two | three | four | five | six)
     def _():
         tick(t)
 
-    @pl.when(s < 5)
-    def _():
-        i = s
-
-        @pl.when(lr == 0)
-        def _():
-            d[i] = jnp.zeros((RP, D), F32)
-            d[i, 0:SEQ, :] = cot_ref[0].astype(F32)
-        up = d[i]
-        db[i] = up.astype(BF)
-        dv[l, 7:8] += rsum(up)
-        acc = None
-        for j in range(12):
-            cs = slice(256 * j, 256 * j + 256)
-            r = (5 * D + 256 * j)
-            t1 = dot_t(db[i], wk[r:r + 256, :]) * g_ref[0, 0, :, cs].astype(F32)
-            dv[l, 8 + j // 3:9 + j // 3, 256 * (j % 3):256 * (j % 3) + 256] += rsum(t1)
-            du[i, :, cs] = t1.astype(BF)
-            t2 = dot_t(du[i, :, cs], wk[(j // 3) * D:(j // 3) * D + D, 256 * (j % 3):256 * (j % 3) + 256])
-            acc = t2 if acc is None else acc + t2
-        dx, dg, dc = norm_back(h1_ref[0, 0], vec_ref[l, 5:6], acc)
+    @pl.when(s == 0)
+    def _():
+        for i in range(n):
+            up = d[i]
+            db[i] = up.astype(BF)
+            acc[i] = jnp.zeros((RP, D), F32)
+            dv[l, 7:8] += rsum(up)
+
+    @pl.when((s < 8) & (s % 2 == 0))
+    def _():
+        j = s // 2
+        whole = db[...].reshape(rows, D)
+        cols = pl.multiple_of(j * D, 128)
+        for q in range(3):
+            t1 = dot_t(whole, wk[pl.ds(pl.multiple_of((5 + j) * D + 256 * q, 16), 256), :])
+            t1 = t1 * g_ref[0, :, :, 256 * q:256 * q + 256].reshape(rows, 256).astype(F32)
+            dv[l, pl.ds(8 + j, 1), 256 * q:256 * q + 256] += rsum(t1)
+            du[:, :, pl.ds(pl.multiple_of(cols + 256 * q, 128), 256)] = t1.astype(BF).reshape(n, RP, 256)
+        acc[...] += dot_t(du[:, :, pl.ds(cols, D)].reshape(rows, D), wk[pl.ds(pl.multiple_of(j * D, 16), D), :]).reshape(n, RP, D)
+
+    @pl.when((s >= 8) & (s < 13))
+    def _():
+        i = s - 8
+        dx, dg, dc = norm_back(h1_ref[0, 0], vec_ref[l, 5:6], acc[i])
         dv[l, 5:6] += dg
         dv[l, 6:7] += dc
         dh1 = d[i] + dx
         d[i] = dh1
         dv[l, 4:5] += rsum(dh1)
         dhb[i] = dh1.astype(BF)
-        do[i] = dot_t(dhb[i], wk[4 * D:5 * D, :]).astype(BF)
+        du[i, :, 3 * D:4 * D] = dot_t(dhb[i], wk[4 * D:5 * D, :]).astype(BF)
 
     def grad(lhs, rhs, store):
         for m in range(2):
@@ -640,47 +678,52 @@
                 gb[4 + b % 5, b // 10, (b // 5) % 2] = r[q]
         grad(lhs, rhs[...].reshape(rows, D), store)
 
-    @pl.when((s >= 5) & (s < 9))
-    def _():
-        inner(s - 5, s - 5)
-
-    @pl.when(s == 9)
+    @pl.when((s < 8) & (s % 2 == 1))
+    def _():
+        inner(s // 2, s // 2)
+
+    @pl.when(s == 13)
     def _():
         outer(0, lambda m: ab[1, :, :, m:m + 384].reshape(rows, 384), dhb)
 
-    @pl.when((s >= 10) & (s < 14))
-    def _():
-        outer(s - 9, lambda m: e_ref[0, :, :, m:m + 384].reshape(rows, 384), db)
-
-    @pl.when((s >= 14) & (s < 19))
-    def _():
-        i = s - 14
+    @pl.when((s >= 14) & (s < 18))
+    def _():
+        outer(s - 13, lambda m: e_ref[0, :, :, m:m + 384].reshape(rows, 384), db)
+
+    @pl.when((s >= 18) & (s < 23))
+    def _():
+        i = s - 18
         for p in range(6):
             b = 128 * p
             dq, dk, dvv = attn_bwd(qkv_ref[0, 0, :, b:b + 128], qkv_ref[0, 0, :, D + b:D + b + 128], qkv_ref[0, 0, :, 2 * D + b:2 * D + b + 128],
-                                   do[i, :, b:b + 128])
+                                   du[i, :, 3 * D + b:3 * D + b + 128])
             dv[l, 2:3, b:b + 128] += rsum(dq)
             dv[l, 3:4, b:b + 128] += rsum(dvv)
             du[i, :, b:b + 128] = dq.astype(BF)
             du[i, :, D + b:D + b + 128] = dk.astype(BF)
             du[i, :, 2 * D + b:2 * D + b + 128] = dvv.astype(BF)
 
-    @pl.when((s >= 19) & (s < 22))
-    def _():
-        inner(s - 19, s - 19)
-
-    @pl.when(s >= 22)
-    def _():
-        i = s - 22
-        da = dot_t(du[i, :, 0:D], wk[0:D, :]) + dot_t(du[i, :, D:2 * D], wk[D:2 * D, :]) + dot_t(du[i, :, 2 * D:3 * D], wk[2 * D:3 * D, :])
-        dx, dg, dc = norm_back(hs_ref[0, 0], vec_ref[l, 0:1], da)
+    @pl.when((s >= 23) & (s < 26))
+    def _():
+        inner(s - 23, s - 23)
+
+    @pl.when(s == 26)
+    def _():
+        acc[...] = dot_t(du[:, :, 0:D].reshape(rows, D), wk[0:D, :]).reshape(n, RP, D)
+        acc[...] += dot_t(du[:, :, D:2 * D].reshape(rows, D), wk[D:2 * D, :]).reshape(n, RP, D)
+        acc[...] += dot_t(du[:, :, 2 * D:3 * D].reshape(rows, D), wk[2 * D:3 * D, :]).reshape(n, RP, D)
+
+    @pl.when(s >= 27)
+    def _():
+        i = s - 27
+        dx, dg, dc = norm_back(hs_ref[0, 0], vec_ref[l, 0:1], acc[i])
         dv[l, 0:1] += dg
         dv[l, 1:2] += dc
         dh = d[i] + dx
         d[i] = dh
         di_ref[0] = dh[0:SEQ]
 
-    @pl.when((lr == 1) & (s == 26))
+    @pl.when((lr == 1) & (s == 31))
     def _():
         for layer in range(LAYERS):
             for c in range(72):
@@ -720,14 +763,14 @@
     VB = lambda *shape: pltpu.VMEM(shape, BF)
     half = CH // 2
     return pl.pallas_call(
-        bwd_kernel, grid=(LAYERS, 27),
-        in_specs=[tok(lambda lr, s: (jnp.minimum(s + 4 * lr, 4), 0, 0)), anyw, pl.BlockSpec(vec.shape, lambda lr, s: (0, 0, 0)),
-                  row(D, 22), row(D, 0), row(4 * D, 0),
-                  pl.BlockSpec((1, n, RP, D), lambda lr, s: (LAYERS - 1 - lr, 0, 0, jnp.clip(s - 10, 0, 3))),
-                  row(3 * D, 14), anyw, anyw, anyw],
-        out_specs=[tok(lambda lr, s: (lr * jnp.clip(s - 22, 0, 4), 0, 0)), anyw, anyw, pl.BlockSpec((LAYERS, 16, 128), lambda lr, s: (0, 0, 0))],
+        bwd_kernel, grid=(LAYERS, 32),
+        in_specs=[pl.BlockSpec(cotangent.shape, lambda lr, s: (0, 0, 0), pipeline_mode=pl.Buffered(1)), anyw, pl.BlockSpec(vec.shape, lambda lr, s: (0, 0, 0)),
+                  row(D, 27), row(D, 8), pl.BlockSpec((1, n, RP, D), lambda lr, s: (LAYERS - 1 - lr, 0, 0, jnp.minimum(s // 2, 3))),
+                  pl.BlockSpec((1, n, RP, D), lambda lr, s: (LAYERS - 1 - lr, 0, 0, jnp.clip(s - 14, 0, 3))),
+                  row(3 * D, 18), anyw, anyw, anyw],
+        out_specs=[tok(lambda lr, s: (lr * jnp.clip(s - 27, 0, 4), 0, 0)), anyw, anyw, pl.BlockSpec((LAYERS, 16, 128), lambda lr, s: (0, 0, 0))],
         out_shape=[S(cotangent.shape, F32), S(shard_in, F32), S(shard_out, F32), S((LAYERS, 16, 128), F32)],
-        scratch_shapes=[VB(9 * D, D), pltpu.VMEM((n, RP, D), F32), VB(n, RP, D), VB(n, RP, D), VB(n, RP, D), VB(n, RP, 4 * D), VB(2, n, RP, D),
+        scratch_shapes=[VB(9 * D, D), pltpu.VMEM((n, RP, D), F32), pltpu.VMEM((n, RP, D), F32), VB(n, RP, D), VB(n, RP, D), VB(n, RP, 4 * D), VB(2, n, RP, D),
                         VB(9, 4, 2, CH, D), pltpu.VMEM((LAYERS, 16, D), F32),
                         VB(2, 4, CH, D), VB(2, 2, 2, CH, D), VB(4, 2, half, D), VB(4, 2, half, D), VB(2, 2, half, D), VB(2, 2, half, D),
                         VB(2, half, D), VB(2, half, D), VB(2, CH, D), VB(4, half, D), VB(2, half, D), VB(4, half, D), VB(2, half, D), VB(2, half, D),
@@ -755,6 +798,47 @@
     corr_two = 1.0 - beta_two**STEP
     adam_move = moment_one / corr_one / (jnp.sqrt(moment_two / corr_two) + adam_eps)
     return (master - rate * (adam_move + decay_rate * master), moment_one, moment_two)
+
+
+def adam_kernel(g_ref, w_ref, m_ref, v_ref, go_ref, wo_ref, mo_ref, vo_ref, enc_ref, dim_ref,
+                g_out, w_out, m_out, v_out, go_out, wo_out, mo_out, vo_out, enc_out, dim_out, steps):
+    i = pl.program_id(0)
+
+    def update(g, w, m, v, outs):
+        grad = g[...]
+        new, moment, square = adam_update(w[...], grad, m[...], v[...], matrix_rate, matrix_decay)
+        outs[0][...], outs[1][...], outs[2][...], outs[3][...] = grad, new, moment, square
+
+    @pl.when(i < steps)
+    def _():
+        update(g_ref, w_ref, m_ref, v_ref, (g_out, w_out, m_out, v_out))
+
+    @pl.when(i >= steps)
+    def _():
+        update(go_ref, wo_ref, mo_ref, vo_ref, (go_out, wo_out, mo_out, vo_out))
+
+    @pl.when(i < enc_steps)
+    def _():
+        enc_out[...] = enc_ref[...]
+        dim_out[...] = dim_ref[...]
+
+
+enc_steps = 5
+
+
+def adam_all(ins, outs, encoded, dimg):
+    a, b = ins[0].shape, outs[0].shape
+    steps = 3 * LAYERS
+    first = pl.BlockSpec((1, a[1], a[2] // 3), lambda i: (jnp.minimum(i, steps - 1) // 3, 0, jnp.minimum(i, steps - 1) % 3))
+    second = pl.BlockSpec((1, b[1] // 3, b[2]), lambda i: (jnp.maximum(i - steps, 0) // 3, jnp.maximum(i - steps, 0) % 3, 0))
+    tok = pl.BlockSpec((1,) + encoded.shape[1:], lambda i: (jnp.minimum(i, enc_steps - 1), 0, 0))
+    S = jax.ShapeDtypeStruct
+    return pl.pallas_call(
+        functools.partial(adam_kernel, steps=steps), grid=(2 * steps,),
+        in_specs=[first] * 4 + [second] * 4 + [tok] * 2, out_specs=[first] * 4 + [second] * 4 + [tok] * 2,
+        out_shape=[S(a, F32)] * 4 + [S(b, F32)] * 4 + [S(encoded.shape, BF), S(dimg.shape, F32)],
+        compiler_params=PAR,
+    )(*ins, *outs, encoded, dimg)
 
 
 def swap(x, axis, size, mask):
@@ -794,15 +878,9 @@
     return y
 
 
-def own_shard(weight_in, weight_out):
-    a = weight_in.astype(BF).reshape(LAYERS, CH, 7, D).transpose(0, 2, 1, 3)
-    b = weight_out.astype(BF).reshape(LAYERS, 5, CH, D)
-    return jnp.concatenate([a[:, :3], b, a[:, 3:]], axis=1).reshape(LAYERS * NC, CH, D)
-
-
 def fused_step(images, cotangent, weight_in, weight_out, vector_params):
     vs = jnp.pad(vector_params.astype(BF).astype(F32).reshape(LAYERS, 9, 128), ((0, 0), (0, 7), (0, 0)))
-    hs, qkv, a1, o, h1, a2, e, g, encoded, w, vec = fwd(images, own_shard(weight_in, weight_out), vs)
+    hs, qkv, a1, o, h1, a2, e, g, encoded, w, vec = fwd(images, weight_in, weight_out, vs)
     dimg, gi, go, gv = bwd(cotangent, w, vec, hs, h1, g, e, qkv, a2, o, a1, weight_in.shape, weight_out.shape)
     return encoded, dimg, gi, go, gv[:, :9].reshape(vector_params.shape)
 
@@ -846,10 +924,12 @@
     def shards(images, cotangent, weight_in, weight_out, vector_params, first_in, first_out, first_vec, second_in, second_out, second_vec):
         if nf == 8 and nr == 4:
             encoded, d, gi, go, gv = fused_step(images, cotangent, weight_in, weight_out, vector_params)
+            gi, new_in, moment_in, square_in, go, new_out, moment_out, square_out, encoded, d = adam_all(
+                (gi, weight_in, first_in, second_in), (go, weight_out, first_out, second_out), encoded, d)
         else:
             encoded, d, gi, go, gv = plain_step(nf, nr, images, cotangent, weight_in, weight_out, vector_params)
-        new_in, moment_in, square_in = adam_update(weight_in, gi, first_in, second_in, matrix_rate, matrix_decay)
-        new_out, moment_out, square_out = adam_update(weight_out, go, first_out, second_out, matrix_rate, matrix_decay)
+            new_in, moment_in, square_in = adam_update(weight_in, gi, first_in, second_in, matrix_rate, matrix_decay)
+            new_out, moment_out, square_out = adam_update(weight_out, go, first_out, second_out, matrix_rate, matrix_decay)
         new_vec, moment_vec, square_vec = adam_update(vector_params, gv, first_vec, second_vec, vector_rate, 0.0)
         return (encoded, d, gi, go, gv, new_in, new_out, new_vec, moment_in, moment_out, moment_vec, square_in, square_out, square_vec)
 

time: 419 us -> 379 us (0.905)
  other arithmetic: 22.4 us -> 1.97 us
  local copies, waits for them, and re-layouts: 20 us -> 0.76 us
    unnamed x29 -> x7, local copies, waits for them, and re-layouts: 14.8 us -> 0.74 us
    sub x3 -> x1, other arithmetic: 14.2 us -> 0.65 us  [adam_update(): master - rate * (adam_move + decay_rate * master)]
    pallas_call x1, Pallas kernels: 141 us -> 136 us  [fwd(): pl.pallas_call(fwd_kernel, grid=(LAYERS, 14), in_specs=[pl.BlockSpec(imag...]
    pallas_call x1 -> x2, Pallas kernels: 232 us -> 237 us  [the longest x1 211 us: bwd(): pl.pallas_call(bwd_kernel, grid=(LAYERS, 32), in_specs=[pl.BlockSpec(cota...]
    convert_element_type x2 -> x0, other arithmetic: 4.91 us -> none  [the longest x1 3.4 us: own_shard(): b = weight_out.astype(BF).reshape(LAYERS, 5, CH, D)]
where the time goes in v5:
time: 379 us; the launch traced here: 377 us
  Pallas kernels  373 us (98%)
    pallas_call x1, Pallas kernels, bwd(): pl.pallas_call(bwd_kernel, grid=(LAYERS, 32), in_specs=[pl.BlockSpec(cota...  211 us
    pallas_call x1, Pallas kernels, fwd(): pl.pallas_call(fwd_kernel, grid=(LAYERS, 14), in_specs=[pl.BlockSpec(imag...  136 us
    pallas_call x1, Pallas kernels, adam_all(): pl.pallas_call(functools.partial(adam_kernel, steps=steps), grid=(2 * ste...  26 us

profile of v5, /device:TPU:8, one launch (start us, length us, event | category | flops | bytes accessed | tf_op | source)
XLA Modules:
  0.0 376.5 jit_solution(12790472017836517832)
XLA Ops:
  0.6 0.7 convert_element_type.6
  1.4 0.6 pad_convert_fusion.vs_ref
  2.0 135.7 %shard_map.218 = (f32[2,5,208,768]{3,2,1,0:T(8,128)}, bf16[2,5,208,2304]{3,2,1,0:T(8,128)(2,1)}, bf16[2,5,208,768]{3,2,1,0:T(8,128)(2,1)}, bf16[2,5,208,768]{3,2...) custom-call(bf16[5,197,768]{2,1,0:T(8,128)(2,1)} %img_ref.1, ...), custom_call_target="tpu_custom_call" | custom-call | tf_op jit(solution)/shard_map/pallas_call | solution.py:412
  137.7 0.0 copy-start
  137.7 0.0 copy-start.1
  137.7 0.0 copy-start.2
  137.8 211.2 %shard_map.219 = (f32[5,197,768]{2,1,0:T(8,128)}, f32[2,96,5376]{2,1,0:T(8,128)}, f32[2,480,768]{2,1,0:T(8,128)}, f32[2,16,128]{2,1,0:T(8,128)}) custom-call(bf16[5,197,768]{2,1,0:T(8,128)(2,1)} %cot_ref.1, bf16[18432,768]{1,0:T(8,128)(2,1)} %get-tuple-element.39.w_ref, f32[2,16,768]{2,1,0:T(8,128)} %get-tuple-element.40.vec_ref, ...), custom_call_target="tpu_custom_call" | custom-call | tf_op jit(solution)/shard_map/pallas_call | solution.py:765
  348.9 0.7 slice_bitcast_fusion
  349.7 0.0 copy-done
  349.7 0.0 copy-done.1
  349.7 0.0 copy-done.2
  349.7 0.6 multiply_subtract_fusion
  350.3 26.0 %shard_map.220 = (f32[2,96,5376]{2,1,0:T(8,128)}, f32[2,96,5376]{2,1,0:T(8,128)}, f32[2,96,5376]{2,1,0:T(8,128)}, f32[2,96,5376]{2,1,0:T(8,128)}, f32[2,480,768]...) custom-call(f32[2,96,5376]{2,1,0:T(8,128)} %get-tuple-element.49.g_r, ...), custom_call_target="tpu_custom_call" | custom-call | tf_op jit(solution)/shard_map/pallas_call | solution.py:836
  (1 shorter events, 0.0 us)
Async XLA Ops:
  137.7 211.9 %copy-start = (f32[2,1152]{1,0:T(2,128)S(1)}, f32[2,1152]{1,0:T(2,128)}, u32[]{:S(2)}) copy-start(f32[2,1152]{1,0:T(2,128)} %param.15) | copy-start | bytes 27652
  137.7 211.9 %copy-start.1 = (f32[2,1152]{1,0:T(2,128)S(1)}, f32[2,1152]{1,0:T(2,128)}, u32[]{:S(2)}) copy-start(f32[2,1152]{1,0:T(2,128)} %param.18) | copy-start | bytes 27652
  137.7 211.9 %copy-start.2 = (f32[2,1152]{1,0:T(2,128)S(1)}, f32[2,1152]{1,0:T(2,128)}, u32[]{:S(2)}) copy-start(f32[2,1152]{1,0:T(2,128)} %param.21) | copy-start | bytes 27652

commit v6 on v5

--- a/solution.py
+++ b/solution.py
@@ -209,13 +209,18 @@
     f, core, x, y = plane()
     fc, fx, fy = f + 1 - 2 * core, f + 2 - 4 * x, f + 4 - 8 * y
     fd = fx + fy - f
+    z = lax.axis_index("rep")
+    side = z % 2
+    zp = z + 1 - 2 * side
+    part = pl.ds(pl.multiple_of(256 * side, 128), 512)
+    give = pl.ds(pl.multiple_of(512 * side, 128), 256)
 
     def wrow(c, who, lo=0, n=CH):
-        return w.at[pl.ds(pl.multiple_of(chunk_rows(c, who) + lo, 16), n)]
-
-    def send(c, kind, src, dst, to):
-        return pltpu.make_async_remote_copy(src_ref=src, dst_ref=dst, send_sem=ssem.at[c % 8, kind], recv_sem=rsem.at[c % 8, kind],
-                                            device_id={"fsdp": to}, device_id_type=MESH)
+        return pl.ds(pl.multiple_of(chunk_rows(c, who) + lo, 16), n)
+
+    def send(c, kind, where, **to):
+        return pltpu.make_async_remote_copy(src_ref=w.at[where], dst_ref=w.at[where], send_sem=ssem.at[c % 8, kind], recv_sem=rsem.at[c % 8, kind],
+                                            device_id=to, device_id_type=MESH)
 
     def fetch(c, act):
         layer, j = c // NC, c % NC
@@ -230,12 +235,13 @@
             act(pltpu.make_async_copy(win_ref.at[layer, :, pl.ds(pl.multiple_of((j - 5 * (j // 8)) * D, 128), D)], st.at[c % 4], lsem.at[c % 4]))
 
     def kinds(c):
-        mine, half = wrow(c, f), CH // 2
-        return [lambda: send(c, 0, mine, mine, fx), lambda: send(c, 1, mine, mine, fy), lambda: send(c, 2, mine, mine, fc),
-                lambda: send(c, 3, wrow(c, fx, 0, half), wrow(c, fx, 0, half), fy),
-                lambda: send(c, 4, wrow(c, fy, half, half), wrow(c, fy, half, half), fx),
-                lambda: send(c, 5, wrow(c, fx), wrow(c, fx), fc), lambda: send(c, 6, wrow(c, fy), wrow(c, fy), fc),
-                lambda: send(c, 7, wrow(c, fd), wrow(c, fd), fc)]
+        half = CH // 2
+        return [lambda: send(c, 0, (wrow(c, f), part), fsdp=fx), lambda: send(c, 1, (wrow(c, f), part), fsdp=fy),
+                lambda: send(c, 2, (wrow(c, f),), fsdp=fc),
+                lambda: send(c, 3, (wrow(c, fx, 0, half), part), fsdp=fy), lambda: send(c, 4, (wrow(c, fy, half, half), part), fsdp=fx),
+                lambda: send(c, 5, (wrow(c, fx), give), rep=zp), lambda: send(c, 6, (wrow(c, fy), give), rep=zp),
+                lambda: send(c, 7, (wrow(c, fd), give), rep=zp),
+                lambda: send(c, 8, (wrow(c, fx),), fsdp=fc), lambda: send(c, 9, (wrow(c, fy),), fsdp=fc), lambda: send(c, 10, (wrow(c, fd),), fsdp=fc)]
 
     def start(c, which):
         k = kinds(c)
@@ -248,9 +254,19 @@
             k[i]().wait()
 
     def tick(t):
+        @pl.when((t >= 6) & (t < 30))
+        def _():
+            wait(t - 6, (2, 8, 9, 10))
+
+        @pl.when((t >= 5) & (t < 29))
+        def _():
+            wait(t - 5, (7,))
+            start(t - 5, (10,))
+
         @pl.when((t >= 4) & (t < 28))
         def _():
-            wait(t - 4, (2, 5, 6, 7))
+            wait(t - 4, (5, 6))
+            start(t - 4, (8, 9))
 
         @pl.when((t >= 3) & (t < 27))
         def _():
@@ -282,7 +298,8 @@
         bar = pltpu.get_barrier_semaphore()
         for k in range(1, 8):
             pl.semaphore_signal(bar, inc=1, device_id={"fsdp": (f + k) % 8}, device_id_type=MESH)
-        pl.semaphore_wait(bar, 7)
+        pl.semaphore_signal(bar, inc=1, device_id={"rep": zp}, device_id_type=MESH)
+        pl.semaphore_wait(bar, 8)
 
         def vcopy(k):
             return pltpu.make_async_remote_copy(src_ref=vs_ref, dst_ref=vg.at[f], send_sem=vssem.at[k - 1], recv_sem=vrsem.at[k - 1],
@@ -291,7 +308,7 @@
             vcopy(k).start()
         vg[f] = vs_ref[...]
 
-        @pl.loop(0, 7)
+        @pl.loop(0, 9)
         def _(t):
             tick(t)
         for k in range(1, 8):
@@ -304,13 +321,16 @@
         cp.start()
         cp.wait()
 
-    early = (1 - l) * (s + 6) + l * (s + 18)
-    late = (1 - l) * (s + 2) + l * (s + 14)
+    early = (1 - l) * (s + 8) + l * (s + 20)
+    late = (1 - l) * (s + 4 + s // 11) + l * (s + 16)
 
     @pl.when((s == 0) & (l == 1))
     def _():
-        tick(16)
-        tick(17)
+        tick(19)
+
+    @pl.when((s == 11) & (l == 0))
+    def _():
+        tick(15)
 
     @pl.when((s <= 5) & (l + s > 0))
     def _():
@@ -418,7 +438,7 @@
                    S(images.shape, BF), S((rows, D), BF), S((LAYERS, 16, D), F32)],
         scratch_shapes=[pltpu.VMEM((rows, D), BF), pltpu.VMEM((n, RP, D), F32), pltpu.VMEM((n, RP, D), BF), pltpu.VMEM((n, RP, D), BF),
                         pltpu.VMEM((8, LAYERS, 16, 128), F32), pltpu.VMEM((LAYERS, 16, D), F32), pltpu.VMEM((4, CH, D), F32),
-                        pltpu.SemaphoreType.DMA((4,)), pltpu.SemaphoreType.DMA((8, 8)), pltpu.SemaphoreType.DMA((8, 8)),
+                        pltpu.SemaphoreType.DMA((4,)), pltpu.SemaphoreType.DMA((8, 11)), pltpu.SemaphoreType.DMA((8, 11)),
                         pltpu.SemaphoreType.DMA((7,)), pltpu.SemaphoreType.DMA((7,)), pltpu.SemaphoreType.DMA, pltpu.SemaphoreType.DMA],
         compiler_params=pltpu.CompilerParams(collective_id=0, has_side_effects=True, vmem_limit_bytes=62 * 2**20),
     )(images, weight_in, weight_out, vshard)

time: 379 us -> 362 us (0.955)
  Pallas kernels: 373 us -> 356 us
    pallas_call x1, Pallas kernels: 136 us -> 121 us  [fwd(): pl.pallas_call(fwd_kernel, grid=(LAYERS, 14), in_specs=[pl.BlockSpec(imag...]
where the time goes in v6:
time: 362 us; the launch traced here: 359 us
  Pallas kernels  356 us (98%)
    pallas_call x1, Pallas kernels, bwd(): pl.pallas_call(bwd_kernel, grid=(LAYERS, 32), in_specs=[pl.BlockSpec(cota...  209 us
    pallas_call x1, Pallas kernels, fwd(): pl.pallas_call(fwd_kernel, grid=(LAYERS, 14), in_specs=[pl.BlockSpec(imag...  121 us
    pallas_call x1, Pallas kernels, adam_all(): pl.pallas_call(functools.partial(adam_kernel, steps=steps), grid=(2 * ste...  26 us

profile of v6, /device:TPU:8, one launch (start us, length us, event | category | flops | bytes accessed | tf_op | source)
XLA Modules:
  0.0 359.5 jit_solution(3006052801971461298)
XLA Ops:
  0.6 0.7 convert_element_type.6
  1.4 0.6 pad_convert_fusion.vs_ref
  2.0 120.6 %shard_map.218 = (f32[2,5,208,768]{3,2,1,0:T(8,128)}, bf16[2,5,208,2304]{3,2,1,0:T(8,128)(2,1)}, bf16[2,5,208,768]{3,2,1,0:T(8,128)(2,1)}, bf16[2,5,208,768]{3,2...) custom-call(bf16[5,197,768]{2,1,0:T(8,128)(2,1)} %img_ref.1, ...), custom_call_target="tpu_custom_call" | custom-call | tf_op jit(solution)/shard_map/pallas_call | solution.py:432
  122.6 0.0 copy-start
  122.6 0.0 copy-start.1
  122.6 0.0 copy-start.2
  122.6 209.3 %shard_map.219 = (f32[5,197,768]{2,1,0:T(8,128)}, f32[2,96,5376]{2,1,0:T(8,128)}, f32[2,480,768]{2,1,0:T(8,128)}, f32[2,16,128]{2,1,0:T(8,128)}) custom-call(bf16[5,197,768]{2,1,0:T(8,128)(2,1)} %cot_ref.1, bf16[18432,768]{1,0:T(8,128)(2,1)} %get-tuple-element.39.w_ref, f32[2,16,768]{2,1,0:T(8,128)} %get-tuple-element.40.vec_ref, ...), custom_call_target="tpu_custom_call" | custom-call | tf_op jit(solution)/shard_map/pallas_call | solution.py:785
  331.9 0.7 slice_bitcast_fusion
  332.6 0.0 copy-done
  332.6 0.0 copy-done.1
  332.6 0.0 copy-done.2
  332.6 0.6 multiply_subtract_fusion
  333.3 26.0 %shard_map.220 = (f32[2,96,5376]{2,1,0:T(8,128)}, f32[2,96,5376]{2,1,0:T(8,128)}, f32[2,96,5376]{2,1,0:T(8,128)}, f32[2,96,5376]{2,1,0:T(8,128)}, f32[2,480,768]...) custom-call(f32[2,96,5376]{2,1,0:T(8,128)} %get-tuple-element.49.g_r, ...), custom_call_target="tpu_custom_call" | custom-call | tf_op jit(solution)/shard_map/pallas_call | solution.py:856
  (1 shorter events, 0.0 us)
Async XLA Ops:
  122.6 210.1 %copy-start = (f32[2,1152]{1,0:T(2,128)S(1)}, f32[2,1152]{1,0:T(2,128)}, u32[]{:S(2)}) copy-start(f32[2,1152]{1,0:T(2,128)} %param.15) | copy-start | bytes 27652
  122.6 210.0 %copy-start.1 = (f32[2,1152]{1,0:T(2,128)S(1)}, f32[2,1152]{1,0:T(2,128)}, u32[]{:S(2)}) copy-start(f32[2,1152]{1,0:T(2,128)} %param.18) | copy-start | bytes 27652
  122.6 210.0 %copy-start.2 = (f32[2,1152]{1,0:T(2,128)S(1)}, f32[2,1152]{1,0:T(2,128)}, u32[]{:S(2)}) copy-start(f32[2,1152]{1,0:T(2,128)} %param.21) | copy-start | bytes 27652

commit v7 on v6

--- a/solution.py
+++ b/solution.py
@@ -219,7 +219,7 @@
         return pl.ds(pl.multiple_of(chunk_rows(c, who) + lo, 16), n)
 
     def send(c, kind, where, **to):
-        return pltpu.make_async_remote_copy(src_ref=w.at[where], dst_ref=w.at[where], send_sem=ssem.at[c % 8, kind], recv_sem=rsem.at[c % 8, kind],
+        return pltpu.make_async_remote_copy(src_ref=w.at[where], dst_ref=w.at[where], send_sem=ssem.at[c % 12, kind], recv_sem=rsem.at[c % 12, kind],
                                             device_id=to, device_id_type=MESH)
 
     def fetch(c, act):
@@ -254,35 +254,37 @@
             k[i]().wait()
 
     def tick(t):
+        @pl.when((t >= 7) & (t < 31))
+        def _():
+            wait(t - 7, (2, 8, 9, 10))
+
         @pl.when((t >= 6) & (t < 30))
         def _():
-            wait(t - 6, (2, 8, 9, 10))
-
-        @pl.when((t >= 5) & (t < 29))
-        def _():
-            wait(t - 5, (7,))
-            start(t - 5, (10,))
+            wait(t - 6, (7,))
+            start(t - 6, (10,))
 
         @pl.when((t >= 4) & (t < 28))
         def _():
-            wait(t - 4, (5, 6))
-            start(t - 4, (8, 9))
-
-        @pl.when((t >= 3) & (t < 27))
-        def _():
-            wait(t - 3, (3, 4))
-            start(t - 3, (7,))
+            wait(t - 4, (3, 4, 5, 6))
+            start(t - 4, (7, 8, 9))
 
         @pl.when((t >= 2) & (t < 26))
         def _():
             wait(t - 2, (0, 1))
             start(t - 2, (3, 4, 5, 6))
 
-        @pl.when(t < 24)
-        def _():
-            fetch(t, lambda a: a.wait())
-            w[pl.ds(chunk_rows(t, f), CH)] = st[t % 4].astype(BF)
-            start(t, (0, 1, 2))
+        def launch(c):
+            fetch(c, lambda a: a.wait())
+            w[pl.ds(chunk_rows(c, f), CH)] = st[c % 4].astype(BF)
+            start(c, (0, 1, 2))
+
+        @pl.when(t <= 8)
+        def _():
+            launch(t)
+
+        @pl.when((t >= 8) & (t < 23))
+        def _():
+            launch(t + 1)
 
         @pl.when(t < 21)
         def _():
@@ -308,37 +310,30 @@
             vcopy(k).start()
         vg[f] = vs_ref[...]
 
-        @pl.loop(0, 9)
+        @pl.loop(0, 10)
         def _(t):
             tick(t)
-        for k in range(1, 8):
-            vcopy(k).wait()
-        for layer in range(LAYERS):
-            for c in range(72):
-                vec[layer, c // 6:c // 6 + 1, 128 * (c % 6):128 * (c % 6) + 128] = vg[c // 9, layer, c % 9:c % 9 + 1, :]
-        hb[...] = jnp.zeros_like(hb)
-        cp = pltpu.make_async_copy(vec, vo_ref, vosem)
-        cp.start()
-        cp.wait()
-
-    early = (1 - l) * (s + 8) + l * (s + 20)
-    late = (1 - l) * (s + 4 + s // 11) + l * (s + 16)
-
-    @pl.when((s == 0) & (l == 1))
-    def _():
-        tick(19)
-
-    @pl.when((s == 11) & (l == 0))
-    def _():
-        tick(15)
-
-    @pl.when((s <= 5) & (l + s > 0))
-    def _():
-        tick(early)
-
-    @pl.when(s >= 10)
-    def _():
-        tick(late)
+
+            @pl.when(t == 0)
+            def _():
+                hb[...] = jnp.zeros_like(hb)
+
+            @pl.when(t == 3)
+            def _():
+                for k in range(1, 8):
+                    vcopy(k).wait()
+                for layer in range(LAYERS):
+                    for c in range(72):
+                        vec[layer, c // 6:c // 6 + 1, 128 * (c % 6):128 * (c % 6) + 128] = vg[c // 9, layer, c % 9:c % 9 + 1, :]
+                pltpu.make_async_copy(vec, vo_ref, vosem).start()
+
+    early = s <= 5
+    late = (s == 8) | ((s >= 10) & (s + l <= 13))
+    t = jnp.where(early, (1 - l) * (s + 9) + l * (s + 21), jnp.where(s == 8, 15 + 12 * l, (1 - l) * (s + 6 + s // 12) + l * (s + 18)))
+
+    @pl.when((early & (l + s > 0)) | late)
+    def _():
+        tick(t)
 
     @pl.when(s < 5)
     def _():
@@ -394,6 +389,10 @@
             g_ref[0, i] = g.astype(BF)
             hb[i] += dot(e, w[pl.ds(down, D), :])
             u = later
+            if i == 2:
+                @pl.when((s == 11) & (l == 0))
+                def _():
+                    tick(18)
 
         @pl.when((l == 1) & (s == 13))
         def _():
@@ -419,6 +418,7 @@
     @pl.when((l == 1) & (s == 13))
     def _():
         pltpu.make_async_copy(w, wo_ref, osem).wait()
+        pltpu.make_async_copy(vec, vo_ref, vosem).wait()
 
 
 def fwd(images, weight_in, weight_out, vshard):
@@ -438,7 +438,7 @@
                    S(images.shape, BF), S((rows, D), BF), S((LAYERS, 16, D), F32)],
         scratch_shapes=[pltpu.VMEM((rows, D), BF), pltpu.VMEM((n, RP, D), F32), pltpu.VMEM((n, RP, D), BF), pltpu.VMEM((n, RP, D), BF),
                         pltpu.VMEM((8, LAYERS, 16, 128), F32), pltpu.VMEM((LAYERS, 16, D), F32), pltpu.VMEM((4, CH, D), F32),
-                        pltpu.SemaphoreType.DMA((4,)), pltpu.SemaphoreType.DMA((8, 11)), pltpu.SemaphoreType.DMA((8, 11)),
+                        pltpu.SemaphoreType.DMA((4,)), pltpu.SemaphoreType.DMA((12, 11)), pltpu.SemaphoreType.DMA((12, 11)),
                         pltpu.SemaphoreType.DMA((7,)), pltpu.SemaphoreType.DMA((7,)), pltpu.SemaphoreType.DMA, pltpu.SemaphoreType.DMA],
         compiler_params=pltpu.CompilerParams(collective_id=0, has_side_effects=True, vmem_limit_bytes=62 * 2**20),
     )(images, weight_in, weight_out, vshard)
@@ -446,7 +446,7 @@
 
 def bwd_kernel(cot_ref, w_ref, vec_ref, hs_ref, h1_ref, g_ref, e_ref, qkv_ref, a2_ref, o_ref, a1_ref,
                di_ref, gin_ref, gout_ref, gv_ref,
-               wk, d, acc, db, dhb, du, ab, gb, dv, rc, s2, ra, rb, s3a, s3b, r3a, r3b, s4, rz, s5, ry, s6, rw, fin,
+               wk, d, acc, db, du, ab, gb, dv, rc, s2, ra, rb, s3a, s3b, r3a, r3b, s4, rz, s5, ry, s6, rw, fin,
                vs, vr, vz, wsem, asem, ssem, rsem, osem, vssem, vrsem):
     lr, s = pl.program_id(0), pl.program_id(1)
     l = LAYERS - 1 - lr
@@ -483,14 +483,14 @@
         if n == 2:
             return remote(2, q, s2.at[p, 1 - y, :, pl.ds(half, half)], rb.at[q], fsdp=fy)
         if n == 3:
-            return remote(3, q, s3a.at[p, 1 - y], r3a.at[p], fsdp=fy)
+            return remote(3, q, s3a.at[p, 1 - y], r3a.at[q], fsdp=fy)
         if n == 4:
-            return remote(4, q, s3b.at[p, 1 - x], r3b.at[p], fsdp=fx)
+            return remote(4, q, s3b.at[p, 1 - x], r3b.at[q], fsdp=fx)
         if n == 5:
             return remote(5, q, s4.at[p, pl.ds(theirs, half)], rz.at[q], rep=z1)
         if n == 6:
             return remote(6, q, s5.at[p], ry.at[q], rep=z3)
-        return remote(7, q, s6.at[p], rw.at[p], rep=z1)
+        return remote(7, q, s6.at[p], rw.at[q], rep=z1)
 
     def put(v, act):
         lc, layer = v % NC, LAYERS - 1 - v // NC
@@ -499,7 +499,7 @@
 
         @pl.when(out)
         def _():
-            act(pltpu.make_async_copy(fin.at[p], gout_ref.at[layer, pl.ds(pl.multiple_of((lc - 4) * CH, 8), CH)], osem.at[p]))
+            act(pltpu.make_async_copy(fin.at[p], gout_ref.at[layer, pl.ds(pl.multiple_of((lc - 4) * CH, 16), CH)], osem.at[p]))
 
         @pl.when(jnp.logical_not(out))
         def _():
@@ -511,43 +511,43 @@
         return a + b
 
     def tick(t):
-        @pl.when(live(t - 10))
-        def _():
-            put(t - 10, lambda a: a.wait())
-
-        @pl.when(live(t - 9))
-        def _():
-            v = t - 9
+        @pl.when(live(t - 12))
+        def _():
+            put(t - 12, lambda a: a.wait())
+
+        @pl.when(live(t - 11))
+        def _():
+            v = t - 11
             p = v % 2
             kind(7, v).wait()
-            fin[p, pl.ds(mine, half)] = s6[p].astype(F32)
-            fin[p, pl.ds(theirs, half)] = rw[p].astype(F32)
+            fin[p, pl.ds(mine, half)] = s6[p]
+            fin[p, pl.ds(theirs, half)] = rw[v % 4]
             put(v, lambda a: a.start())
 
-        @pl.when(live(t - 8))
-        def _():
-            v = t - 8
+        @pl.when(live(t - 9))
+        def _():
+            v = t - 9
             p = v % 2
             kind(6, v).wait()
             s6[p] = add(s5[p], ry[v % 4]).astype(BF)
             kind(7, v).start()
 
-        @pl.when(live(t - 6))
-        def _():
-            v = t - 6
+        @pl.when(live(t - 7))
+        def _():
+            v = t - 7
             p = v % 2
             kind(5, v).wait()
             s5[p] = add(s4[p, pl.ds(mine, half)], rz[v % 4]).astype(BF)
             kind(6, v).start()
 
-        @pl.when(live(t - 4))
-        def _():
-            v = t - 4
-            p = v % 2
+        @pl.when(live(t - 5))
+        def _():
+            v = t - 5
+            p, q = v % 2, v % 4
             kind(3, v).wait()
             kind(4, v).wait()
-            s4[p, 0:half] = add(s3a[p, y], r3a[p]).astype(BF)
-            s4[p, half:CH] = add(s3b[p, x], r3b[p]).astype(BF)
+            s4[p, 0:half] = add(s3a[p, y], r3a[q]).astype(BF)
+            s4[p, half:CH] = add(s3b[p, x], r3b[q]).astype(BF)
             kind(5, v).start()
 
         @pl.when(live(t - 3))
@@ -591,58 +591,56 @@
         for i in range(n):
             d[i] = jnp.zeros((RP, D), F32)
             d[i, 0:SEQ, :] = cot_ref[i].astype(F32)
-        load(l, 3, 9, 0).wait()
-
-    @pl.when((lr == 1) & (s == 0))
-    def _():
-        load(l, 3, 3, 0).wait()
-        load(l, 6, 6, 3).wait()
 
     @pl.when(s == 0)
     def _():
         fetch(o_ref, 1, l).start()
 
-    @pl.when(s == 1)
+    @pl.when(s == 4)
     def _():
         fetch(a2_ref, 0, l).wait()
 
+        @pl.when(lr == 0)
+        def _():
+            load(l, 3, 9, 0).wait()
+
+        @pl.when(lr == 1)
+        def _():
+            load(l, 3, 3, 0).wait()
+            load(l, 6, 6, 3).wait()
+
     @pl.when(s == 8)
     def _():
         fetch(a1_ref, 0, l).start()
+        load(l, 0, 3, 0).start()
 
     @pl.when(s == 13)
     def _():
         fetch(o_ref, 1, l).wait()
-        load(l, 0, 3, 0).start()
 
         @pl.when(lr == 0)
         def _():
             load(l - 1, 6, 6, 3).start()
 
-    @pl.when(s == 23)
+    @pl.when(s == 19)
     def _():
         fetch(a1_ref, 0, l).wait()
-
-    @pl.when(s == 26)
-    def _():
         load(l, 0, 3, 0).wait()
 
-    @pl.when((s == 27) & (lr == 0))
+    @pl.when((s == 20) & (lr == 0))
     def _():
         fetch(a2_ref, 0, l - 1).start()
         load(l - 1, 3, 3, 0).start()
 
-    one = (s >= 2) & (s <= 8) & (s % 2 == 0)
-    two = (s >= 18) & (s <= 22) & (s != 20)
-    three = s == 24
-    four = (lr == 0) & ((s == 26) | (s == 28))
-    five = (lr == 1) & (s >= 25)
-    six = (lr == 1) & (s == 0)
-    back = s - 18
-    t = jnp.where(one, 12 * lr + s // 2 - 1, jnp.where(two, 12 * lr + 4 + back - back // 3, jnp.where(three, 12 * lr + 8, jnp.where(
-        four, 9 + (s - 26) // 2, jnp.where(five, s - 4, 11)))))
-
-    @pl.when(one | two | three | four | five | six)
+    one = (s >= 5) & (s <= 8)
+    two = (s >= 14) & (s <= 19) & (s != 16)
+    three = (lr == 0) & (s == 21)
+    four = (lr == 1) & ((s == 0) | (s == 2))
+    five = (lr == 1) & (s >= 20)
+    back = s - 14
+    t = jnp.where(one, 12 * lr + s - 5, jnp.where(two, 12 * lr + 4 + back - (back + 1) // 4, jnp.where(three, 9, jnp.where(four, 10 + s // 2, s + 3))))
+
+    @pl.when(one | two | three | four | five)
     def _():
         tick(t)
 
@@ -654,9 +652,9 @@
             acc[i] = jnp.zeros((RP, D), F32)
             dv[l, 7:8] += rsum(up)
 
-    @pl.when((s < 8) & (s % 2 == 0))
-    def _():
-        j = s // 2
+    @pl.when((s >= 4) & (s < 8))
+    def _():
+        j = s - 4
         whole = db[...].reshape(rows, D)
         cols = pl.multiple_of(j * D, 128)
         for q in range(3):
@@ -675,8 +673,8 @@
         dh1 = d[i] + dx
         d[i] = dh1
         dv[l, 4:5] += rsum(dh1)
-        dhb[i] = dh1.astype(BF)
-        du[i, :, 3 * D:4 * D] = dot_t(dhb[i], wk[4 * D:5 * D, :]).astype(BF)
+        du[i, :, 0:D] = dh1.astype(BF)
+        du[i, :, 3 * D:4 * D] = dot_t(du[i, :, 0:D], wk[4 * D:5 * D, :]).astype(BF)
 
     def grad(lhs, rhs, store):
         for m in range(2):
@@ -696,23 +694,23 @@
             for q in range(4):
                 b = 8 * step + m + q
                 gb[4 + b % 5, b // 10, (b // 5) % 2] = r[q]
-        grad(lhs, rhs[...].reshape(rows, D), store)
-
-    @pl.when((s < 8) & (s % 2 == 1))
-    def _():
-        inner(s // 2, s // 2)
+        grad(lhs, rhs.reshape(rows, D), store)
+
+    @pl.when((s >= 4) & (s < 8))
+    def _():
+        inner(s - 4, s - 4)
 
     @pl.when(s == 13)
     def _():
-        outer(0, lambda m: ab[1, :, :, m:m + 384].reshape(rows, 384), dhb)
-
-    @pl.when((s >= 14) & (s < 18))
-    def _():
-        outer(s - 13, lambda m: e_ref[0, :, :, m:m + 384].reshape(rows, 384), db)
-
-    @pl.when((s >= 18) & (s < 23))
-    def _():
-        i = s - 18
+        outer(0, lambda m: ab[1, :, :, m:m + 384].reshape(rows, 384), du[:, :, 0:D])
+
+    @pl.when(s < 4)
+    def _():
+        outer(s + 1, lambda m: e_ref[0, :, :, m:m + 384].reshape(rows, 384), db[...])
+
+    @pl.when((s >= 14) & (s < 19))
+    def _():
+        i = s - 14
         for p in range(6):
             b = 128 * p
             dq, dk, dvv = attn_bwd(qkv_ref[0, 0, :, b:b + 128], qkv_ref[0, 0, :, D + b:D + b + 128], qkv_ref[0, 0, :, 2 * D + b:2 * D + b + 128],
@@ -723,19 +721,22 @@
             du[i, :, D + b:D + b + 128] = dk.astype(BF)
             du[i, :, 2 * D + b:2 * D + b + 128] = dvv.astype(BF)
 
-    @pl.when((s >= 23) & (s < 26))
-    def _():
-        inner(s - 23, s - 23)
-
-    @pl.when(s == 26)
-    def _():
+    @pl.when(s == 19)
+    def _():
+        @pl.loop(0, 3)
+        def _(j):
+            inner(j, j)
+
+            @pl.when((lr == 1) & (j >= 1))
+            def _():
+                tick(20 + j)
         acc[...] = dot_t(du[:, :, 0:D].reshape(rows, D), wk[0:D, :]).reshape(n, RP, D)
         acc[...] += dot_t(du[:, :, D:2 * D].reshape(rows, D), wk[D:2 * D, :]).reshape(n, RP, D)
         acc[...] += dot_t(du[:, :, 2 * D:3 * D].reshape(rows, D), wk[2 * D:3 * D, :]).reshape(n, RP, D)
 
-    @pl.when(s >= 27)
-    def _():
-        i = s - 27
+    @pl.when(s >= 20)
+    def _():
+        i = s - 20
         dx, dg, dc = norm_back(hs_ref[0, 0], vec_ref[l, 0:1], acc[i])
         dv[l, 0:1] += dg
         dv[l, 1:2] += dc
@@ -743,7 +744,7 @@
         d[i] = dh
         di_ref[0] = dh[0:SEQ]
 
-    @pl.when((lr == 1) & (s == 31))
+    @pl.when((lr == 1) & (s == 24))
     def _():
         for layer in range(LAYERS):
             for c in range(72):
@@ -759,16 +760,21 @@
                                                 device_id={"rep": (z + k) % 4}, device_id_type=MESH)
         for k in range(1, 8):
             vcopy(k).start()
-        for t in range(28, 34):
-            tick(jnp.int32(t))
-        for k in range(1, 8):
-            vcopy(k).wait()
-        total = vs[f]
-        for k in range(7):
-            total = total + vr[k]
-        vz[z] = total
-        for k in range(1, 4):
-            zcopy(k).start()
+
+        @pl.loop(28, 36)
+        def _(t):
+            @pl.when(t == 30)
+            def _():
+                for k in range(1, 8):
+                    vcopy(k).wait()
+                total = vs[f]
+                for k in range(7):
+                    total = total + vr[k]
+                vz[z] = total
+                for k in range(1, 4):
+                    zcopy(k).start()
+            tick(t)
+
         for k in range(1, 4):
             zcopy(k).wait()
         gv_ref[...] = (vz[0] + vz[1]) + (vz[2] + vz[3])
@@ -779,22 +785,21 @@
     S = jax.ShapeDtypeStruct
     anyw = pl.BlockSpec(memory_space=pl.ANY)
     row = lambda cols, at: pl.BlockSpec((1, 1, RP, cols), lambda lr, s: (LAYERS - 1 - lr, jnp.clip(s - at, 0, 4), 0, 0))
+    cols = lambda at: pl.BlockSpec((1, n, RP, D), lambda lr, s: (LAYERS - 1 - lr, 0, 0, jnp.clip(s - at, 0, 3)))
     tok = lambda index: pl.BlockSpec((1, SEQ, D), index)
     VB = lambda *shape: pltpu.VMEM(shape, BF)
     half = CH // 2
     return pl.pallas_call(
-        bwd_kernel, grid=(LAYERS, 32),
+        bwd_kernel, grid=(LAYERS, 25),
         in_specs=[pl.BlockSpec(cotangent.shape, lambda lr, s: (0, 0, 0), pipeline_mode=pl.Buffered(1)), anyw, pl.BlockSpec(vec.shape, lambda lr, s: (0, 0, 0)),
-                  row(D, 27), row(D, 8), pl.BlockSpec((1, n, RP, D), lambda lr, s: (LAYERS - 1 - lr, 0, 0, jnp.minimum(s // 2, 3))),
-                  pl.BlockSpec((1, n, RP, D), lambda lr, s: (LAYERS - 1 - lr, 0, 0, jnp.clip(s - 14, 0, 3))),
-                  row(3 * D, 18), anyw, anyw, anyw],
-        out_specs=[tok(lambda lr, s: (lr * jnp.clip(s - 27, 0, 4), 0, 0)), anyw, anyw, pl.BlockSpec((LAYERS, 16, 128), lambda lr, s: (0, 0, 0))],
-        out_shape=[S(cotangent.shape, F32), S(shard_in, F32), S(shard_out, F32), S((LAYERS, 16, 128), F32)],
-        scratch_shapes=[VB(9 * D, D), pltpu.VMEM((n, RP, D), F32), pltpu.VMEM((n, RP, D), F32), VB(n, RP, D), VB(n, RP, D), VB(n, RP, 4 * D), VB(2, n, RP, D),
+                  row(D, 20), row(D, 8), cols(4), cols(0), row(3 * D, 14), anyw, anyw, anyw],
+        out_specs=[tok(lambda lr, s: (lr * jnp.clip(s - 20, 0, 4), 0, 0)), anyw, anyw, pl.BlockSpec((LAYERS, 16, 128), lambda lr, s: (0, 0, 0))],
+        out_shape=[S(cotangent.shape, F32), S(shard_in, BF), S(shard_out, BF), S((LAYERS, 16, 128), F32)],
+        scratch_shapes=[VB(9 * D, D), pltpu.VMEM((n, RP, D), F32), pltpu.VMEM((n, RP, D), F32), VB(n, RP, D), VB(n, RP, 4 * D), VB(2, n, RP, D),
                         VB(9, 4, 2, CH, D), pltpu.VMEM((LAYERS, 16, D), F32),
                         VB(2, 4, CH, D), VB(2, 2, 2, CH, D), VB(4, 2, half, D), VB(4, 2, half, D), VB(2, 2, half, D), VB(2, 2, half, D),
-                        VB(2, half, D), VB(2, half, D), VB(2, CH, D), VB(4, half, D), VB(2, half, D), VB(4, half, D), VB(2, half, D), VB(2, half, D),
-                        pltpu.VMEM((2, CH, D), F32),
+                        VB(4, half, D), VB(4, half, D), VB(2, CH, D), VB(4, half, D), VB(2, half, D), VB(4, half, D), VB(2, half, D), VB(4, half, D),
+                        VB(2, CH, D),
                         pltpu.VMEM((8, LAYERS, 16, 128), F32), pltpu.VMEM((7, LAYERS, 16, 128), F32), pltpu.VMEM((4, LAYERS, 16, 128), F32),
                         pltpu.SemaphoreType.DMA((2,)), pltpu.SemaphoreType.DMA((2,)), pltpu.SemaphoreType.DMA((4, 8)), pltpu.SemaphoreType.DMA((4, 8)),
                         pltpu.SemaphoreType.DMA((2,)), pltpu.SemaphoreType.DMA((10,)), pltpu.SemaphoreType.DMA((10,))],
@@ -825,7 +830,7 @@
     i = pl.program_id(0)
 
     def update(g, w, m, v, outs):
-        grad = g[...]
+        grad = g[...].astype(F32)
         new, moment, square = adam_update(w[...], grad, m[...], v[...], matrix_rate, matrix_decay)
         outs[0][...], outs[1][...], outs[2][...], outs[3][...] = grad, new, moment, square
 
@@ -848,9 +853,9 @@
 
 def adam_all(ins, outs, encoded, dimg):
     a, b = ins[0].shape, outs[0].shape
-    steps = 3 * LAYERS
-    first = pl.BlockSpec((1, a[1], a[2] // 3), lambda i: (jnp.minimum(i, steps - 1) // 3, 0, jnp.minimum(i, steps - 1) % 3))
-    second = pl.BlockSpec((1, b[1] // 3, b[2]), lambda i: (jnp.maximum(i - steps, 0) // 3, jnp.maximum(i - steps, 0) % 3, 0))
+    steps = 2 * LAYERS
+    first = pl.BlockSpec((1, a[1] // 2, a[2]), lambda i: (jnp.minimum(i, steps - 1) // 2, jnp.minimum(i, steps - 1) % 2, 0))
+    second = pl.BlockSpec((1, b[1] // 2, b[2]), lambda i: (jnp.maximum(i - steps, 0) // 2, jnp.maximum(i - steps, 0) % 2, 0))
     tok = pl.BlockSpec((1,) + encoded.shape[1:], lambda i: (jnp.minimum(i, enc_steps - 1), 0, 0))
     S = jax.ShapeDtypeStruct
     return pl.pallas_call(

time: 362 us -> 348 us (0.961)
  Pallas kernels: 356 us -> 343 us
    pallas_call x1, Pallas kernels: 209 us -> 204 us  [bwd(): pl.pallas_call(bwd_kernel, grid=(LAYERS, 25), in_specs=[pl.BlockSpec(cota...]
where the time goes in v7:
time: 348 us; the launch traced here: 347 us
  Pallas kernels  343 us (99%)
    pallas_call x1, Pallas kernels, bwd(): pl.pallas_call(bwd_kernel, grid=(LAYERS, 25), in_specs=[pl.BlockSpec(cota...  204 us
    pallas_call x1, Pallas kernels, fwd(): pl.pallas_call(fwd_kernel, grid=(LAYERS, 14), in_specs=[pl.BlockSpec(imag...  117 us
    pallas_call x1, Pallas kernels, adam_all(): pl.pallas_call(functools.partial(adam_kernel, steps=steps), grid=(2 * ste...  22.5 us

profile of v7, /device:TPU:8, one launch (start us, length us, event | category | flops | bytes accessed | tf_op | source)
XLA Modules:
  0.0 346.8 jit_solution(5169762003454806488)
XLA Ops:
  0.6 0.7 convert_element_type.6
  1.4 0.6 pad_convert_fusion.vs_ref
  2.0 117.0 %shard_map.218 = (f32[2,5,208,768]{3,2,1,0:T(8,128)}, bf16[2,5,208,2304]{3,2,1,0:T(8,128)(2,1)}, bf16[2,5,208,768]{3,2,1,0:T(8,128)(2,1)}, bf16[2,5,208,768]{3,2...) custom-call(bf16[5,197,768]{2,1,0:T(8,128)(2,1)} %img_ref.1, ...), custom_call_target="tpu_custom_call" | custom-call | tf_op jit(solution)/shard_map/pallas_call | solution.py:432
  119.0 0.0 copy-start
  119.0 0.0 copy-start.1
  119.0 0.0 copy-start.2
  119.0 203.7 %shard_map.219 = (f32[5,197,768]{2,1,0:T(8,128)}, bf16[2,96,5376]{2,1,0:T(8,128)(2,1)}, bf16[2,480,768]{2,1,0:T(8,128)(2,1)}, f32[2,16,128]{2,1,0:T(8,128)}) custom-call(bf16[5,197,768]{2,1,0:T(8,128)(2,1)} %cot_ref.1, bf16[18432,768]{1,0:T(8,128)(2,1)} %get-tuple-element.39.w_ref, f32[2,16,768]{2,1,0:T(8,128)} %get-tuple-element.40.vec_ref, ...), custom_call_target="tpu_custom_call" | custom-call | tf_op jit(solution)/shard_map/pallas_call | solution.py:792
  322.8 0.7 slice_bitcast_fusion
  323.5 0.0 copy-done
  323.5 0.0 copy-done.1
  323.5 0.0 copy-done.2
  323.5 0.6 multiply_subtract_fusion
  324.1 22.5 %shard_map.220 = (f32[2,96,5376]{2,1,0:T(8,128)}, f32[2,96,5376]{2,1,0:T(8,128)}, f32[2,96,5376]{2,1,0:T(8,128)}, f32[2,96,5376]{2,1,0:T(8,128)}, f32[2,480,768]...) custom-call(bf16[2,96,5376]{2,1,0:T(8,128)(2,1)} %get-tuple-element., ...), custom_call_target="tpu_custom_call" | custom-call | tf_op jit(solution)/shard_map/pallas_call | solution.py:861
  (1 shorter events, 0.0 us)
Async XLA Ops:
  119.0 204.5 %copy-start = (f32[2,1152]{1,0:T(2,128)S(1)}, f32[2,1152]{1,0:T(2,128)}, u32[]{:S(2)}) copy-start(f32[2,1152]{1,0:T(2,128)} %param.15) | copy-start | bytes 27652
  119.0 204.5 %copy-start.1 = (f32[2,1152]{1,0:T(2,128)S(1)}, f32[2,1152]{1,0:T(2,128)}, u32[]{:S(2)}) copy-start(f32[2,1152]{1,0:T(2,128)} %param.18) | copy-start | bytes 27652
  119.0 204.5 %copy-start.2 = (f32[2,1152]{1,0:T(2,128)S(1)}, f32[2,1152]{1,0:T(2,128)}, u32[]{:S(2)}) copy-start(f32[2,1152]{1,0:T(2,128)} %param.21) | copy-start | bytes 27652

commit v8 on v7

--- a/solution.py
+++ b/solution.py
@@ -51,6 +51,22 @@
     dk = dot(ds[0], q * scaled[0]) + dot(ds[1], q * scaled[1])
     dq = dot_0(ds[0], k * scaled[0]) + dot_0(ds[1], k * scaled[1])
     return dq, dk, dv
+
+
+TAIL = SEQ - RP + 16
+
+
+def fold_rows(first, last):
+    r = lax.broadcasted_iota(jnp.int32, (16, 16), 0)
+    c = lax.broadcasted_iota(jnp.int32, (16, 16), 1)
+    move = jnp.where((r == c + TAIL) & (c < TAIL), 1.0, 0.0).astype(BF)
+    row = lax.broadcasted_iota(jnp.int32, (16, 1), 0)
+    return jnp.where((row >= TAIL) & (row < 2 * TAIL), dot(move, last), first.astype(F32)).astype(BF)
+
+
+def clear_rows(first):
+    row = lax.broadcasted_iota(jnp.int32, (16, 1), 0)
+    return jnp.where(row < TAIL, first.astype(F32), 0.0).astype(BF)
 
 
 def ka_kernel(h_ref,w_ref,vec_ref,qkv_ref,o_ref,a_ref):
@@ -278,13 +294,9 @@
             w[pl.ds(chunk_rows(c, f), CH)] = st[c % 4].astype(BF)
             start(c, (0, 1, 2))
 
-        @pl.when(t <= 8)
+        @pl.when(t < 24)
         def _():
             launch(t)
-
-        @pl.when((t >= 8) & (t < 23))
-        def _():
-            launch(t + 1)
 
         @pl.when(t < 21)
         def _():
@@ -393,6 +405,8 @@
                 @pl.when((s == 11) & (l == 0))
                 def _():
                     tick(18)
+
+        e_ref[0, 0, RP - 16:RP] = fold_rows(e_ref[0, 0, RP - 16:RP], e_ref[0, n - 1, RP - 16:RP])
 
         @pl.when((l == 1) & (s == 13))
         def _():
@@ -599,6 +613,7 @@
     @pl.when(s == 4)
     def _():
         fetch(a2_ref, 0, l).wait()
+        ab[0, 0, RP - 16:RP] = fold_rows(ab[0, 0, RP - 16:RP], ab[0, n - 1, RP - 16:RP])
 
         @pl.when(lr == 0)
         def _():
@@ -617,6 +632,7 @@
     @pl.when(s == 13)
     def _():
         fetch(o_ref, 1, l).wait()
+        ab[1, 0, RP - 16:RP] = fold_rows(ab[1, 0, RP - 16:RP], ab[1, n - 1, RP - 16:RP])
 
         @pl.when(lr == 0)
         def _():
@@ -625,6 +641,7 @@
     @pl.when(s == 19)
     def _():
         fetch(a1_ref, 0, l).wait()
+        ab[0, 0, RP - 16:RP] = fold_rows(ab[0, 0, RP - 16:RP], ab[0, n - 1, RP - 16:RP])
         load(l, 0, 3, 0).wait()
 
     @pl.when((s == 20) & (lr == 0))
@@ -633,12 +650,11 @@
         load(l - 1, 3, 3, 0).start()
 
     one = (s >= 5) & (s <= 8)
-    two = (s >= 14) & (s <= 19) & (s != 16)
-    three = (lr == 0) & (s == 21)
-    four = (lr == 1) & ((s == 0) | (s == 2))
+    two = (s >= 14) & (s <= 18)
+    three = (lr == 0) & ((s == 20) | (s == 23))
+    four = (lr == 1) & (s == 1)
     five = (lr == 1) & (s >= 20)
-    back = s - 14
-    t = jnp.where(one, 12 * lr + s - 5, jnp.where(two, 12 * lr + 4 + back - (back + 1) // 4, jnp.where(three, 9, jnp.where(four, 10 + s // 2, s + 3))))
+    t = jnp.where(one, 12 * lr + s - 5, jnp.where(two, 12 * lr + s - 10, jnp.where(three, 9 + (s - 20) // 3, jnp.where(four, 11, s + 4))))
 
     @pl.when(one | two | three | four | five)
     def _():
@@ -651,6 +667,11 @@
             db[i] = up.astype(BF)
             acc[i] = jnp.zeros((RP, D), F32)
             dv[l, 7:8] += rsum(up)
+        db[0, RP - 16:RP] = fold_rows(db[0, RP - 16:RP], db[n - 1, RP - 16:RP])
+
+    @pl.when(s == 4)
+    def _():
+        db[0, RP - 16:RP] = clear_rows(db[0, RP - 16:RP])
 
     @pl.when((s >= 4) & (s < 8))
     def _():
@@ -677,8 +698,9 @@
         du[i, :, 3 * D:4 * D] = dot_t(du[i, :, 0:D], wk[4 * D:5 * D, :]).astype(BF)
 
     def grad(lhs, rhs, store):
+        rhs = rhs[:rows - 16]
         for m in range(2):
-            r = dot_0(lhs(384 * m), rhs).astype(BF).reshape(4, CH, D)
+            r = dot_0(lhs(384 * m)[:rows - 16], rhs).astype(BF).reshape(4, CH, D)
             store(4 * m, r)
 
     def inner(slot, j):
@@ -698,10 +720,13 @@
 
     @pl.when((s >= 4) & (s < 8))
     def _():
+        at = pl.ds(pl.multiple_of((s - 4) * D, 128), D)
+        du[0, RP - 16:RP, at] = fold_rows(du[0, RP - 16:RP, at], du[n - 1, RP - 16:RP, at])
         inner(s - 4, s - 4)
 
     @pl.when(s == 13)
     def _():
+        du[0, RP - 16:RP, 0:D] = fold_rows(du[0, RP - 16:RP, 0:D], du[n - 1, RP - 16:RP, 0:D])
         outer(0, lambda m: ab[1, :, :, m:m + 384].reshape(rows, 384), du[:, :, 0:D])
 
     @pl.when(s < 4)
@@ -723,13 +748,16 @@
 
     @pl.when(s == 19)
     def _():
+        du[0, RP - 16:RP, 0:3 * D] = fold_rows(du[0, RP - 16:RP, 0:3 * D], du[n - 1, RP - 16:RP, 0:3 * D])
+
         @pl.loop(0, 3)
         def _(j):
             inner(j, j)
 
-            @pl.when((lr == 1) & (j >= 1))
+            @pl.when(lr == 1)
             def _():
-                tick(20 + j)
+                tick(21 + j)
+        du[0, RP - 16:RP, 0:3 * D] = clear_rows(du[0, RP - 16:RP, 0:3 * D])
         acc[...] = dot_t(du[:, :, 0:D].reshape(rows, D), wk[0:D, :]).reshape(n, RP, D)
         acc[...] += dot_t(du[:, :, D:2 * D].reshape(rows, D), wk[D:2 * D, :]).reshape(n, RP, D)
         acc[...] += dot_t(du[:, :, 2 * D:3 * D].reshape(rows, D), wk[2 * D:3 * D, :]).reshape(n, RP, D)
@@ -761,7 +789,7 @@
         for k in range(1, 8):
             vcopy(k).start()
 
-        @pl.loop(28, 36)
+        @pl.loop(29, 36)
         def _(t):
             @pl.when(t == 30)
             def _():

time: 348 us -> 342 us (0.983)
  Pallas kernels: 343 us -> 338 us
    pallas_call x1, Pallas kernels: 204 us -> 198 us  [bwd(): pl.pallas_call(bwd_kernel, grid=(LAYERS, 25), in_specs=[pl.BlockSpec(cota...]
where the time goes in v8:
time: 342 us; the launch traced here: 341 us
  Pallas kernels  338 us (99%)
    pallas_call x1, Pallas kernels, bwd(): pl.pallas_call(bwd_kernel, grid=(LAYERS, 25), in_specs=[pl.BlockSpec(cota...  198 us
    pallas_call x1, Pallas kernels, fwd(): pl.pallas_call(fwd_kernel, grid=(LAYERS, 14), in_specs=[pl.BlockSpec(imag...  117 us
    pallas_call x1, Pallas kernels, adam_all(): pl.pallas_call(functools.partial(adam_kernel, steps=steps), grid=(2 * ste...  22.5 us

profile of v8, /device:TPU:8, one launch (start us, length us, event | category | flops | bytes accessed | tf_op | source)
XLA Modules:
  0.0 341.4 jit_solution(3597880280401883807)
XLA Ops:
  0.6 0.7 convert_element_type.6
  1.4 0.6 pad_convert_fusion.vs_ref
  2.0 117.2 %shard_map.218 = (f32[2,5,208,768]{3,2,1,0:T(8,128)}, bf16[2,5,208,2304]{3,2,1,0:T(8,128)(2,1)}, bf16[2,5,208,768]{3,2,1,0:T(8,128)(2,1)}, bf16[2,5,208,768]{3,2...) custom-call(bf16[5,197,768]{2,1,0:T(8,128)(2,1)} %img_ref.1, ...), custom_call_target="tpu_custom_call" | custom-call | tf_op jit(solution)/shard_map/pallas_call | solution.py:446
  119.2 0.0 copy-start
  119.2 0.0 copy-start.1
  119.2 0.0 copy-start.2
  119.2 198.2 %shard_map.219 = (f32[5,197,768]{2,1,0:T(8,128)}, bf16[2,96,5376]{2,1,0:T(8,128)(2,1)}, bf16[2,480,768]{2,1,0:T(8,128)(2,1)}, f32[2,16,128]{2,1,0:T(8,128)}) custom-call(bf16[5,197,768]{2,1,0:T(8,128)(2,1)} %cot_ref.1, bf16[18432,768]{1,0:T(8,128)(2,1)} %get-tuple-element.39.w_ref, f32[2,16,768]{2,1,0:T(8,128)} %get-tuple-element.40.vec_ref, ...), custom_call_target="tpu_custom_call" | custom-call | tf_op jit(solution)/shard_map/pallas_call | solution.py:820
  317.4 0.7 slice_bitcast_fusion
  318.1 0.0 copy-done
  318.1 0.0 copy-done.1
  318.1 0.0 copy-done.2
  318.1 0.6 multiply_subtract_fusion
  318.8 22.5 %shard_map.220 = (f32[2,96,5376]{2,1,0:T(8,128)}, f32[2,96,5376]{2,1,0:T(8,128)}, f32[2,96,5376]{2,1,0:T(8,128)}, f32[2,96,5376]{2,1,0:T(8,128)}, f32[2,480,768]...) custom-call(bf16[2,96,5376]{2,1,0:T(8,128)(2,1)} %get-tuple-element., ...), custom_call_target="tpu_custom_call" | custom-call | tf_op jit(solution)/shard_map/pallas_call | solution.py:889
  (1 shorter events, 0.0 us)
Async XLA Ops:
  119.2 198.9 %copy-start = (f32[2,1152]{1,0:T(2,128)S(1)}, f32[2,1152]{1,0:T(2,128)}, u32[]{:S(2)}) copy-start(f32[2,1152]{1,0:T(2,128)} %param.15) | copy-start | bytes 27652
  119.2 198.9 %copy-start.1 = (f32[2,1152]{1,0:T(2,128)S(1)}, f32[2,1152]{1,0:T(2,128)}, u32[]{:S(2)}) copy-start(f32[2,1152]{1,0:T(2,128)} %param.18) | copy-start | bytes 27652
  119.2 198.9 %copy-start.2 = (f32[2,1152]{1,0:T(2,128)S(1)}, f32[2,1152]{1,0:T(2,128)}, u32[]{:S(2)}) copy-start(f32[2,1152]{1,0:T(2,128)} %param.21) | copy-start | bytes 27652

commit v9 on v8

--- a/solution.py
+++ b/solution.py
@@ -19,13 +19,6 @@
 def head_masks(scale):
     lane = lax.broadcasted_iota(jnp.int32, (1, 128), 1)
     return jnp.where(lane < 64, scale, 0.0).astype(BF), jnp.where(lane < 64, 0.0, scale).astype(BF)
-
-
-def weights_t(q, k, masks):
-    row = lax.broadcasted_iota(jnp.int32, (RP, 1), 0)
-    s = [jnp.where(row < SEQ, dot_t(k, q * m), -1e30) for m in masks]
-    e = [jnp.exp(x - jnp.max(x, axis=0, keepdims=True)) for x in s]
-    return [x * (1.0 / jnp.sum(x, axis=0, keepdims=True)) for x in e]
 
 
 def attn_fwd(q, k, v):
@@ -40,17 +33,27 @@
     return (dot_0(ps[0], v * ones[0]) + dot_0(ps[1], v * ones[1])).astype(BF)
 
 
-def attn_bwd(q, k, v, do):
+def attn_bwd_products(q, k, v, do):
     scaled, ones = head_masks(0.125), head_masks(1.0)
-    p = weights_t(q, k, scaled)
-    dos = [do * m for m in ones]
-    dp = [dot_t(v, x) for x in dos]
+    row = lax.broadcasted_iota(jnp.int32, (RP, 1), 0)
+    qs, ks, dos = [q * m for m in scaled], [k * m for m in scaled], [do * m for m in ones]
+    s = [jnp.where(row < SEQ, dot_t(k, x), -1e30) for x in qs]
+    return qs, ks, dos, s, [dot_t(v, x) for x in dos]
+
+
+def attn_bwd_rest(qs, ks, dos, s, dp):
+    e = [jnp.exp(x - jnp.max(x, axis=0, keepdims=True)) for x in s]
+    p = [x * (1.0 / jnp.sum(x, axis=0, keepdims=True)) for x in e]
     pb = [x.astype(BF) for x in p]
     ds = [(a * (b - jnp.sum(a * b, axis=0, keepdims=True))).astype(BF) for a, b in zip(p, dp)]
     dv = dot(pb[0], dos[0]) + dot(pb[1], dos[1])
-    dk = dot(ds[0], q * scaled[0]) + dot(ds[1], q * scaled[1])
-    dq = dot_0(ds[0], k * scaled[0]) + dot_0(ds[1], k * scaled[1])
+    dk = dot(ds[0], qs[0]) + dot(ds[1], qs[1])
+    dq = dot_0(ds[0], ks[0]) + dot_0(ds[1], ks[1])
     return dq, dk, dv
+
+
+def attn_bwd(q, k, v, do):
+    return attn_bwd_rest(*attn_bwd_products(q, k, v, do))
 
 
 TAIL = SEQ - RP + 16
@@ -650,11 +653,11 @@
         load(l - 1, 3, 3, 0).start()
 
     one = (s >= 5) & (s <= 8)
-    two = (s >= 14) & (s <= 18)
-    three = (lr == 0) & ((s == 20) | (s == 23))
-    four = (lr == 1) & (s == 1)
+    two = (lr == 1) & (s >= 14) & (s <= 18)
+    three = (lr == 0) & ((s == 14) | (s == 16) | (s == 18) | (s == 19))
+    four = ((lr == 0) & (s == 21)) | ((lr == 1) & ((s == 0) | (s == 2)))
     five = (lr == 1) & (s >= 20)
-    t = jnp.where(one, 12 * lr + s - 5, jnp.where(two, 12 * lr + s - 10, jnp.where(three, 9 + (s - 20) // 3, jnp.where(four, 11, s + 4))))
+    t = jnp.where(one, 12 * lr + s - 5, jnp.where(two, s + 2, jnp.where(three, 4 + (s - 14) // 2 + s // 19, jnp.where(four, 9 + lr * (1 + s // 2), s + 4))))
 
     @pl.when(one | two | three | four | five)
     def _():
@@ -736,10 +739,16 @@
     @pl.when((s >= 14) & (s < 19))
     def _():
         i = s - 14
+
+        def products(p):
+            b = 128 * p
+            return attn_bwd_products(qkv_ref[0, 0, :, b:b + 128], qkv_ref[0, 0, :, D + b:D + b + 128], qkv_ref[0, 0, :, 2 * D + b:2 * D + b + 128],
+                                     du[i, :, 3 * D + b:3 * D + b + 128])
+        later = products(0)
         for p in range(6):
             b = 128 * p
-            dq, dk, dvv = attn_bwd(qkv_ref[0, 0, :, b:b + 128], qkv_ref[0, 0, :, D + b:D + b + 128], qkv_ref[0, 0, :, 2 * D + b:2 * D + b + 128],
-                                   du[i, :, 3 * D + b:3 * D + b + 128])
+            now, later = later, (products(p + 1) if p < 5 else None)
+            dq, dk, dvv = attn_bwd_rest(*now)
             dv[l, 2:3, b:b + 128] += rsum(dq)
             dv[l, 3:4, b:b + 128] += rsum(dvv)
             du[i, :, b:b + 128] = dq.astype(BF)
@@ -754,9 +763,9 @@
         def _(j):
             inner(j, j)
 
-            @pl.when(lr == 1)
+            @pl.when((lr == 1) | (j == 1))
             def _():
-                tick(21 + j)
+                tick(lr * (21 + j) + (1 - lr) * 8)
         du[0, RP - 16:RP, 0:3 * D] = clear_rows(du[0, RP - 16:RP, 0:3 * D])
         acc[...] = dot_t(du[:, :, 0:D].reshape(rows, D), wk[0:D, :]).reshape(n, RP, D)
         acc[...] += dot_t(du[:, :, D:2 * D].reshape(rows, D), wk[D:2 * D, :]).reshape(n, RP, D)

time: 342 us -> 339 us (level)
  Pallas kernels: 338 us -> 334 us
    pallas_call x1, Pallas kernels: 198 us -> 194 us  [bwd(): pl.pallas_call(bwd_kernel, grid=(LAYERS, 25), in_specs=[pl.BlockSpec(cota...]
where the time goes in v9:
time: 339 us; the launch traced here: 338 us
  Pallas kernels  334 us (99%)
    pallas_call x1, Pallas kernels, bwd(): pl.pallas_call(bwd_kernel, grid=(LAYERS, 25), in_specs=[pl.BlockSpec(cota...  194 us
    pallas_call x1, Pallas kernels, fwd(): pl.pallas_call(fwd_kernel, grid=(LAYERS, 14), in_specs=[pl.BlockSpec(imag...  117 us
    pallas_call x1, Pallas kernels, adam_all(): pl.pallas_call(functools.partial(adam_kernel, steps=steps), grid=(2 * ste...  22.5 us

profile of v9, /device:TPU:8, one launch (start us, length us, event | category | flops | bytes accessed | tf_op | source)
XLA Modules:
  0.0 337.7 jit_solution(17450870138085119576)
XLA Ops:
  0.6 0.7 convert_element_type.6
  1.4 0.6 pad_convert_fusion.vs_ref
  2.0 117.2 %shard_map.218 = (f32[2,5,208,768]{3,2,1,0:T(8,128)}, bf16[2,5,208,2304]{3,2,1,0:T(8,128)(2,1)}, bf16[2,5,208,768]{3,2,1,0:T(8,128)(2,1)}, bf16[2,5,208,768]{3,2...) custom-call(bf16[5,197,768]{2,1,0:T(8,128)(2,1)} %img_ref.1, ...), custom_call_target="tpu_custom_call" | custom-call | tf_op jit(solution)/shard_map/pallas_call | solution.py:449
  119.2 0.0 copy-start
  119.2 0.0 copy-start.1
  119.2 0.0 copy-start.2
  119.2 194.5 %shard_map.219 = (f32[5,197,768]{2,1,0:T(8,128)}, bf16[2,96,5376]{2,1,0:T(8,128)(2,1)}, bf16[2,480,768]{2,1,0:T(8,128)(2,1)}, f32[2,16,128]{2,1,0:T(8,128)}) custom-call(bf16[5,197,768]{2,1,0:T(8,128)(2,1)} %cot_ref.1, bf16[18432,768]{1,0:T(8,128)(2,1)} %get-tuple-element.39.w_ref, f32[2,16,768]{2,1,0:T(8,128)} %get-tuple-element.40.vec_ref, ...), custom_call_target="tpu_custom_call" | custom-call | tf_op jit(solution)/shard_map/pallas_call | solution.py:829
  313.7 0.7 slice_bitcast_fusion
  314.4 0.0 copy-done
  314.4 0.0 copy-done.1
  314.4 0.0 copy-done.2
  314.4 0.6 multiply_subtract_fusion
  315.1 22.5 %shard_map.220 = (f32[2,96,5376]{2,1,0:T(8,128)}, f32[2,96,5376]{2,1,0:T(8,128)}, f32[2,96,5376]{2,1,0:T(8,128)}, f32[2,96,5376]{2,1,0:T(8,128)}, f32[2,480,768]...) custom-call(bf16[2,96,5376]{2,1,0:T(8,128)(2,1)} %get-tuple-element., ...), custom_call_target="tpu_custom_call" | custom-call | tf_op jit(solution)/shard_map/pallas_call | solution.py:898
  (1 shorter events, 0.0 us)
Async XLA Ops:
  119.2 195.2 %copy-start = (f32[2,1152]{1,0:T(2,128)S(1)}, f32[2,1152]{1,0:T(2,128)}, u32[]{:S(2)}) copy-start(f32[2,1152]{1,0:T(2,128)} %param.15) | copy-start | bytes 27652
  119.2 195.2 %copy-start.1 = (f32[2,1152]{1,0:T(2,128)S(1)}, f32[2,1152]{1,0:T(2,128)}, u32[]{:S(2)}) copy-start(f32[2,1152]{1,0:T(2,128)} %param.18) | copy-start | bytes 27652
  119.2 195.2 %copy-start.2 = (f32[2,1152]{1,0:T(2,128)S(1)}, f32[2,1152]{1,0:T(2,128)}, u32[]{:S(2)}) copy-start(f32[2,1152]{1,0:T(2,128)} %param.21) | copy-start | bytes 27652

commit v10 on v9

--- a/solution.py
+++ b/solution.py
@@ -602,7 +602,6 @@
             pl.semaphore_signal(bar, inc=1, device_id={"fsdp": (f + k) % 8}, device_id_type=MESH)
         for k in range(1, 4):
             pl.semaphore_signal(bar, inc=1, device_id={"rep": (z + k) % 4}, device_id_type=MESH)
-        pl.semaphore_wait(bar, 10)
         dv[...] = jnp.zeros_like(dv)
         fetch(a2_ref, 0, l).start()
         for i in range(n):
@@ -651,6 +650,10 @@
     def _():
         fetch(a2_ref, 0, l - 1).start()
         load(l - 1, 3, 3, 0).start()
+
+    @pl.when((lr == 0) & (s == 5))
+    def _():
+        pl.semaphore_wait(pltpu.get_barrier_semaphore(), 10)
 
     one = (s >= 5) & (s <= 8)
     two = (lr == 1) & (s >= 14) & (s <= 18)

time: 339 us -> 338 us (level)
  no operation moved by 1% of the time
where the time goes in v10:
time: 338 us; the launch traced here: 337 us
  Pallas kernels  334 us (99%)
    pallas_call x1, Pallas kernels, bwd(): pl.pallas_call(bwd_kernel, grid=(LAYERS, 25), in_specs=[pl.BlockSpec(cota...  194 us
    pallas_call x1, Pallas kernels, fwd(): pl.pallas_call(fwd_kernel, grid=(LAYERS, 14), in_specs=[pl.BlockSpec(imag...  117 us
    pallas_call x1, Pallas kernels, adam_all(): pl.pallas_call(functools.partial(adam_kernel, steps=steps), grid=(2 * ste...  22.5 us

profile of v10, /device:TPU:8, one launch (start us, length us, event | category | flops | bytes accessed | tf_op | source)
XLA Modules:
  0.0 337.3 jit_solution(6792067895551729630)
XLA Ops:
  0.6 0.7 convert_element_type.6
  1.4 0.6 pad_convert_fusion.vs_ref
  2.0 117.2 %shard_map.218 = (f32[2,5,208,768]{3,2,1,0:T(8,128)}, bf16[2,5,208,2304]{3,2,1,0:T(8,128)(2,1)}, bf16[2,5,208,768]{3,2,1,0:T(8,128)(2,1)}, bf16[2,5,208,768]{3,2...) custom-call(bf16[5,197,768]{2,1,0:T(8,128)(2,1)} %img_ref.1, ...), custom_call_target="tpu_custom_call" | custom-call | tf_op jit(solution)/shard_map/pallas_call | solution.py:449
  119.2 0.0 copy-start
  119.2 0.0 copy-start.1
  119.2 0.0 copy-start.2
  119.2 194.1 %shard_map.219 = (f32[5,197,768]{2,1,0:T(8,128)}, bf16[2,96,5376]{2,1,0:T(8,128)(2,1)}, bf16[2,480,768]{2,1,0:T(8,128)(2,1)}, f32[2,16,128]{2,1,0:T(8,128)}) custom-call(bf16[5,197,768]{2,1,0:T(8,128)(2,1)} %cot_ref.1, bf16[18432,768]{1,0:T(8,128)(2,1)} %get-tuple-element.39.w_ref, f32[2,16,768]{2,1,0:T(8,128)} %get-tuple-element.40.vec_ref, ...), custom_call_target="tpu_custom_call" | custom-call | tf_op jit(solution)/shard_map/pallas_call | solution.py:832
  313.3 0.7 slice_bitcast_fusion
  314.1 0.0 copy-done
  314.1 0.0 copy-done.1
  314.1 0.0 copy-done.2
  314.1 0.6 multiply_subtract_fusion
  314.7 22.5 %shard_map.220 = (f32[2,96,5376]{2,1,0:T(8,128)}, f32[2,96,5376]{2,1,0:T(8,128)}, f32[2,96,5376]{2,1,0:T(8,128)}, f32[2,96,5376]{2,1,0:T(8,128)}, f32[2,480,768]...) custom-call(bf16[2,96,5376]{2,1,0:T(8,128)(2,1)} %get-tuple-element., ...), custom_call_target="tpu_custom_call" | custom-call | tf_op jit(solution)/shard_map/pallas_call | solution.py:901
  (1 shorter events, 0.0 us)
Async XLA Ops:
  119.2 194.9 %copy-start = (f32[2,1152]{1,0:T(2,128)S(1)}, f32[2,1152]{1,0:T(2,128)}, u32[]{:S(2)}) copy-start(f32[2,1152]{1,0:T(2,128)} %param.15) | copy-start | bytes 27652
  119.2 194.9 %copy-start.1 = (f32[2,1152]{1,0:T(2,128)S(1)}, f32[2,1152]{1,0:T(2,128)}, u32[]{:S(2)}) copy-start(f32[2,1152]{1,0:T(2,128)} %param.18) | copy-start | bytes 27652
  119.2 194.9 %copy-start.2 = (f32[2,1152]{1,0:T(2,128)S(1)}, f32[2,1152]{1,0:T(2,128)}, u32[]{:S(2)}) copy-start(f32[2,1152]{1,0:T(2,128)} %param.21) | copy-start | bytes 27652
